TPU v7x, 32 devices: a whole 2x2x4 slice. The times are simulated.
32 devices in a mesh: space: 4 (over z), tm: 8 (over y, x, core).
Axes of the slice: x: 2, y: 2, z: 4, core: 2. Of those that a mesh axis runs over, the one named last changes fastest.
Arguments:
- snapshots: float32 [8192, 3072], P('space', 'tm'), may hold values from -40 to 40, as said below
Outputs:
- window_gram: float32 [3072, 3072], P('tm', 'space')
Inputs may be any that keep to these rules, and one draw needn't show every extreme that they name: `snapshots`: real-valued snapshot entries.
All inputs are finite; a program needn't handle non-finite values.
Results may differ from a plain program's by a relative error of at most 0.000058.
Values sent between devices are 32-bit elements; how exact they have to be, the bound alone decides.
No kernel may reach another device: no remote copies, remote signals or barrier semaphores. Data moves between devices by JAX's collectives and lax.ppermute only.
A program may use at most 128 MiB of HBM per device.

v0:
```python
import jax
import jax.numpy as jnp
from jax import lax
from jax.sharding import PartitionSpec as P

WINDOW = 16


def shifted(block, axis, distance):
    devices = range(lax.axis_size(axis))
    route = [(i - distance, i) for i in devices if i - distance in devices]
    return lax.ppermute(block, axis, route)


def cross(left, right):
    return lax.dot_general(
        left,
        right,
        (((0,), (0,)), ((), ())),
        precision=lax.Precision.HIGHEST,
        preferred_element_type=jnp.float32,
    )


def local(snapshots):
    block = snapshots.shape[1]
    rows = snapshots.shape[0] * lax.axis_size("space")
    reach = WINDOW - 1
    partial_value = cross(snapshots, lax.all_gather(snapshots, "tm", axis=1, tiled=True))
    gram = lax.psum_scatter(partial_value, "space", scatter_dimension=1, tiled=True) / rows
    share = gram.shape[1]
    below = shifted(gram[:reach], "tm", -1)
    taller = jnp.concatenate([gram, below], 0)
    beside = shifted(taller[:, :reach], "space", -1)
    extended = jnp.concatenate([taller, beside], 1)
    total = jnp.zeros((block, share), jnp.float32)
    for offset in range(WINDOW):
        total = total + extended[offset : offset + block, offset : offset + share]
    return total / WINDOW


def solution(mesh):
    placed = (P("space", "tm"),)
    return jax.shard_map(
        local, mesh=mesh, in_specs=placed, out_specs=P("tm", "space"), check_vma=False
    )
```

profile of v0, /device:TPU:1, one launch (start us, length us, event | category | flops | bytes accessed | tf_op | source)
XLA Modules:
  0.0 285.1 jit_solution(1424260581626865839)
XLA Ops:
  6.5 0.0 all-gather.2.cloned.1.call-start
  6.5 0.0 copy-start.1
  6.5 0.7 all-gather.2.cloned.1.call-update
  7.3 0.0 reduce-scatter.2.cloned.1.call-start
  7.3 129.3 %all-gather.2.cloned.1.call-done = f32[2048,3072]{1,0:T(8,128)} async-done(((f32[2048,384]{1,0:T(8,128)}), f32[2048,3072]{1,0:T(8,128)}) %all-gather.2.cloned.1.call-update) | async-done | bytes 25165840 | tf_op jit(solution)/shard_map/all_gather | solution.py:29
  136.6 0.0 copy-done.1
  136.6 35.4 %fusion.1 = f32[384,3072]{1,0:T(8,128)} fusion(f32[2048,384]{1,0:T(8,128)S(1)} %copy-done.1, f32[2048,3072]{1,0:T(8,128)} %all-gather.2.cloned.1.call-done), kind=kOutput, calls=%fused_computation.19 | convolution fusion | flops 28991029248 | bytes 33030144 | tf_op jit(solution)/shard_map/dot_general | solution.py:16
  172.0 0.0 reduce-scatter.2.cloned.1.call-update
  172.0 85.0 %reduce-scatter.2.cloned.1.call-done = f32[384,768]{1,0:T(8,128)} async-done(((f32[384,3072]{1,0:T(8,128)}), f32[384,768]{1,0:T(8,128)}) %reduce-scatter.2.cloned.1.call-update) | async-done | bytes 1179664 | tf_op jit(solution)/shard_map/reduce_scatter | solution.py:30
  257.0 1.3 broadcast_multiply_fusion
  258.4 2.5 collective-permute-start
  260.9 2.9 %collective-permute-done = f32[15,768]{1,0:T(8,128)S(1)} collective-permute-done((f32[15,768]{1,0:T(8,128)S(1)}, f32[15,768]{1,0:T(8,128)S(1)}, u32[]{:S(2)}, u32[]{:S(2)}) %collective-permute-start) | collective-permute-done | bytes 46112 | tf_op jit(solution)/shard_map/ppermute | solution.py:12
  263.8 0.0 copy-start
  263.8 1.4 collective-permute-start.1
  265.3 6.2 %collective-permute-done.1 = f32[399,15]{1,0:T(8,128)S(1)} collective-permute-done((f32[399,15]{1,0:T(8,128)S(1)}, f32[399,15]{1,0:T(8,128)S(1)}, u32[]{:S(2)}, u32[]{:S(2)}) %collective-permute-start.1) | collective-permute-done | bytes 23972 | tf_op jit(solution)/shard_map/ppermute | solution.py:12
  271.5 0.1 pad_maximum_fusion
  271.6 0.0 copy-done
  271.6 6.6 %fusion = f32[384,768]{1,0:T(8,128)} fusion(f32[399,783]{1,0:T(8,128)S(1)} %pad_maximum_fusion, f32[384,768]{1,0:T(8,128)S(1)} %copy-done), kind=kLoop, calls=%fused_computation.2 | loop fusion | flops 5013504 | bytes 20054016 | tf_op jit(solution)/shard_map/div | solution.py:39
  (2 shorter events, 0.0 us)
Async XLA Ops:
  6.5 130.0 %all-gather.2.cloned.1.call-start = ((), (), s32[]{:S(2)}) async-start(), calls=%async_computation.1 | async-start | bytes 28311552 | tf_op jit(solution)/shard_map/all_gather | solution.py:29
  6.5 130.0 %copy-start.1 = (f32[2048,384]{1,0:T(8,128)S(1)}, f32[2048,384]{1,0:T(8,128)}, u32[]{:S(2)}) copy-start(f32[2048,384]{1,0:T(8,128)} %param.1) | copy-start | bytes 9437188
  7.3 249.8 %reduce-scatter.2.cloned.1.call-start = ((), (), s32[]{:S(2)}) async-start(), calls=%async_computation.2 | async-start | bytes 5898240 | tf_op jit(solution)/shard_map/reduce_scatter | solution.py:30
  258.4 5.4 %collective-permute-start = (f32[15,768]{1,0:T(8,128)S(1)}, f32[15,768]{1,0:T(8,128)S(1)}, u32[]{:S(2)}, u32[]{:S(2)}) collective-permute-start(f32[15,768]{1,0:T(8,128)S(1)} %slice.68), channel_id=1, source_target_pairs={{1,0},{2,1},{3,2},{4,3},{5,4},{6,5},{7,6},{9,8},{10,9},{11,10},{12... | collective-permute-start | bytes 138248 | tf_op jit(solution)/shard_map/ppermute | solution.py:12
  263.8 7.8 %copy-start = (f32[384,768]{1,0:T(8,128)S(1)}, f32[384,768]{1,0:T(8,128)}, u32[]{:S(2)}) copy-start(f32[384,768]{1,0:T(8,128)} %reduce-scatter.2.cloned.1.call-done) | copy-start | bytes 3538948
  263.8 7.6 %collective-permute-start.1 = (f32[399,15]{1,0:T(8,128)S(1)}, f32[399,15]{1,0:T(8,128)S(1)}, u32[]{:S(2)}, u32[]{:S(2)}) collective-permute-start(f32[399,15]{1,0:T(8,128)S(1)} %pad_maximum_fusion.1), channel_id=1, source_target_pairs={{8,0},{16,8},{24,16},{9,1},{17,9},{25,17},{10,2},{18,10},{26,18},{... | collective-permute-start | bytes 71828 | tf_op jit(solution)/shard_map/ppermute | solution.py:12
Sparse Core Ops, SparseCore 0:
  9.3 127.2 all-gather.1
  172.1 84.8 reduce-scatter.1
where the time goes:
time: 286 us; the launch traced here: 285 us
  waiting for transfers between devices  224 us (78%)
  matrix products  35.4 us (12%)
  between operations  13.5 us (5%)
  other arithmetic  8.09 us (3%)
  starting transfers between devices  4.01 us (1%)
    all_gather x1, waiting for transfers between devices, local(): lax.all_gather(snapshots, 'tm', axis=1, tiled=True)  129 us
    reduce_scatter x1, waiting for transfers between devices, local(): lax.psum_scatter(partial_value, 'space', scatter_dimension=1, tiled=True)  85 us
    dot_general x1, matrix products, cross(): lax.dot_general(left, right, (((0,), (0,)), ((), ())), precision=lax.Prec...  35.4 us
    ppermute x2, waiting for transfers between devices, shifted(): return lax.ppermute(block, axis, route)  9.06 us
    div x1, other arithmetic, local(): return total / WINDOW  6.63 us
  transfers between devices with their start and end apart: 4, of which 4 were waited for; matrix products, arithmetic and copies ran while one was open for 0% of the time, Pallas kernels for 0%

commit v1 on v0

v1 whole, which is shorter than its diff:
```python
import functools

import jax
import jax.numpy as jnp
from jax import lax
from jax.experimental import pallas as pl
from jax.experimental.pallas import tpu as pltpu
from jax.sharding import PartitionSpec as P

WINDOW = 16
PARTS = (3, 3, 3, 2, 1)
DEPTH = 512
MEMORY = 48 * 2**20


def params():
    return pltpu.CompilerParams(vmem_limit_bytes=MEMORY)


def swapped(block, bit, axis="tm"):
    size = lax.axis_size(axis)
    return lax.ppermute(block, axis, [(i, i ^ bit) for i in range(size)])


def shifted(block, axis, distance):
    devices = range(lax.axis_size(axis))
    route = [(i - distance, i) for i in devices if i - distance in devices]
    return lax.ppermute(block, axis, route)


def split(value):
    high = value.astype(jnp.bfloat16)
    low = (value - high.astype(jnp.float32)).astype(jnp.bfloat16)
    return high, low


def turn_kernel(source, *chunks):
    turned = source[...].T
    start = 0
    for chunk in chunks:
        chunk[...] = turned[start : start + chunk.shape[0]]
        start += chunk.shape[0]


def turn(source, widths):
    rows, columns = source.shape
    step = 512
    return pl.pallas_call(
        turn_kernel,
        grid=(rows // step,),
        in_specs=[pl.BlockSpec((step, columns), lambda k: (k, 0))],
        out_specs=[pl.BlockSpec((width, step), lambda k: (0, k)) for width in widths],
        out_shape=[jax.ShapeDtypeStruct((width, rows), jnp.float32) for width in widths],
        compiler_params=params(),
    )(source)


def multiply_kernel(steps, place, own, mate, *refs):
    *pieces, keep, send, total = refs
    step = pl.program_id(0)
    left_high, left_low = split(jnp.concatenate([piece[...] for piece in pieces], 0))
    right_high, right_low = split(jnp.concatenate([own[...], mate[...]], 1))
    left = jnp.concatenate([left_high, left_low, left_high], 1)
    right = jnp.concatenate([right_high, right_high, right_low], 0)
    partial = jnp.dot(left, right, preferred_element_type=jnp.float32)

    @pl.when(step == 0)
    def _():
        total[...] = partial

    @pl.when(jnp.logical_and(step > 0, step < steps - 1))
    def _():
        total[...] += partial

    @pl.when(step == steps - 1)
    def _():
        ready = total[...] + partial
        count, width = keep.shape[:2]
        for offset in range(2 * count):
            block = ready[offset * width : (offset + 1) * width]
            distance = place[offset]
            slot, rest, bit = 0, lax.shift_right_logical(distance, 1), count // 2
            while bit:
                slot = slot + bit * lax.bitwise_and(rest, 1)
                rest, bit = lax.shift_right_logical(rest, 1), bit // 2
            odd = lax.bitwise_and(distance, 1)

            @pl.when(odd == 0)
            def _():
                keep[slot] = block

            @pl.when(odd == 1)
            def _():
                send[slot] = block


def multiply(place, own, mate, pieces):
    depth, block = own.shape
    steps = depth // DEPTH
    width = pieces[0].shape[0]
    chips = sum(piece.shape[0] for piece in pieces) // width
    shape = (chips // 2, width, 2 * block)
    right = pl.BlockSpec((DEPTH, block), lambda k: (k, 0))
    return pl.pallas_call(
        functools.partial(multiply_kernel, steps),
        grid=(steps,),
        in_specs=[pl.BlockSpec(memory_space=pltpu.SMEM), right, right]
        + [pl.BlockSpec((p.shape[0], DEPTH), lambda k: (0, k)) for p in pieces],
        out_specs=[pl.BlockSpec(shape, lambda k: (0, 0, 0))] * 2,
        out_shape=[jax.ShapeDtypeStruct(shape, jnp.float32)] * 2,
        scratch_shapes=[pltpu.VMEM((chips * width, 2 * block), jnp.float32)],
        compiler_params=params(),
        cost_estimate=pl.CostEstimate(flops=1, bytes_accessed=1, transcendentals=0),
    )(place, own, mate, *pieces)


def window_kernel(scale, turned, below, beside, corner, out, wide):
    rows, columns = out.shape
    wide[:rows, :columns] = turned[...].T
    wide[rows:, :columns] = below[...]
    edge = jnp.concatenate([beside[...].T, corner[:, :WINDOW]], 0)
    wide[:, columns:] = jnp.concatenate(
        [edge, jnp.zeros((rows + WINDOW, 128 - WINDOW), jnp.float32)], 1
    )
    total = wide[...] * scale
    distance = 1
    while distance < WINDOW:
        moved = pltpu.roll(total, total.shape[0] - distance, 0)
        total = total + pltpu.roll(moved, total.shape[1] - distance, 1)
        distance *= 2
    out[...] = total[:rows, :columns]


def window(scale, turned, below, beside, corner):
    columns, rows = turned.shape
    return pl.pallas_call(
        functools.partial(window_kernel, scale),
        out_shape=jax.ShapeDtypeStruct((rows, columns), jnp.float32),
        scratch_shapes=[pltpu.VMEM((rows + WINDOW, columns + 128), jnp.float32)],
        compiler_params=params(),
    )(turned, below, beside, corner)


def halve_kernel(keep, came, first, second):
    half = first.shape[0]
    first[...] = keep[:half] + came[:half]
    second[...] = keep[half:] + came[half:]


def halve(keep, came):
    half = (keep.shape[0] // 2,) + keep.shape[1:]
    return pl.pallas_call(
        halve_kernel,
        out_shape=[jax.ShapeDtypeStruct(half, jnp.float32)] * 2,
        compiler_params=params(),
    )(keep, came)


def collect_kernel(count, *refs):
    own, other = refs[2 * count :]
    start = 0
    for keep, came in zip(refs[:count], refs[count : 2 * count]):
        total = keep[0] + came[0]
        rows = pl.ds(start, total.shape[0])
        own[rows, :], other[rows, :] = total[:, : own.shape[1]], total[:, own.shape[1] :]
        start += total.shape[0]


def collect(keeps, cames):
    columns = sum(keep.shape[1] for keep in keeps)
    shape = jax.ShapeDtypeStruct((columns, keeps[0].shape[2] // 2), jnp.float32)
    return pl.pallas_call(
        functools.partial(collect_kernel, len(keeps)),
        out_shape=[shape] * 2,
        compiler_params=params(),
    )(*keeps, *cames)


def routed(block, ways):
    size = lax.axis_size("tm")
    return lax.ppermute(block, "tm", [(i, i ^ (2 << ways[i % 2])) for i in range(size)])


def local(snapshots):
    tm, space = lax.axis_index("tm"), lax.axis_index("space")
    chips, planes = lax.axis_size("tm") // 2, lax.axis_size("space")
    core = lax.rem(tm, 2)
    depth, block = snapshots.shape
    scale = 1.0 / (depth * planes * WINDOW)
    offsets = [jnp.int32(0), 1 + core, 2 - core, jnp.int32(3)]
    bit = 4
    while bit < chips:
        offsets += [lax.bitwise_xor(offset, bit) for offset in offsets]
        bit *= 2
    place = lax.bitwise_xor(jnp.stack(offsets), lax.bitwise_xor(lax.div(tm, 2), space))

    chunks = list(turn(snapshots, [block * part // sum(PARTS) for part in PARTS]))
    mate = swapped(snapshots, 1)
    count = len(chunks)
    steps = [(j, step) for j in range(count) for step in range(3)]
    got, firsts, halved, seconds = {}, {}, {}, {}

    def product(j):
        pieces = [chunks[j]] + [got[j, step] for step in range(3)]
        bit = 4
        while bit < chips:
            pieces += [swapped(piece, 2 * bit) for piece in pieces]
            bit *= 2
        keep, send = multiply(place, snapshots, mate, pieces)
        firsts[j] = keep, swapped(send, 1, "space")

    def halving(j):
        keep, send = halved[j]
        seconds[j] = keep, swapped(send, 2, "space")

    for k, (j, step) in enumerate(steps):
        tied = {"chunk": chunks[j]}
        if k >= 2:
            last = steps[k - 2]
            tied["got"] = got[last]
            if k == 2:
                tied["mate"] = mate
            i = last[0] if last[1] == 2 else -1
            if i >= 1:
                tied["halved"] = halve(*firsts[i - 1])
            if i >= 2:
                tied["second"] = seconds[i - 2]
            tied = lax.optimization_barrier(tied)
            chunks[j], got[last] = tied["chunk"], tied["got"]
            mate = tied.get("mate", mate)
            if i >= 1:
                halved[i - 1] = tied["halved"]
                halving(i - 1)
            if i >= 2:
                seconds[i - 2] = tied["second"]
        if step == 0:
            got[j, 0] = routed(chunks[j], (0, 1))
        elif step == 1:
            got[j, 1] = routed(chunks[j], (1, 0))
        else:
            got[j, 2] = routed(got[j, 0], (1, 0))
        if k >= 2 and i >= 0:
            product(i)
    for i in range(len(firsts), count):
        product(i)
    for i in range(count):
        if i not in halved:
            halved[i] = halve(*firsts[i])
            halving(i)
    for i, (keep, came) in seconds.items():
        bit = 2
        while keep.shape[0] > 1:
            bit *= 2
            keep, send = halve(keep, came)
            came = swapped(send, bit, "space")
        seconds[i] = keep, came
    own, other = collect(
        [seconds[j][0] for j in range(count)], [seconds[j][1] for j in range(count)]
    )
    other = swapped(other, 1)
    turned = jnp.concatenate(
        [jnp.where(core == 0, own, other), jnp.where(core == 0, other, own)], 0
    )
    below = shifted(turned[:, :WINDOW].T, "tm", -1)
    beside = shifted(turned[:WINDOW], "space", -1)
    corner = shifted(beside[:, :128].T[:WINDOW], "tm", -1)
    return window(scale, turned, below, beside, corner)


def solution(mesh):
    placed = (P("space", "tm"),)
    return jax.shard_map(
        local, mesh=mesh, in_specs=placed, out_specs=P("tm", "space"), check_vma=False
    )
```

time: 286 us -> 201 us (0.70)
  waiting for transfers between devices: 224 us -> 107 us
  starting transfers between devices: 4.01 us -> 45.6 us
  Pallas kernels: 0 us -> 35.9 us
  matrix products: 35.4 us -> 0 us
  between operations: 13.5 us -> 0.26 us
  local copies, waits for them, and re-layouts: 0.01 us -> 9.82 us
  other arithmetic: 8.09 us -> 0.24 us
    all_gather x1 -> x0, waiting for transfers between devices: 129 us -> none  [local(): lax.all_gather(snapshots, 'tm', axis=1, tiled=True)]
    ppermute x0 -> x27, waiting for transfers between devices: none -> 101 us  [the longest x12 64.6 us: swapped(): return lax.ppermute(block, axis, [(i, i ^ bit) for i in range(size)])]
    reduce_scatter x1 -> x0, waiting for transfers between devices: 85 us -> none  [local(): lax.psum_scatter(partial_value, 'space', scatter_dimension=1, tiled=True)]
    ppermute x0 -> x27, starting transfers between devices: none -> 38.9 us  [the longest x15 23.1 us: routed(): lax.ppermute(block, 'tm', [(i, i ^ 2 << ways[i % 2]) for i in range(size)])]
    pallas_call x0 -> x13, Pallas kernels: none -> 35.9 us  [the longest x5 29.3 us: multiply(): pl.pallas_call(functools.partial(multiply_kernel, steps), grid=(steps,),...]
    dot_general x1 -> x0, matrix products: 35.4 us -> none  [cross(): lax.dot_general(left, right, (((0,), (0,)), ((), ())), precision=lax.Prec...]
    unnamed x4 -> x22, local copies, waits for them, and re-layouts: 0.01 us -> 8.9 us
    div x2 -> x0, other arithmetic: 7.98 us -> none  [the longest x1 6.63 us: local(): return total / WINDOW]
  transfers between devices with their start and end apart: 4 -> 30, of which waited for: 4 -> 16; matrix products, arithmetic and copies ran while one was open for 0% -> 0% of each run, Pallas kernels for 0% -> 17%
where the time goes in v1:
time: 201 us; the launch traced here: 199 us
  waiting for transfers between devices  107 us (53%)
  starting transfers between devices  45.6 us (23%)
  Pallas kernels  35.9 us (18%)
  local copies, waits for them, and re-layouts  9.82 us (5%)
    ppermute x12, waiting for transfers between devices, swapped(): return lax.ppermute(block, axis, [(i, i ^ bit) for i in range(size)])  64.6 us
    ppermute x15, waiting for transfers between devices, routed(): lax.ppermute(block, 'tm', [(i, i ^ 2 << ways[i % 2]) for i in range(size)])  36.2 us
    pallas_call x5, Pallas kernels, multiply(): pl.pallas_call(functools.partial(multiply_kernel, steps), grid=(steps,),...  29.3 us
    ppermute x15, starting transfers between devices, routed(): lax.ppermute(block, 'tm', [(i, i ^ 2 << ways[i % 2]) for i in range(size)])  23.1 us
    ppermute x12, starting transfers between devices, swapped(): return lax.ppermute(block, axis, [(i, i ^ bit) for i in range(size)])  15.9 us
    unnamed x22, local copies, waits for them, and re-layouts  8.9 us
    ppermute x3, starting transfers between devices, shifted(): return lax.ppermute(block, axis, route)  6.68 us
    ppermute x3, waiting for transfers between devices, shifted(): return lax.ppermute(block, axis, route)  6.53 us
  transfers between devices with their start and end apart: 30, of which 16 were waited for; matrix products, arithmetic and copies ran while one was open for 0% of the time, Pallas kernels for 17%

profile of v1, /device:TPU:1, one launch (start us, length us, event | category | flops | bytes accessed | tf_op | source)
XLA Modules:
  0.0 199.2 jit_solution(12278609162036857184)
XLA Ops:
  0.1 3.3 %shard_map.17 = (f32[96,2048]{1,0:T(8,128)S(1)}, f32[96,2048]{1,0:T(8,128)S(1)}, f32[96,2048]{1,0:T(8,128)S(1)}, f32[64,2048]{1,0:T(8,128)S(1)}, f32[32,2048]{1,0:T(8,128)S(1)}) custom-call(f32[2048,384]{1,0:T(8,128)} %own.9), custom_call_target="tpu_custom_call" | custom-call | tf_op jit(solution)/shard_map/pallas_call | solution.py:48
  4.2 2.7 %collective-permute-start.1 = (f32[96,2048]{1,0:T(8,128)S(1)}, f32[96,2048]{1,0:T(8,128)S(1)}, u32[]{:S(2)}, u32[]{:S(2)}) collective-permute-start(f32[96,2048]{1,0:T(8,128)S(1)} %get-tuple-element.79.refs_0_), channel_id=1, source_target_pairs={{0,2},{1,5},{2,0},{3,7},{4,6},{5,1},{6,4},{7,3},{8,10},{9,13},{10,... | collective-permute-start | bytes 2359304 | tf_op jit(solution)/shard_map/ppermute | solution.py:181
  8.9 13.8 %collective-permute-done.1.refs_1_ = f32[96,2048]{1,0:T(8,128)S(1)} collective-permute-done((f32[96,2048]{1,0:T(8,128)S(1)}, f32[96,2048]{1,0:T(8,128)S(1)}, u32[]{:S(2)}, u32[]{:S(2)}) %collective-permute-start.1) | collective-permute-done | bytes 786464 | tf_op jit(solution)/shard_map/ppermute | solution.py:181
  22.7 3.3 %collective-permute-start.3 = (f32[96,2048]{1,0:T(8,128)S(1)}, f32[96,2048]{1,0:T(8,128)S(1)}, u32[]{:S(2)}, u32[]{:S(2)}) collective-permute-start(f32[96,2048]{1,0:T(8,128)S(1)} %collective-permute-done.1.refs_1_), channel_id=1, source_target_pairs={{0,4},{1,3},{2,6},{3,1},{4,0},{5,7},{6,2},{7,5},{8,12},{9,11},{10,... | collective-permute-start | bytes 2359304 | tf_op jit(solution)/shard_map/ppermute | solution.py:181
  28.4 10.7 %collective-permute-done.3.refs_3_ = f32[96,2048]{1,0:T(8,128)S(1)} collective-permute-done((f32[96,2048]{1,0:T(8,128)S(1)}, f32[96,2048]{1,0:T(8,128)S(1)}, u32[]{:S(2)}, u32[]{:S(2)}) %collective-permute-start.3) | collective-permute-done | bytes 786464 | tf_op jit(solution)/shard_map/ppermute | solution.py:181
  41.5 3.6 %collective-permute-done.5.refs_1_ = f32[96,2048]{1,0:T(8,128)S(1)} collective-permute-done((f32[96,2048]{1,0:T(8,128)S(1)}, f32[96,2048]{1,0:T(8,128)S(1)}, u32[]{:S(2)}, u32[]{:S(2)}) %collective-permute-start.5) | collective-permute-done | bytes 786464 | tf_op jit(solution)/shard_map/ppermute | solution.py:181
  51.1 6.6 %shard_map.18 = (f32[2,96,768]{2,1,0:T(8,128)S(1)}, f32[2,96,768]{2,1,0:T(8,128)S(1)}) custom-call(s32[4]{0:T(128)S(1)} %add_xor_fusion.place, f32[2048,384]{1,0:T(8,128)} %own.9, f32[2048,384]{1,0:T(8,128)} %collective-permute-done.2.mate, f32[96,2048]{1,0:T(8,128)S(1)} %copy-done.2, f32[96,2048]{1,0:T(8,128)S(1)} %copy-done.4, f32[96,2048]{1,0:T(8,128)S(1)} %copy-done.6, ...), custom_call_target="tpu_custom_call" | custom-call | flops 1 | bytes 1 | tf_op jit(solution)/shard_map/pallas_call | solution.py:104
  60.4 11.4 %collective-permute-done.7.came = f32[2,96,768]{2,1,0:T(8,128)S(1)} collective-permute-done((f32[2,96,768]{2,1,0:T(8,128)S(1)}, f32[2,96,768]{2,1,0:T(8,128)S(1)}, u32[]{:S(2)}, u32[]{:S(2)}) %collective-permute-start.7) | collective-permute-done | bytes 589856 | tf_op jit(solution)/shard_map/ppermute | solution.py:22
  73.4 2.4 %collective-permute-start.10 = (f32[96,2048]{1,0:T(8,128)S(1)}, f32[96,2048]{1,0:T(8,128)S(1)}, u32[]{:S(2)}, u32[]{:S(2)}) collective-permute-start(f32[96,2048]{1,0:T(8,128)S(1)} %collective-permute-done.9.refs_1_), channel_id=1, source_target_pairs={{0,4},{1,3},{2,6},{3,1},{4,0},{5,7},{6,2},{7,5},{8,12},{9,11},{10,... | collective-permute-start | bytes 2359304 | tf_op jit(solution)/shard_map/ppermute | solution.py:181
  75.8 6.6 %shard_map.20 = (f32[2,96,768]{2,1,0:T(8,128)S(1)}, f32[2,96,768]{2,1,0:T(8,128)S(1)}) custom-call(s32[4]{0:T(128)S(1)} %add_xor_fusion.place, f32[2048,384]{1,0:T(8,128)} %own.9, f32[2048,384]{1,0:T(8,128)} %collective-permute-done.2.mate, f32[96,2048]{1,0:T(8,128)S(1)} %get-tuple-element.89.refs_0_, f32[96,2048]{1,0:T(8,128)S(1)} %collective-permute-done.5.refs_1_, ...), custom_call_target="tpu_custom_call" | custom-call | flops 1 | bytes 1 | tf_op jit(solution)/shard_map/pallas_call | solution.py:104
  87.9 15.9 %collective-permute-done.11.came = f32[2,96,768]{2,1,0:T(8,128)S(1)} collective-permute-done((f32[2,96,768]{2,1,0:T(8,128)S(1)}, f32[2,96,768]{2,1,0:T(8,128)S(1)}, u32[]{:S(2)}, u32[]{:S(2)}) %collective-permute-start.11) | collective-permute-done | bytes 589856 | tf_op jit(solution)/shard_map/ppermute | solution.py:22
  104.0 6.8 %shard_map.22 = (f32[2,96,768]{2,1,0:T(8,128)S(1)}, f32[2,96,768]{2,1,0:T(8,128)S(1)}) custom-call(s32[4]{0:T(128)S(1)} %add_xor_fusion.place, f32[2048,384]{1,0:T(8,128)} %own.9, f32[2048,384]{1,0:T(8,128)} %collective-permute-done.2.mate, f32[96,2048]{1,0:T(8,128)S(1)} %get-tuple-element.103.refs_0_, f32[96,2048]{1,0:T(8,128)S(1)} %collective-permute-done.9.refs_1_, ...), custom_call_target="tpu_custom_call" | custom-call | flops 1 | bytes 1 | tf_op jit(solution)/shard_map/pallas_call | solution.py:104
  117.9 12.3 %collective-permute-done.16.came = f32[2,96,768]{2,1,0:T(8,128)S(1)} collective-permute-done((f32[2,96,768]{2,1,0:T(8,128)S(1)}, f32[2,96,768]{2,1,0:T(8,128)S(1)}, u32[]{:S(2)}, u32[]{:S(2)}) %collective-permute-start.16) | collective-permute-done | bytes 589856 | tf_op jit(solution)/shard_map/ppermute | solution.py:22
  130.3 5.2 %shard_map.24 = (f32[2,64,768]{2,1,0:T(8,128)S(1)}, f32[2,64,768]{2,1,0:T(8,128)S(1)}) custom-call(s32[4]{0:T(128)S(1)} %add_xor_fusion.place, f32[2048,384]{1,0:T(8,128)S(1)} %copy-done, f32[2048,384]{1,0:T(8,128)} %collective-permute-done.2.mate, f32[64,2048]{1,0:T(8,128)S(1)} %copy-done.10, f32[64,2048]{1,0:T(8,128)S(1)} %collective-permute-done.14.refs_1_, ...), custom_call_target="tpu_custom_call" | custom-call | flops 1 | bytes 1 | tf_op jit(solution)/shard_map/pallas_call | solution.py:104
  136.4 3.1 %collective-permute-start.20 = (f32[32,2048]{1,0:T(8,128)S(1)}, f32[32,2048]{1,0:T(8,128)S(1)}, u32[]{:S(2)}, u32[]{:S(2)}) collective-permute-start(f32[32,2048]{1,0:T(8,128)S(1)} %get-tuple-element.121.refs_0_), channel_id=1, source_target_pairs={{0,4},{1,3},{2,6},{3,1},{4,0},{5,7},{6,2},{7,5},{8,12},{9,11},{10,... | collective-permute-start | bytes 786440 | tf_op jit(solution)/shard_map/ppermute | solution.py:181
  139.6 4.0 %collective-permute-done.20.refs_2_ = f32[32,2048]{1,0:T(8,128)S(1)} collective-permute-done((f32[32,2048]{1,0:T(8,128)S(1)}, f32[32,2048]{1,0:T(8,128)S(1)}, u32[]{:S(2)}, u32[]{:S(2)}) %collective-permute-start.20) | collective-permute-done | bytes 262176 | tf_op jit(solution)/shard_map/ppermute | solution.py:181
  143.6 2.8 %collective-permute-done.21.refs_3_ = f32[32,2048]{1,0:T(8,128)S(1)} collective-permute-done((f32[32,2048]{1,0:T(8,128)S(1)}, f32[32,2048]{1,0:T(8,128)S(1)}, u32[]{:S(2)}, u32[]{:S(2)}) %collective-permute-start.21) | collective-permute-done | bytes 262176 | tf_op jit(solution)/shard_map/ppermute | solution.py:181
  146.4 4.2 %shard_map.26 = (f32[2,32,768]{2,1,0:T(8,128)S(1)}, f32[2,32,768]{2,1,0:T(8,128)S(1)}) custom-call(s32[4]{0:T(128)S(1)} %add_xor_fusion.place, f32[2048,384]{1,0:T(8,128)S(1)} %copy-done, f32[2048,384]{1,0:T(8,128)} %collective-permute-done.2.mate, f32[32,2048]{1,0:T(8,128)S(1)} %get-tuple-element.121.refs_0_, ...), custom_call_target="tpu_custom_call" | custom-call | flops 1 | bytes 1 | tf_op jit(solution)/shard_map/pallas_call | solution.py:104
  153.5 5.4 %collective-permute-done.22.came = f32[2,32,768]{2,1,0:T(8,128)S(1)} collective-permute-done((f32[2,32,768]{2,1,0:T(8,128)S(1)}, f32[2,32,768]{2,1,0:T(8,128)S(1)}, u32[]{:S(2)}, u32[]{:S(2)}) %collective-permute-start.22) | collective-permute-done | bytes 196640 | tf_op jit(solution)/shard_map/ppermute | solution.py:22
  160.6 14.5 %collective-permute-done.24.refs_8_ = f32[1,64,768]{2,1,0:T(8,128)S(1)} collective-permute-done((f32[1,64,768]{2,1,0:T(8,128)S(1)}, f32[1,64,768]{2,1,0:T(8,128)S(1)}, u32[]{:S(2)}, u32[]{:S(2)}) %collective-permute-start.24) | collective-permute-done | bytes 196640 | tf_op jit(solution)/shard_map/ppermute | solution.py:22
  177.5 3.2 %collective-permute-start.26 = (f32[384,384]{0,1:T(8,128)S(1)}, f32[384,384]{0,1:T(8,128)S(1)}, u32[]{:S(2)}, u32[]{:S(2)}) collective-permute-start(f32[384,384]{0,1:T(8,128)S(1)} %copy.2), channel_id=1, source_target_pairs={{0,1},{1,0},{2,3},{3,2},{4,5},{5,4},{6,7},{7,6},{8,9},{9,8},{10,11... | collective-permute-start | bytes 1769480 | tf_op jit(solution)/shard_map/ppermute | solution.py:22
  186.1 4.4 %collective-permute-done.28 = f32[16,384]{0,1:T(8,128)S(1)} collective-permute-done((f32[16,384]{0,1:T(8,128)S(1)}, f32[16,384]{0,1:T(8,128)S(1)}, u32[]{:S(2)}, u32[]{:S(2)}) %collective-permute-start.28) | collective-permute-done | bytes 24608 | tf_op jit(solution)/shard_map/ppermute | solution.py:28
  190.5 3.1 %collective-permute-start.29 = (f32[16,16]{1,0:T(8,128)S(1)}, f32[16,16]{1,0:T(8,128)S(1)}, u32[]{:S(2)}, u32[]{:S(2)}) collective-permute-start(f32[16,16]{1,0:T(8,128)S(1)} %slice.20), channel_id=1, source_target_pairs={{1,0},{2,1},{3,2},{4,3},{5,4},{6,5},{7,6},{9,8},{10,9},{11,10},{12... | collective-permute-start | bytes 3080 | tf_op jit(solution)/shard_map/ppermute | solution.py:28
  196.3 2.9 %shard_map.29 = f32[384,768]{1,0:T(8,128)} custom-call(f32[768,384]{1,0:T(8,128)S(1)} %copy.5.turned, f32[16,768]{1,0:T(8,128)S(1)} %collective-permute-done.27.below, f32[16,384]{1,0:T(8,128)S(1)} %copy.6.beside, f32[16,16]{1,0:T(8,128)S(1)} %collective-permute-done.29.corner), custom_call_target="tpu_custom_call" | custom-call | tf_op jit(solution)/shard_map/pallas_call | solution.py:136
  (82 shorter events, 46.8 us)
Async XLA Ops:
  0.0 22.7 %collective-permute-start.2 = (f32[2048,384]{1,0:T(8,128)}, f32[2048,384]{1,0:T(8,128)}, u32[]{:S(2)}, u32[]{:S(2)}) collective-permute-start(f32[2048,384]{1,0:T(8,128)} %own.9), channel_id=1, source_target_pairs={{0,1},{1,0},{2,3},{3,2},{4,5},{5,4},{6,7},{7,6},{8,9},{9,8},{10,11... | collective-permute-start | bytes 9437192 | tf_op jit(solution)/shard_map/ppermute | solution.py:22
  4.2 18.5 %collective-permute-start.1 = (f32[96,2048]{1,0:T(8,128)S(1)}, f32[96,2048]{1,0:T(8,128)S(1)}, u32[]{:S(2)}, u32[]{:S(2)}) collective-permute-start(f32[96,2048]{1,0:T(8,128)S(1)} %get-tuple-element.79.refs_0_), channel_id=1, source_target_pairs={{0,2},{1,5},{2,0},{3,7},{4,6},{5,1},{6,4},{7,3},{8,10},{9,13},{10,... | collective-permute-start | bytes 2359304 | tf_op jit(solution)/shard_map/ppermute | solution.py:181
  6.9 20.0 %collective-permute-start = (f32[96,2048]{1,0:T(8,128)S(1)}, f32[96,2048]{1,0:T(8,128)S(1)}, u32[]{:S(2)}, u32[]{:S(2)}) collective-permute-start(f32[96,2048]{1,0:T(8,128)S(1)} %get-tuple-element.79.refs_0_), channel_id=1, source_target_pairs={{0,4},{1,3},{2,6},{3,1},{4,0},{5,7},{6,2},{7,5},{8,12},{9,11},{10,... | collective-permute-start | bytes 2359304 | tf_op jit(solution)/shard_map/ppermute | solution.py:181
  22.7 16.4 %collective-permute-start.3 = (f32[96,2048]{1,0:T(8,128)S(1)}, f32[96,2048]{1,0:T(8,128)S(1)}, u32[]{:S(2)}, u32[]{:S(2)}) collective-permute-start(f32[96,2048]{1,0:T(8,128)S(1)} %collective-permute-done.1.refs_1_), channel_id=1, source_target_pairs={{0,4},{1,3},{2,6},{3,1},{4,0},{5,7},{6,2},{7,5},{8,12},{9,11},{10,... | collective-permute-start | bytes 2359304 | tf_op jit(solution)/shard_map/ppermute | solution.py:181
  27.8 17.3 %collective-permute-start.5 = (f32[96,2048]{1,0:T(8,128)S(1)}, f32[96,2048]{1,0:T(8,128)S(1)}, u32[]{:S(2)}, u32[]{:S(2)}) collective-permute-start(f32[96,2048]{1,0:T(8,128)S(1)} %get-tuple-element.89.refs_0_), channel_id=1, source_target_pairs={{0,2},{1,5},{2,0},{3,7},{4,6},{5,1},{6,4},{7,3},{8,10},{9,13},{10,... | collective-permute-start | bytes 2359304 | tf_op jit(solution)/shard_map/ppermute | solution.py:181
  40.0 19.1 %collective-permute-start.4 = (f32[96,2048]{1,0:T(8,128)S(1)}, f32[96,2048]{1,0:T(8,128)S(1)}, u32[]{:S(2)}, u32[]{:S(2)}) collective-permute-start(f32[96,2048]{1,0:T(8,128)S(1)} %get-tuple-element.89.refs_0_), channel_id=1, source_target_pairs={{0,4},{1,3},{2,6},{3,1},{4,0},{5,7},{6,2},{7,5},{8,12},{9,11},{10,... | collective-permute-start | bytes 2359304 | tf_op jit(solution)/shard_map/ppermute | solution.py:181
  45.1 26.8 %collective-permute-start.6 = (f32[96,2048]{1,0:T(8,128)S(1)}, f32[96,2048]{1,0:T(8,128)}, u32[]{:S(2)}, u32[]{:S(2)}) collective-permute-start(f32[96,2048]{1,0:T(8,128)S(1)} %collective-permute-done.5.refs_1_), channel_id=1, source_target_pairs={{0,4},{1,3},{2,6},{3,1},{4,0},{5,7},{6,2},{7,5},{8,12},{9,11},{10,... | collective-permute-start | bytes 2359304 | tf_op jit(solution)/shard_map/ppermute | solution.py:181
  57.7 14.1 %collective-permute-start.7 = (f32[2,96,768]{2,1,0:T(8,128)S(1)}, f32[2,96,768]{2,1,0:T(8,128)S(1)}, u32[]{:S(2)}, u32[]{:S(2)}) collective-permute-start(f32[2,96,768]{2,1,0:T(8,128)S(1)} %get-tuple-element.83), channel_id=1, source_target_pairs={{0,8},{8,0},{16,24},{24,16},{1,9},{9,1},{17,25},{25,17},{2,10},{10... | collective-permute-start | bytes 1769480 | tf_op jit(solution)/shard_map/ppermute | solution.py:22
  59.1 14.3 %collective-permute-start.9 = (f32[96,2048]{1,0:T(8,128)S(1)}, f32[96,2048]{1,0:T(8,128)S(1)}, u32[]{:S(2)}, u32[]{:S(2)}) collective-permute-start(f32[96,2048]{1,0:T(8,128)S(1)} %get-tuple-element.103.refs_0_), channel_id=1, source_target_pairs={{0,2},{1,5},{2,0},{3,7},{4,6},{5,1},{6,4},{7,3},{8,10},{9,13},{10,... | collective-permute-start | bytes 2359304 | tf_op jit(solution)/shard_map/ppermute | solution.py:181
  72.0 14.1 %collective-permute-start.8 = (f32[96,2048]{1,0:T(8,128)S(1)}, f32[96,2048]{1,0:T(8,128)S(1)}, u32[]{:S(2)}, u32[]{:S(2)}) collective-permute-start(f32[96,2048]{1,0:T(8,128)S(1)} %get-tuple-element.103.refs_0_), channel_id=1, source_target_pairs={{0,4},{1,3},{2,6},{3,1},{4,0},{5,7},{6,2},{7,5},{8,12},{9,11},{10,... | collective-permute-start | bytes 2359304 | tf_op jit(solution)/shard_map/ppermute | solution.py:181
  73.4 30.5 %collective-permute-start.10 = (f32[96,2048]{1,0:T(8,128)S(1)}, f32[96,2048]{1,0:T(8,128)S(1)}, u32[]{:S(2)}, u32[]{:S(2)}) collective-permute-start(f32[96,2048]{1,0:T(8,128)S(1)} %collective-permute-done.9.refs_1_), channel_id=1, source_target_pairs={{0,4},{1,3},{2,6},{3,1},{4,0},{5,7},{6,2},{7,5},{8,12},{9,11},{10,... | collective-permute-start | bytes 2359304 | tf_op jit(solution)/shard_map/ppermute | solution.py:181
  82.4 21.4 %collective-permute-start.11 = (f32[2,96,768]{2,1,0:T(8,128)S(1)}, f32[2,96,768]{2,1,0:T(8,128)S(1)}, u32[]{:S(2)}, u32[]{:S(2)}) collective-permute-start(f32[2,96,768]{2,1,0:T(8,128)S(1)} %get-tuple-element.93), channel_id=1, source_target_pairs={{0,8},{8,0},{16,24},{24,16},{1,9},{9,1},{17,25},{25,17},{2,10},{10... | collective-permute-start | bytes 1769480 | tf_op jit(solution)/shard_map/ppermute | solution.py:22
  83.8 20.1 %collective-permute-start.12 = (f32[1,96,768]{2,1,0:T(8,128)S(1)}, f32[1,96,768]{2,1,0:T(8,128)S(1)}, u32[]{:S(2)}, u32[]{:S(2)}) collective-permute-start(f32[1,96,768]{2,1,0:T(8,128)S(1)} %get-tuple-element.97), channel_id=1, source_target_pairs={{0,16},{8,24},{16,0},{24,8},{1,17},{9,25},{17,1},{25,9},{2,18},{10... | collective-permute-start | bytes 884744 | tf_op jit(solution)/shard_map/ppermute | solution.py:22
  86.1 26.9 %collective-permute-start.14 = (f32[64,2048]{1,0:T(8,128)S(1)}, f32[64,2048]{1,0:T(8,128)S(1)}, u32[]{:S(2)}, u32[]{:S(2)}) collective-permute-start(f32[64,2048]{1,0:T(8,128)S(1)} %copy-done.10), channel_id=1, source_target_pairs={{0,2},{1,5},{2,0},{3,7},{4,6},{5,1},{6,4},{7,3},{8,10},{9,13},{10,... | collective-permute-start | bytes 1572872 | tf_op jit(solution)/shard_map/ppermute | solution.py:181
  103.9 12.0 %collective-permute-start.13 = (f32[64,2048]{1,0:T(8,128)S(1)}, f32[64,2048]{1,0:T(8,128)S(1)}, u32[]{:S(2)}, u32[]{:S(2)}) collective-permute-start(f32[64,2048]{1,0:T(8,128)S(1)} %copy-done.10), channel_id=1, source_target_pairs={{0,4},{1,3},{2,6},{3,1},{4,0},{5,7},{6,2},{7,5},{8,12},{9,11},{10,... | collective-permute-start | bytes 1572872 | tf_op jit(solution)/shard_map/ppermute | solution.py:181
  110.7 19.4 %collective-permute-start.16 = (f32[2,96,768]{2,1,0:T(8,128)S(1)}, f32[2,96,768]{2,1,0:T(8,128)S(1)}, u32[]{:S(2)}, u32[]{:S(2)}) collective-permute-start(f32[2,96,768]{2,1,0:T(8,128)S(1)} %get-tuple-element.107), channel_id=1, source_target_pairs={{0,8},{8,0},{16,24},{24,16},{1,9},{9,1},{17,25},{25,17},{2,10},{10... | collective-permute-start | bytes 1769480 | tf_op jit(solution)/shard_map/ppermute | solution.py:22
  113.0 17.3 %collective-permute-start.15 = (f32[64,2048]{1,0:T(8,128)S(1)}, f32[64,2048]{1,0:T(8,128)S(1)}, u32[]{:S(2)}, u32[]{:S(2)}) collective-permute-start(f32[64,2048]{1,0:T(8,128)S(1)} %collective-permute-done.14.refs_1_), channel_id=1, source_target_pairs={{0,4},{1,3},{2,6},{3,1},{4,0},{5,7},{6,2},{7,5},{8,12},{9,11},{10,... | collective-permute-start | bytes 1572872 | tf_op jit(solution)/shard_map/ppermute | solution.py:181
  114.4 15.8 %collective-permute-start.17 = (f32[1,96,768]{2,1,0:T(8,128)S(1)}, f32[1,96,768]{2,1,0:T(8,128)S(1)}, u32[]{:S(2)}, u32[]{:S(2)}) collective-permute-start(f32[1,96,768]{2,1,0:T(8,128)S(1)} %get-tuple-element.111), channel_id=1, source_target_pairs={{0,16},{8,24},{16,0},{24,8},{1,17},{9,25},{17,1},{25,9},{2,18},{10... | collective-permute-start | bytes 884744 | tf_op jit(solution)/shard_map/ppermute | solution.py:22
  115.9 23.7 %collective-permute-start.19 = (f32[32,2048]{1,0:T(8,128)S(1)}, f32[32,2048]{1,0:T(8,128)S(1)}, u32[]{:S(2)}, u32[]{:S(2)}) collective-permute-start(f32[32,2048]{1,0:T(8,128)S(1)} %get-tuple-element.121.refs_0_), channel_id=1, source_target_pairs={{0,2},{1,5},{2,0},{3,7},{4,6},{5,1},{6,4},{7,3},{8,10},{9,13},{10,... | collective-permute-start | bytes 786440 | tf_op jit(solution)/shard_map/ppermute | solution.py:181
  135.5 17.5 %collective-permute-start.18 = (f32[2,64,768]{2,1,0:T(8,128)S(1)}, f32[2,64,768]{2,1,0:T(8,128)S(1)}, u32[]{:S(2)}, u32[]{:S(2)}) collective-permute-start(f32[2,64,768]{2,1,0:T(8,128)S(1)} %get-tuple-element.118), channel_id=1, source_target_pairs={{0,8},{8,0},{16,24},{24,16},{1,9},{9,1},{17,25},{25,17},{2,10},{10... | collective-permute-start | bytes 1179656 | tf_op jit(solution)/shard_map/ppermute | solution.py:22
  151.0 9.6 %collective-permute-start.23 = (f32[1,96,768]{2,1,0:T(8,128)S(1)}, f32[1,96,768]{2,1,0:T(8,128)S(1)}, u32[]{:S(2)}, u32[]{:S(2)}) collective-permute-start(f32[1,96,768]{2,1,0:T(8,128)S(1)} %get-tuple-element.128), channel_id=1, source_target_pairs={{0,16},{8,24},{16,0},{24,8},{1,17},{9,25},{17,1},{25,9},{2,18},{10... | collective-permute-start | bytes 884744 | tf_op jit(solution)/shard_map/ppermute | solution.py:22
  153.0 22.0 %collective-permute-start.24 = (f32[1,64,768]{2,1,0:T(8,128)S(1)}, f32[1,64,768]{2,1,0:T(8,128)S(1)}, u32[]{:S(2)}, u32[]{:S(2)}) collective-permute-start(f32[1,64,768]{2,1,0:T(8,128)S(1)} %get-tuple-element.129), channel_id=1, source_target_pairs={{0,16},{8,24},{16,0},{24,8},{1,17},{9,25},{17,1},{25,9},{2,18},{10... | collective-permute-start | bytes 589832 | tf_op jit(solution)/shard_map/ppermute | solution.py:22
  158.9 18.3 %collective-permute-start.25 = (f32[1,32,768]{2,1,0:T(8,128)S(1)}, f32[1,32,768]{2,1,0:T(8,128)S(1)}, u32[]{:S(2)}, u32[]{:S(2)}) collective-permute-start(f32[1,32,768]{2,1,0:T(8,128)S(1)} %get-tuple-element.130), channel_id=1, source_target_pairs={{0,16},{8,24},{16,0},{24,8},{1,17},{9,25},{17,1},{25,9},{2,18},{10... | collective-permute-start | bytes 294920 | tf_op jit(solution)/shard_map/ppermute | solution.py:22
  183.8 12.5 %collective-permute-start.27 = (f32[16,768]{1,0:T(8,128)S(1)}, f32[16,768]{1,0:T(8,128)S(1)}, u32[]{:S(2)}, u32[]{:S(2)}) collective-permute-start(f32[16,768]{1,0:T(8,128)S(1)} %fusion.1), channel_id=1, source_target_pairs={{1,0},{2,1},{3,2},{4,3},{5,4},{6,5},{7,6},{9,8},{10,9},{11,10},{12... | collective-permute-start | bytes 147464 | tf_op jit(solution)/shard_map/ppermute | solution.py:28
  (17 other events, 90.3 us)

commit v2 on v1

--- a/solution.py
+++ b/solution.py
@@ -10,11 +10,11 @@
 WINDOW = 16
 PARTS = (3, 3, 3, 2, 1)
 DEPTH = 512
-MEMORY = 48 * 2**20
-
-
-def params():
-    return pltpu.CompilerParams(vmem_limit_bytes=MEMORY)
+MEMORY = 10 * 2**20
+
+
+def params(factor=1):
+    return pltpu.CompilerParams(vmem_limit_bytes=factor * MEMORY)
 
 
 def swapped(block, bit, axis="tm"):
@@ -109,7 +109,7 @@
         out_specs=[pl.BlockSpec(shape, lambda k: (0, 0, 0))] * 2,
         out_shape=[jax.ShapeDtypeStruct(shape, jnp.float32)] * 2,
         scratch_shapes=[pltpu.VMEM((chips * width, 2 * block), jnp.float32)],
-        compiler_params=params(),
+        compiler_params=params(chips // 2),
         cost_estimate=pl.CostEstimate(flops=1, bytes_accessed=1, transcendentals=0),
     )(place, own, mate, *pieces)
 
@@ -221,18 +221,20 @@
             if k == 2:
                 tied["mate"] = mate
             i = last[0] if last[1] == 2 else -1
-            if i >= 1:
-                tied["halved"] = halve(*firsts[i - 1])
-            if i >= 2:
-                tied["second"] = seconds[i - 2]
+            half = last[0] - 2 if last[1] == 0 and last[0] < count - 1 else -1
+            late = last[0] - 3 if last[1] == 1 else -1
+            if half in firsts:
+                tied["halved"] = halve(*firsts[half])
+            if late in seconds:
+                tied["second"] = seconds[late]
             tied = lax.optimization_barrier(tied)
             chunks[j], got[last] = tied["chunk"], tied["got"]
             mate = tied.get("mate", mate)
-            if i >= 1:
-                halved[i - 1] = tied["halved"]
-                halving(i - 1)
-            if i >= 2:
-                seconds[i - 2] = tied["second"]
+            if half in firsts:
+                halved[half] = tied["halved"]
+                halving(half)
+            if late in seconds:
+                seconds[late] = tied["second"]
         if step == 0:
             got[j, 0] = routed(chunks[j], (0, 1))
         elif step == 1:
@@ -242,6 +244,18 @@
         if k >= 2 and i >= 0:
             product(i)
     for i in range(len(firsts), count):
+        tied = {"place": place}
+        if i - 2 not in halved:
+            tied["halved"] = halve(*firsts[i - 2])
+        if i - 3 in seconds:
+            tied["second"] = seconds[i - 3]
+        tied = lax.optimization_barrier(tied)
+        place = tied["place"]
+        if i - 2 not in halved:
+            halved[i - 2] = tied["halved"]
+            halving(i - 2)
+        if i - 3 in seconds:
+            seconds[i - 3] = tied["second"]
         product(i)
     for i in range(count):
         if i not in halved:

time: 201 us -> 183 us (0.910)
  waiting for transfers between devices: 107 us -> 80.8 us
  starting transfers between devices: 45.6 us -> 53.7 us
  local copies, waits for them, and re-layouts: 9.82 us -> 17.2 us
  Pallas kernels: 35.9 us -> 30.6 us
    ppermute x12, waiting for transfers between devices: 64.6 us -> 30.5 us  [swapped(): return lax.ppermute(block, axis, [(i, i ^ bit) for i in range(size)])]
    ppermute x12, starting transfers between devices: 15.9 us -> 27.6 us  [swapped(): return lax.ppermute(block, axis, [(i, i ^ bit) for i in range(size)])]
    ppermute x15, waiting for transfers between devices: 36.2 us -> 43.9 us  [routed(): lax.ppermute(block, 'tm', [(i, i ^ 2 << ways[i % 2]) for i in range(size)])]
    unnamed x22 -> x36, local copies, waits for them, and re-layouts: 8.9 us -> 16.3 us
    pallas_call x5, Pallas kernels: 29.3 us -> 25.1 us  [multiply(): pl.pallas_call(functools.partial(multiply_kernel, steps), grid=(steps,),...]
    ppermute x15, starting transfers between devices: 23.1 us -> 19.4 us  [routed(): lax.ppermute(block, 'tm', [(i, i ^ 2 << ways[i % 2]) for i in range(size)])]
  transfers between devices with their start and end apart: 30 -> 30, of which waited for: 16 -> 19; matrix products, arithmetic and copies ran while one was open for 0% -> 0% of each run, Pallas kernels for 17% -> 15%
where the time goes in v2:
time: 183 us
  waiting for transfers between devices  80.8 us (44%)
  starting transfers between devices  53.7 us (29%)
  Pallas kernels  30.6 us (17%)
  local copies, waits for them, and re-layouts  17.2 us (9%)
    ppermute x15, waiting for transfers between devices, routed(): lax.ppermute(block, 'tm', [(i, i ^ 2 << ways[i % 2]) for i in range(size)])  43.9 us
    ppermute x12, waiting for transfers between devices, swapped(): return lax.ppermute(block, axis, [(i, i ^ bit) for i in range(size)])  30.5 us
    ppermute x12, starting transfers between devices, swapped(): return lax.ppermute(block, axis, [(i, i ^ bit) for i in range(size)])  27.6 us
    pallas_call x5, Pallas kernels, multiply(): pl.pallas_call(functools.partial(multiply_kernel, steps), grid=(steps,),...  25.1 us
    ppermute x15, starting transfers between devices, routed(): lax.ppermute(block, 'tm', [(i, i ^ 2 << ways[i % 2]) for i in range(size)])  19.4 us
    unnamed x36, local copies, waits for them, and re-layouts  16.3 us
    ppermute x3, starting transfers between devices, shifted(): return lax.ppermute(block, axis, route)  6.68 us
    ppermute x3, waiting for transfers between devices, shifted(): return lax.ppermute(block, axis, route)  6.35 us
  transfers between devices with their start and end apart: 30, of which 19 were waited for; matrix products, arithmetic and copies ran while one was open for 0% of the time, Pallas kernels for 15%

profile of v2, /device:TPU:1, one launch (start us, length us, event | category | flops | bytes accessed | tf_op | source)
XLA Modules:
  0.0 182.7 jit_solution(18365120031956368084)
XLA Ops:
  5.0 2.7 %collective-permute-start.1 = (f32[96,2048]{1,0:T(8,128)S(1)}, f32[96,2048]{1,0:T(8,128)S(1)}, u32[]{:S(2)}, u32[]{:S(2)}) collective-permute-start(f32[96,2048]{1,0:T(8,128)S(1)} %get-tuple-element.83.refs_0_), channel_id=1, source_target_pairs={{0,2},{1,5},{2,0},{3,7},{4,6},{5,1},{6,4},{7,3},{8,10},{9,13},{10,... | collective-permute-start | bytes 2359304 | tf_op jit(solution)/shard_map/ppermute | solution.py:181
  9.8 13.7 %collective-permute-done.1.refs_1_ = f32[96,2048]{1,0:T(8,128)S(1)} collective-permute-done((f32[96,2048]{1,0:T(8,128)S(1)}, f32[96,2048]{1,0:T(8,128)S(1)}, u32[]{:S(2)}, u32[]{:S(2)}) %collective-permute-start.1) | collective-permute-done | bytes 786464 | tf_op jit(solution)/shard_map/ppermute | solution.py:181
  25.1 3.3 %collective-permute-start.3 = (f32[96,2048]{1,0:T(8,128)S(1)}, f32[96,2048]{1,0:T(8,128)S(1)}, u32[]{:S(2)}, u32[]{:S(2)}) collective-permute-start(f32[96,2048]{1,0:T(8,128)S(1)} %collective-permute-done.1.refs_1_), channel_id=1, source_target_pairs={{0,4},{1,3},{2,6},{3,1},{4,0},{5,7},{6,2},{7,5},{8,12},{9,11},{10,... | collective-permute-start | bytes 2359304 | tf_op jit(solution)/shard_map/ppermute | solution.py:181
  31.0 10.7 %collective-permute-done.3.refs_3_ = f32[96,2048]{1,0:T(8,128)S(1)} collective-permute-done((f32[96,2048]{1,0:T(8,128)S(1)}, f32[96,2048]{1,0:T(8,128)S(1)}, u32[]{:S(2)}, u32[]{:S(2)}) %collective-permute-start.3) | collective-permute-done | bytes 786464 | tf_op jit(solution)/shard_map/ppermute | solution.py:181
  45.0 2.7 %collective-permute-done.5.refs_1_ = f32[96,2048]{1,0:T(8,128)} collective-permute-done((f32[96,2048]{1,0:T(8,128)S(1)}, f32[96,2048]{1,0:T(8,128)}, u32[]{:S(2)}, u32[]{:S(2)}) %collective-permute-start.5) | collective-permute-done | bytes 786464 | tf_op jit(solution)/shard_map/ppermute | solution.py:181
  49.1 5.9 %collective-permute-done.4.refs_2_ = f32[96,2048]{1,0:T(8,128)S(1)} collective-permute-done((f32[96,2048]{1,0:T(8,128)S(1)}, f32[96,2048]{1,0:T(8,128)S(1)}, u32[]{:S(2)}, u32[]{:S(2)}) %collective-permute-start.4) | collective-permute-done | bytes 786464 | tf_op jit(solution)/shard_map/ppermute | solution.py:181
  63.0 5.7 %shard_map.18 = (f32[2,96,768]{2,1,0:T(8,128)S(1)}, f32[2,96,768]{2,1,0:T(8,128)S(1)}) custom-call(s32[4]{0:T(128)S(1)} %add_xor_fusion.place, f32[2048,384]{1,0:T(8,128)S(1)} %copy-done.1, f32[2048,384]{1,0:T(8,128)S(1)} %copy-done.3, f32[96,2048]{1,0:T(8,128)S(1)} %copy-done.9, f32[96,2048]{1,0:T(8,128)S(1)} %copy-done.11, f32[96,2048]{1,0:T(8,128)S(1)} %copy-done.13, ...), custom_call_target="tpu_custom_call" | custom-call | flops 1 | bytes 1 | tf_op jit(solution)/shard_map/pallas_call | solution.py:104
  71.6 6.0 %collective-permute-done.9.came = f32[2,96,768]{2,1,0:T(8,128)S(1)} collective-permute-done((f32[2,96,768]{2,1,0:T(8,128)S(1)}, f32[2,96,768]{2,1,0:T(8,128)S(1)}, u32[]{:S(2)}, u32[]{:S(2)}) %collective-permute-start.9) | collective-permute-done | bytes 589856 | tf_op jit(solution)/shard_map/ppermute | solution.py:22
  79.2 6.1 %shard_map.22 = (f32[2,96,768]{2,1,0:T(8,128)S(1)}, f32[2,96,768]{2,1,0:T(8,128)S(1)}) custom-call(s32[4]{0:T(128)S(1)} %add_xor_fusion.place, f32[2048,384]{1,0:T(8,128)S(1)} %copy-done.1, f32[2048,384]{1,0:T(8,128)S(1)} %copy-done.3, f32[96,2048]{1,0:T(8,128)S(1)} %copy-done.5, f32[96,2048]{1,0:T(8,128)} %collective-permute-done.5.refs_1_, ...), custom_call_target="tpu_custom_call" | custom-call | flops 1 | bytes 1 | tf_op jit(solution)/shard_map/pallas_call | solution.py:104
  87.3 4.6 %collective-permute-done.10.refs_3_ = f32[96,2048]{1,0:T(8,128)S(1)} collective-permute-done((f32[96,2048]{1,0:T(8,128)}, f32[96,2048]{1,0:T(8,128)S(1)}, u32[]{:S(2)}, u32[]{:S(2)}) %collective-permute-start.10) | collective-permute-done | bytes 786464 | tf_op jit(solution)/shard_map/ppermute | solution.py:181
  94.7 2.3 %collective-permute-start.12 = (f32[1,96,768]{2,1,0:T(8,128)S(1)}, f32[1,96,768]{2,1,0:T(8,128)S(1)}, u32[]{:S(2)}, u32[]{:S(2)}) collective-permute-start(f32[1,96,768]{2,1,0:T(8,128)S(1)} %get-tuple-element.93), channel_id=1, source_target_pairs={{0,16},{8,24},{16,0},{24,8},{1,17},{9,25},{17,1},{25,9},{2,18},{10... | collective-permute-start | bytes 884744 | tf_op jit(solution)/shard_map/ppermute | solution.py:22
  97.0 4.0 %collective-permute-done.14.refs_1_ = f32[64,2048]{1,0:T(8,128)S(1)} collective-permute-done((f32[64,2048]{1,0:T(8,128)S(1)}, f32[64,2048]{1,0:T(8,128)S(1)}, u32[]{:S(2)}, u32[]{:S(2)}) %collective-permute-start.14) | collective-permute-done | bytes 524320 | tf_op jit(solution)/shard_map/ppermute | solution.py:181
  101.1 6.1 %shard_map.20 = (f32[2,96,768]{2,1,0:T(8,128)S(1)}, f32[2,96,768]{2,1,0:T(8,128)S(1)}) custom-call(s32[4]{0:T(128)S(1)} %add_xor_fusion.place, f32[2048,384]{1,0:T(8,128)S(1)} %copy-done.1, f32[2048,384]{1,0:T(8,128)S(1)} %copy-done.3, f32[96,2048]{1,0:T(8,128)} %get-tuple-element.95.refs_0_, f32[96,2048]{1,0:T(8,128)} %collective-permute-done.8.refs_1_, ...), custom_call_target="tpu_custom_call" | custom-call | flops 1 | bytes 1 | tf_op jit(solution)/shard_map/pallas_call | solution.py:104
  112.7 4.3 %shard_map.24 = (f32[2,64,768]{2,1,0:T(8,128)S(1)}, f32[2,64,768]{2,1,0:T(8,128)S(1)}) custom-call(s32[4]{0:T(128)S(1)} %add_xor_fusion.place, f32[2048,384]{1,0:T(8,128)S(1)} %copy-done.1, f32[2048,384]{1,0:T(8,128)S(1)} %copy-done.3, f32[64,2048]{1,0:T(8,128)S(1)} %copy-done.17, f32[64,2048]{1,0:T(8,128)S(1)} %collective-permute-done.14.refs_1_, ...), custom_call_target="tpu_custom_call" | custom-call | flops 1 | bytes 1 | tf_op jit(solution)/shard_map/pallas_call | solution.py:104
  118.8 3.4 %collective-permute-done.13.came = f32[2,96,768]{2,1,0:T(8,128)S(1)} collective-permute-done((f32[2,96,768]{2,1,0:T(8,128)S(1)}, f32[2,96,768]{2,1,0:T(8,128)S(1)}, u32[]{:S(2)}, u32[]{:S(2)}) %collective-permute-start.13) | collective-permute-done | bytes 589856 | tf_op jit(solution)/shard_map/ppermute | solution.py:22
  122.3 2.5 %collective-permute-done.16.refs_6_ = f32[1,96,768]{2,1,0:T(8,128)S(1)} collective-permute-done((f32[1,96,768]{2,1,0:T(8,128)S(1)}, f32[1,96,768]{2,1,0:T(8,128)S(1)}, u32[]{:S(2)}, u32[]{:S(2)}) %collective-permute-start.16) | collective-permute-done | bytes 294944 | tf_op jit(solution)/shard_map/ppermute | solution.py:22
  125.7 2.9 %shard_map.26 = (f32[2,32,768]{2,1,0:T(8,128)S(1)}, f32[2,32,768]{2,1,0:T(8,128)S(1)}) custom-call(s32[4]{0:T(128)S(1)} %add_xor_fusion.place, f32[2048,384]{1,0:T(8,128)S(1)} %copy-done.1, f32[2048,384]{1,0:T(8,128)S(1)} %copy-done.3, f32[32,2048]{1,0:T(8,128)S(1)} %get-tuple-element.123.refs_0_, f32[32,2048]{1,0:T(8,128)S(1)} %collective-permute-done.19.refs_1_, ...), custom_call_target="tpu_custom_call" | custom-call | flops 1 | bytes 1 | tf_op jit(solution)/shard_map/pallas_call | solution.py:104
  132.1 5.0 %collective-permute-done.18.came = f32[2,64,768]{2,1,0:T(8,128)S(1)} collective-permute-done((f32[2,64,768]{2,1,0:T(8,128)S(1)}, f32[2,64,768]{2,1,0:T(8,128)S(1)}, u32[]{:S(2)}, u32[]{:S(2)}) %collective-permute-start.18) | collective-permute-done | bytes 393248 | tf_op jit(solution)/shard_map/ppermute | solution.py:22
  137.1 4.1 %collective-permute-done.22.came = f32[2,32,768]{2,1,0:T(8,128)S(1)} collective-permute-done((f32[2,32,768]{2,1,0:T(8,128)S(1)}, f32[2,32,768]{2,1,0:T(8,128)S(1)}, u32[]{:S(2)}, u32[]{:S(2)}) %collective-permute-start.22) | collective-permute-done | bytes 196640 | tf_op jit(solution)/shard_map/ppermute | solution.py:22
  141.4 5.0 %collective-permute-done.24.refs_8_ = f32[1,64,768]{2,1,0:T(8,128)S(1)} collective-permute-done((f32[1,64,768]{2,1,0:T(8,128)S(1)}, f32[1,64,768]{2,1,0:T(8,128)S(1)}, u32[]{:S(2)}, u32[]{:S(2)}) %collective-permute-start.24) | collective-permute-done | bytes 196640 | tf_op jit(solution)/shard_map/ppermute | solution.py:22
  148.8 15.6 %collective-permute-start.26 = (f32[384,384]{0,1:T(8,128)S(1)}, f32[384,384]{0,1:T(8,128)S(1)}, u32[]{:S(2)}, u32[]{:S(2)}) collective-permute-start(f32[384,384]{0,1:T(8,128)S(1)} %copy.2), channel_id=1, source_target_pairs={{0,1},{1,0},{2,3},{3,2},{4,5},{5,4},{6,7},{7,6},{8,9},{9,8},{10,11... | collective-permute-start | bytes 1769480 | tf_op jit(solution)/shard_map/ppermute | solution.py:22
  169.8 4.4 %collective-permute-done.28 = f32[16,384]{0,1:T(8,128)S(1)} collective-permute-done((f32[16,384]{0,1:T(8,128)S(1)}, f32[16,384]{0,1:T(8,128)S(1)}, u32[]{:S(2)}, u32[]{:S(2)}) %collective-permute-start.28) | collective-permute-done | bytes 24608 | tf_op jit(solution)/shard_map/ppermute | solution.py:28
  174.2 3.1 %collective-permute-start.29 = (f32[16,16]{1,0:T(8,128)S(1)}, f32[16,16]{1,0:T(8,128)S(1)}, u32[]{:S(2)}, u32[]{:S(2)}) collective-permute-start(f32[16,16]{1,0:T(8,128)S(1)} %slice.20), channel_id=1, source_target_pairs={{1,0},{2,1},{3,2},{4,3},{5,4},{6,5},{7,6},{9,8},{10,9},{11,10},{12... | collective-permute-start | bytes 3080 | tf_op jit(solution)/shard_map/ppermute | solution.py:28
  179.8 2.9 %shard_map.29 = f32[384,768]{1,0:T(8,128)} custom-call(f32[768,384]{1,0:T(8,128)S(1)} %copy.5.turned, f32[16,768]{1,0:T(8,128)S(1)} %collective-permute-done.27.below, f32[16,384]{1,0:T(8,128)S(1)} %copy.6.beside, f32[16,16]{1,0:T(8,128)S(1)} %collective-permute-done.29.corner), custom_call_target="tpu_custom_call" | custom-call | tf_op jit(solution)/shard_map/pallas_call | solution.py:136
  (96 shorter events, 55.7 us)
Async XLA Ops:
  0.0 23.5 %collective-permute-start.2 = (f32[2048,384]{1,0:T(8,128)}, f32[2048,384]{1,0:T(8,128)S(1)}, u32[]{:S(2)}, u32[]{:S(2)}) collective-permute-start(f32[2048,384]{1,0:T(8,128)} %own.9), channel_id=1, source_target_pairs={{0,1},{1,0},{2,3},{3,2},{4,5},{5,4},{6,7},{7,6},{8,9},{9,8},{10,11... | collective-permute-start | bytes 9437192 | tf_op jit(solution)/shard_map/ppermute | solution.py:22
  5.0 18.5 %collective-permute-start.1 = (f32[96,2048]{1,0:T(8,128)S(1)}, f32[96,2048]{1,0:T(8,128)S(1)}, u32[]{:S(2)}, u32[]{:S(2)}) collective-permute-start(f32[96,2048]{1,0:T(8,128)S(1)} %get-tuple-element.83.refs_0_), channel_id=1, source_target_pairs={{0,2},{1,5},{2,0},{3,7},{4,6},{5,1},{6,4},{7,3},{8,10},{9,13},{10,... | collective-permute-start | bytes 2359304 | tf_op jit(solution)/shard_map/ppermute | solution.py:181
  7.7 21.6 %collective-permute-start = (f32[96,2048]{1,0:T(8,128)S(1)}, f32[96,2048]{1,0:T(8,128)S(1)}, u32[]{:S(2)}, u32[]{:S(2)}) collective-permute-start(f32[96,2048]{1,0:T(8,128)S(1)} %get-tuple-element.83.refs_0_), channel_id=1, source_target_pairs={{0,4},{1,3},{2,6},{3,1},{4,0},{5,7},{6,2},{7,5},{8,12},{9,11},{10,... | collective-permute-start | bytes 2359304 | tf_op jit(solution)/shard_map/ppermute | solution.py:181
  25.1 16.5 %collective-permute-start.3 = (f32[96,2048]{1,0:T(8,128)S(1)}, f32[96,2048]{1,0:T(8,128)S(1)}, u32[]{:S(2)}, u32[]{:S(2)}) collective-permute-start(f32[96,2048]{1,0:T(8,128)S(1)} %collective-permute-done.1.refs_1_), channel_id=1, source_target_pairs={{0,4},{1,3},{2,6},{3,1},{4,0},{5,7},{6,2},{7,5},{8,12},{9,11},{10,... | collective-permute-start | bytes 2359304 | tf_op jit(solution)/shard_map/ppermute | solution.py:181
  30.3 17.4 %collective-permute-start.5 = (f32[96,2048]{1,0:T(8,128)S(1)}, f32[96,2048]{1,0:T(8,128)}, u32[]{:S(2)}, u32[]{:S(2)}) collective-permute-start(f32[96,2048]{1,0:T(8,128)S(1)} %get-tuple-element.102.refs_0_), channel_id=1, source_target_pairs={{0,2},{1,5},{2,0},{3,7},{4,6},{5,1},{6,4},{7,3},{8,10},{9,13},{10,... | collective-permute-start | bytes 2359304 | tf_op jit(solution)/shard_map/ppermute | solution.py:181
  42.5 12.4 %collective-permute-start.4 = (f32[96,2048]{1,0:T(8,128)S(1)}, f32[96,2048]{1,0:T(8,128)S(1)}, u32[]{:S(2)}, u32[]{:S(2)}) collective-permute-start(f32[96,2048]{1,0:T(8,128)S(1)} %get-tuple-element.102.refs_0_), channel_id=1, source_target_pairs={{0,4},{1,3},{2,6},{3,1},{4,0},{5,7},{6,2},{7,5},{8,12},{9,11},{10,... | collective-permute-start | bytes 2359304 | tf_op jit(solution)/shard_map/ppermute | solution.py:181
  47.6 22.5 %collective-permute-start.6 = (f32[96,2048]{1,0:T(8,128)}, f32[96,2048]{1,0:T(8,128)}, u32[]{:S(2)}, u32[]{:S(2)}) collective-permute-start(f32[96,2048]{1,0:T(8,128)} %collective-permute-done.5.refs_1_), channel_id=1, source_target_pairs={{0,4},{1,3},{2,6},{3,1},{4,0},{5,7},{6,2},{7,5},{8,12},{9,11},{10,... | collective-permute-start | bytes 2359304 | tf_op jit(solution)/shard_map/ppermute | solution.py:181
  55.8 21.8 %collective-permute-start.8 = (f32[96,2048]{1,0:T(8,128)}, f32[96,2048]{1,0:T(8,128)}, u32[]{:S(2)}, u32[]{:S(2)}) collective-permute-start(f32[96,2048]{1,0:T(8,128)} %get-tuple-element.95.refs_0_), channel_id=1, source_target_pairs={{0,2},{1,5},{2,0},{3,7},{4,6},{5,1},{6,4},{7,3},{8,10},{9,13},{10,... | collective-permute-start | bytes 2359304 | tf_op jit(solution)/shard_map/ppermute | solution.py:181
  70.1 17.0 %collective-permute-start.7 = (f32[96,2048]{1,0:T(8,128)}, f32[96,2048]{1,0:T(8,128)S(1)}, u32[]{:S(2)}, u32[]{:S(2)}) collective-permute-start(f32[96,2048]{1,0:T(8,128)} %get-tuple-element.95.refs_0_), channel_id=1, source_target_pairs={{0,4},{1,3},{2,6},{3,1},{4,0},{5,7},{6,2},{7,5},{8,12},{9,11},{10,... | collective-permute-start | bytes 2359304 | tf_op jit(solution)/shard_map/ppermute | solution.py:181
  77.6 14.2 %collective-permute-start.10 = (f32[96,2048]{1,0:T(8,128)}, f32[96,2048]{1,0:T(8,128)S(1)}, u32[]{:S(2)}, u32[]{:S(2)}) collective-permute-start(f32[96,2048]{1,0:T(8,128)} %collective-permute-done.8.refs_1_), channel_id=1, source_target_pairs={{0,4},{1,3},{2,6},{3,1},{4,0},{5,7},{6,2},{7,5},{8,12},{9,11},{10,... | collective-permute-start | bytes 2359304 | tf_op jit(solution)/shard_map/ppermute | solution.py:181
  85.3 9.3 %collective-permute-start.15 = (f32[2,96,768]{2,1,0:T(8,128)S(1)}, f32[2,96,768]{2,1,0:T(8,128)S(1)}, u32[]{:S(2)}, u32[]{:S(2)}) collective-permute-start(f32[2,96,768]{2,1,0:T(8,128)S(1)} %get-tuple-element.106), channel_id=1, source_target_pairs={{0,8},{8,0},{16,24},{24,16},{1,9},{9,1},{17,25},{25,17},{2,10},{10... | collective-permute-start | bytes 1769480 | tf_op jit(solution)/shard_map/ppermute | solution.py:22
  87.1 14.0 %collective-permute-start.14 = (f32[64,2048]{1,0:T(8,128)S(1)}, f32[64,2048]{1,0:T(8,128)S(1)}, u32[]{:S(2)}, u32[]{:S(2)}) collective-permute-start(f32[64,2048]{1,0:T(8,128)S(1)} %copy-done.17), channel_id=1, source_target_pairs={{0,2},{1,5},{2,0},{3,7},{4,6},{5,1},{6,4},{7,3},{8,10},{9,13},{10,... | collective-permute-start | bytes 1572872 | tf_op jit(solution)/shard_map/ppermute | solution.py:181
  91.8 15.6 %collective-permute-start.11 = (f32[64,2048]{1,0:T(8,128)S(1)}, f32[64,2048]{1,0:T(8,128)S(1)}, u32[]{:S(2)}, u32[]{:S(2)}) collective-permute-start(f32[64,2048]{1,0:T(8,128)S(1)} %copy-done.17), channel_id=1, source_target_pairs={{0,4},{1,3},{2,6},{3,1},{4,0},{5,7},{6,2},{7,5},{8,12},{9,11},{10,... | collective-permute-start | bytes 1572872 | tf_op jit(solution)/shard_map/ppermute | solution.py:181
  94.7 12.7 %collective-permute-start.12 = (f32[1,96,768]{2,1,0:T(8,128)S(1)}, f32[1,96,768]{2,1,0:T(8,128)S(1)}, u32[]{:S(2)}, u32[]{:S(2)}) collective-permute-start(f32[1,96,768]{2,1,0:T(8,128)S(1)} %get-tuple-element.93), channel_id=1, source_target_pairs={{0,16},{8,24},{16,0},{24,8},{1,17},{9,25},{17,1},{25,9},{2,18},{10... | collective-permute-start | bytes 884744 | tf_op jit(solution)/shard_map/ppermute | solution.py:22
  101.1 11.6 %collective-permute-start.17 = (f32[64,2048]{1,0:T(8,128)S(1)}, f32[64,2048]{1,0:T(8,128)S(1)}, u32[]{:S(2)}, u32[]{:S(2)}) collective-permute-start(f32[64,2048]{1,0:T(8,128)S(1)} %collective-permute-done.14.refs_1_), channel_id=1, source_target_pairs={{0,4},{1,3},{2,6},{3,1},{4,0},{5,7},{6,2},{7,5},{8,12},{9,11},{10,... | collective-permute-start | bytes 1572872 | tf_op jit(solution)/shard_map/ppermute | solution.py:181
  107.2 15.0 %collective-permute-start.13 = (f32[2,96,768]{2,1,0:T(8,128)S(1)}, f32[2,96,768]{2,1,0:T(8,128)S(1)}, u32[]{:S(2)}, u32[]{:S(2)}) collective-permute-start(f32[2,96,768]{2,1,0:T(8,128)S(1)} %get-tuple-element.99), channel_id=1, source_target_pairs={{0,8},{8,0},{16,24},{24,16},{1,9},{9,1},{17,25},{25,17},{2,10},{10... | collective-permute-start | bytes 1769480 | tf_op jit(solution)/shard_map/ppermute | solution.py:22
  107.4 11.4 %collective-permute-start.19 = (f32[32,2048]{1,0:T(8,128)S(1)}, f32[32,2048]{1,0:T(8,128)S(1)}, u32[]{:S(2)}, u32[]{:S(2)}) collective-permute-start(f32[32,2048]{1,0:T(8,128)S(1)} %get-tuple-element.123.refs_0_), channel_id=1, source_target_pairs={{0,2},{1,5},{2,0},{3,7},{4,6},{5,1},{6,4},{7,3},{8,10},{9,13},{10,... | collective-permute-start | bytes 786440 | tf_op jit(solution)/shard_map/ppermute | solution.py:181
  108.9 15.9 %collective-permute-start.16 = (f32[1,96,768]{2,1,0:T(8,128)S(1)}, f32[1,96,768]{2,1,0:T(8,128)S(1)}, u32[]{:S(2)}, u32[]{:S(2)}) collective-permute-start(f32[1,96,768]{2,1,0:T(8,128)S(1)} %get-tuple-element.110), channel_id=1, source_target_pairs={{0,16},{8,24},{16,0},{24,8},{1,17},{9,25},{17,1},{25,9},{2,18},{10... | collective-permute-start | bytes 884744 | tf_op jit(solution)/shard_map/ppermute | solution.py:22
  117.0 20.1 %collective-permute-start.18 = (f32[2,64,768]{2,1,0:T(8,128)S(1)}, f32[2,64,768]{2,1,0:T(8,128)S(1)}, u32[]{:S(2)}, u32[]{:S(2)}) collective-permute-start(f32[2,64,768]{2,1,0:T(8,128)S(1)} %get-tuple-element.119), channel_id=1, source_target_pairs={{0,8},{8,0},{16,24},{24,16},{1,9},{9,1},{17,25},{25,17},{2,10},{10... | collective-permute-start | bytes 1179656 | tf_op jit(solution)/shard_map/ppermute | solution.py:22
  128.5 12.7 %collective-permute-start.22 = (f32[2,32,768]{2,1,0:T(8,128)S(1)}, f32[2,32,768]{2,1,0:T(8,128)S(1)}, u32[]{:S(2)}, u32[]{:S(2)}) collective-permute-start(f32[2,32,768]{2,1,0:T(8,128)S(1)} %get-tuple-element.126), channel_id=1, source_target_pairs={{0,8},{8,0},{16,24},{24,16},{1,9},{9,1},{17,25},{25,17},{2,10},{10... | collective-permute-start | bytes 589832 | tf_op jit(solution)/shard_map/ppermute | solution.py:22
  129.8 11.6 %collective-permute-start.23 = (f32[1,96,768]{2,1,0:T(8,128)S(1)}, f32[1,96,768]{2,1,0:T(8,128)S(1)}, u32[]{:S(2)}, u32[]{:S(2)}) collective-permute-start(f32[1,96,768]{2,1,0:T(8,128)S(1)} %get-tuple-element.130), channel_id=1, source_target_pairs={{0,16},{8,24},{16,0},{24,8},{1,17},{9,25},{17,1},{25,9},{2,18},{10... | collective-permute-start | bytes 884744 | tf_op jit(solution)/shard_map/ppermute | solution.py:22
  137.1 9.3 %collective-permute-start.24 = (f32[1,64,768]{2,1,0:T(8,128)S(1)}, f32[1,64,768]{2,1,0:T(8,128)S(1)}, u32[]{:S(2)}, u32[]{:S(2)}) collective-permute-start(f32[1,64,768]{2,1,0:T(8,128)S(1)} %get-tuple-element.131), channel_id=1, source_target_pairs={{0,16},{8,24},{16,0},{24,8},{1,17},{9,25},{17,1},{25,9},{2,18},{10... | collective-permute-start | bytes 589832 | tf_op jit(solution)/shard_map/ppermute | solution.py:22
  148.8 17.2 %collective-permute-start.26 = (f32[384,384]{0,1:T(8,128)S(1)}, f32[384,384]{0,1:T(8,128)S(1)}, u32[]{:S(2)}, u32[]{:S(2)}) collective-permute-start(f32[384,384]{0,1:T(8,128)S(1)} %copy.2), channel_id=1, source_target_pairs={{0,1},{1,0},{2,3},{3,2},{4,5},{5,4},{6,7},{7,6},{8,9},{9,8},{10,11... | collective-permute-start | bytes 1769480 | tf_op jit(solution)/shard_map/ppermute | solution.py:22
  167.5 12.3 %collective-permute-start.27 = (f32[16,768]{1,0:T(8,128)S(1)}, f32[16,768]{1,0:T(8,128)S(1)}, u32[]{:S(2)}, u32[]{:S(2)}) collective-permute-start(f32[16,768]{1,0:T(8,128)S(1)} %fusion.1), channel_id=1, source_target_pairs={{1,0},{2,1},{3,2},{4,3},{5,4},{6,5},{7,6},{9,8},{10,9},{11,10},{12... | collective-permute-start | bytes 147464 | tf_op jit(solution)/shard_map/ppermute | solution.py:28
  (24 other events, 150.9 us)

commit v3 on v2

--- a/solution.py
+++ b/solution.py
@@ -8,9 +8,10 @@
 from jax.sharding import PartitionSpec as P
 
 WINDOW = 16
+FLIGHT = 3
 PARTS = (3, 3, 3, 2, 1)
 DEPTH = 512
-MEMORY = 10 * 2**20
+MEMORY = 12 * 2**20
 
 
 def params(factor=1):
@@ -109,7 +110,7 @@
         out_specs=[pl.BlockSpec(shape, lambda k: (0, 0, 0))] * 2,
         out_shape=[jax.ShapeDtypeStruct(shape, jnp.float32)] * 2,
         scratch_shapes=[pltpu.VMEM((chips * width, 2 * block), jnp.float32)],
-        compiler_params=params(chips // 2),
+        compiler_params=params(5),
         cost_estimate=pl.CostEstimate(flops=1, bytes_accessed=1, transcendentals=0),
     )(place, own, mate, *pieces)
 
@@ -197,7 +198,8 @@
     chunks = list(turn(snapshots, [block * part // sum(PARTS) for part in PARTS]))
     mate = swapped(snapshots, 1)
     count = len(chunks)
-    steps = [(j, step) for j in range(count) for step in range(3)]
+    steps = [(0, 0)] + [(j + (step == 0), step) for j in range(count) for step in (1, 0, 2)]
+    steps.remove((count, 0))
     got, firsts, halved, seconds = {}, {}, {}, {}
 
     def product(j):
@@ -215,19 +217,24 @@
 
     for k, (j, step) in enumerate(steps):
         tied = {"chunk": chunks[j]}
-        if k >= 2:
-            last = steps[k - 2]
+        ready = -1
+        if k >= FLIGHT:
+            last = steps[k - FLIGHT]
             tied["got"] = got[last]
-            if k == 2:
+            if k == FLIGHT:
                 tied["mate"] = mate
-            i = last[0] if last[1] == 2 else -1
-            half = last[0] - 2 if last[1] == 0 and last[0] < count - 1 else -1
-            late = last[0] - 3 if last[1] == 1 else -1
+            if k > FLIGHT:
+                tied["before"] = chunks[steps[k - 1][0]]
+            ready = last[0] if last[1] == 2 else -1
+            half = len(firsts) - 2 if steps[k - FLIGHT - 1][1] == 2 and k > FLIGHT else -1
+            late = -1
             if half in firsts:
                 tied["halved"] = halve(*firsts[half])
             if late in seconds:
                 tied["second"] = seconds[late]
             tied = lax.optimization_barrier(tied)
+            if k > FLIGHT:
+                chunks[steps[k - 1][0]] = tied["before"]
             chunks[j], got[last] = tied["chunk"], tied["got"]
             mate = tied.get("mate", mate)
             if half in firsts:
@@ -241,8 +248,8 @@
             got[j, 1] = routed(chunks[j], (1, 0))
         else:
             got[j, 2] = routed(got[j, 0], (1, 0))
-        if k >= 2 and i >= 0:
-            product(i)
+        if ready >= 0:
+            product(ready)
     for i in range(len(firsts), count):
         tied = {"place": place}
         if i - 2 not in halved:

time: 183 us -> 192 us (1.049)
  waiting for transfers between devices: 80.8 us -> 103 us
  starting transfers between devices: 53.7 us -> 38.5 us
  Pallas kernels: 30.6 us -> 43.2 us
  local copies, waits for them, and re-layouts: 17.2 us -> 5.23 us
    ppermute x12, starting transfers between devices: 27.6 us -> 13.3 us  [swapped(): return lax.ppermute(block, axis, [(i, i ^ bit) for i in range(size)])]
    ppermute x12, waiting for transfers between devices: 30.5 us -> 42.5 us  [swapped(): return lax.ppermute(block, axis, [(i, i ^ bit) for i in range(size)])]
    unnamed x36, local copies, waits for them, and re-layouts: 16.3 us -> 4.3 us
    pallas_call x5, Pallas kernels: 25.1 us -> 36.3 us  [multiply(): pl.pallas_call(functools.partial(multiply_kernel, steps), grid=(steps,),...]
    ppermute x15, waiting for transfers between devices: 43.9 us -> 54.4 us  [routed(): lax.ppermute(block, 'tm', [(i, i ^ 2 << ways[i % 2]) for i in range(size)])]
  transfers between devices with their start and end apart: 30 -> 30, of which waited for: 19 -> 17; matrix products, arithmetic and copies ran while one was open for 0% -> 1% of each run, Pallas kernels for 15% -> 21%
where the time goes in v3:
time: 192 us; the launch traced here: 191 us
  waiting for transfers between devices  103 us (54%)
  Pallas kernels  43.2 us (22%)
  starting transfers between devices  38.5 us (20%)
  local copies, waits for them, and re-layouts  5.23 us (3%)
    ppermute x15, waiting for transfers between devices, routed(): lax.ppermute(block, 'tm', [(i, i ^ 2 << ways[i % 2]) for i in range(size)])  54.4 us
    ppermute x12, waiting for transfers between devices, swapped(): return lax.ppermute(block, axis, [(i, i ^ bit) for i in range(size)])  42.5 us
    pallas_call x5, Pallas kernels, multiply(): pl.pallas_call(functools.partial(multiply_kernel, steps), grid=(steps,),...  36.3 us
    ppermute x15, starting transfers between devices, routed(): lax.ppermute(block, 'tm', [(i, i ^ 2 << ways[i % 2]) for i in range(size)])  18.5 us
    ppermute x12, starting transfers between devices, swapped(): return lax.ppermute(block, axis, [(i, i ^ bit) for i in range(size)])  13.3 us
    ppermute x3, starting transfers between devices, shifted(): return lax.ppermute(block, axis, route)  6.68 us
    ppermute x3, waiting for transfers between devices, shifted(): return lax.ppermute(block, axis, route)  6.29 us
    unnamed x36, local copies, waits for them, and re-layouts  4.3 us
  transfers between devices with their start and end apart: 30, of which 17 were waited for; matrix products, arithmetic and copies ran while one was open for 1% of the time, Pallas kernels for 21%

profile of v3, /device:TPU:1, one launch (start us, length us, event | category | flops | bytes accessed | tf_op | source)
XLA Modules:
  0.0 191.2 jit_solution(18170417203201222246)
XLA Ops:
  1.9 2.2 %shard_map.17 = (f32[96,2048]{1,0:T(8,128)S(1)}, f32[96,2048]{1,0:T(8,128)S(1)}, f32[96,2048]{1,0:T(8,128)S(1)}, f32[64,2048]{1,0:T(8,128)S(1)}, f32[32,2048]{1,0:T(8,128)}) custom-call(f32[2048,384]{1,0:T(8,128)S(1)} %copy-done), custom_call_target="tpu_custom_call" | custom-call | tf_op jit(solution)/shard_map/pallas_call | solution.py:49
  4.2 2.8 %collective-permute-start = (f32[96,2048]{1,0:T(8,128)S(1)}, f32[96,2048]{1,0:T(8,128)S(1)}, u32[]{:S(2)}, u32[]{:S(2)}) collective-permute-start(f32[96,2048]{1,0:T(8,128)S(1)} %get-tuple-element.97.refs_0_), channel_id=1, source_target_pairs={{0,2},{1,5},{2,0},{3,7},{4,6},{5,1},{6,4},{7,3},{8,10},{9,13},{10,... | collective-permute-start | bytes 2359304 | tf_op jit(solution)/shard_map/ppermute | solution.py:182
  8.4 14.5 %collective-permute-done.refs_1_ = f32[96,2048]{1,0:T(8,128)S(1)} collective-permute-done((f32[96,2048]{1,0:T(8,128)S(1)}, f32[96,2048]{1,0:T(8,128)S(1)}, u32[]{:S(2)}, u32[]{:S(2)}) %collective-permute-start) | collective-permute-done | bytes 786464 | tf_op jit(solution)/shard_map/ppermute | solution.py:182
  22.9 3.3 %collective-permute-start.4 = (f32[96,2048]{1,0:T(8,128)S(1)}, f32[96,2048]{1,0:T(8,128)S(1)}, u32[]{:S(2)}, u32[]{:S(2)}) collective-permute-start(f32[96,2048]{1,0:T(8,128)S(1)} %collective-permute-done.refs_1_), channel_id=1, source_target_pairs={{0,4},{1,3},{2,6},{3,1},{4,0},{5,7},{6,2},{7,5},{8,12},{9,11},{10,... | collective-permute-start | bytes 2359304 | tf_op jit(solution)/shard_map/ppermute | solution.py:182
  27.7 10.7 %collective-permute-done.3.refs_1_ = f32[96,2048]{1,0:T(8,128)} collective-permute-done((f32[96,2048]{1,0:T(8,128)S(1)}, f32[96,2048]{1,0:T(8,128)}, u32[]{:S(2)}, u32[]{:S(2)}) %collective-permute-start.3) | collective-permute-done | bytes 786464 | tf_op jit(solution)/shard_map/ppermute | solution.py:182
  42.0 15.3 %collective-permute-done.5.refs_2_ = f32[96,2048]{1,0:T(8,128)S(1)} collective-permute-done((f32[96,2048]{1,0:T(8,128)S(1)}, f32[96,2048]{1,0:T(8,128)S(1)}, u32[]{:S(2)}, u32[]{:S(2)}) %collective-permute-start.5) | collective-permute-done | bytes 786464 | tf_op jit(solution)/shard_map/ppermute | solution.py:182
  59.7 8.1 %shard_map.18 = (f32[2,96,768]{2,1,0:T(8,128)}, f32[2,96,768]{2,1,0:T(8,128)}) custom-call(s32[4]{0:T(128)} %add_xor_fusion.place, f32[2048,384]{1,0:T(8,128)} %own.9, f32[2048,384]{1,0:T(8,128)} %copy-done.12, f32[96,2048]{1,0:T(8,128)} %copy-done.3, f32[96,2048]{1,0:T(8,128)} %copy-done.14, f32[96,2048]{1,0:T(8,128)} %collective-permute-done.2.refs_2_, ...), custom_call_target="tpu_custom_call" | custom-call | flops 1 | bytes 1 | tf_op jit(solution)/shard_map/pallas_call | solution.py:105
  70.8 8.1 %shard_map.22 = (f32[2,96,768]{2,1,0:T(8,128)}, f32[2,96,768]{2,1,0:T(8,128)}) custom-call(s32[4]{0:T(128)} %add_xor_fusion.place, f32[2048,384]{1,0:T(8,128)} %own.9, f32[2048,384]{1,0:T(8,128)} %copy-done.12, f32[96,2048]{1,0:T(8,128)} %copy-done.2, f32[96,2048]{1,0:T(8,128)} %collective-permute-done.3.refs_1_, f32[96,2048]{1,0:T(8,128)} %copy-done.13, ...), custom_call_target="tpu_custom_call" | custom-call | flops 1 | bytes 1 | tf_op jit(solution)/shard_map/pallas_call | solution.py:105
  84.2 5.7 %collective-permute-done.12.refs_3_ = f32[96,2048]{1,0:T(8,128)} collective-permute-done((f32[96,2048]{1,0:T(8,128)}, f32[96,2048]{1,0:T(8,128)}, u32[]{:S(2)}, u32[]{:S(2)}) %collective-permute-start.12) | collective-permute-done | bytes 786464 | tf_op jit(solution)/shard_map/ppermute | solution.py:182
  89.9 8.0 %shard_map.20 = (f32[2,96,768]{2,1,0:T(8,128)}, f32[2,96,768]{2,1,0:T(8,128)}) custom-call(s32[4]{0:T(128)} %add_xor_fusion.place, f32[2048,384]{1,0:T(8,128)} %own.9, f32[2048,384]{1,0:T(8,128)} %copy-done.12, f32[96,2048]{1,0:T(8,128)} %copy-done.1, f32[96,2048]{1,0:T(8,128)} %collective-permute-done.6.refs_1_, f32[96,2048]{1,0:T(8,128)} %collective-permute-done.8.refs_2_, ...), custom_call_target="tpu_custom_call" | custom-call | flops 1 | bytes 1 | tf_op jit(solution)/shard_map/pallas_call | solution.py:105
  99.7 2.3 %collective-permute-start.10 = (f32[1,96,768]{2,1,0:T(8,128)S(1)}, f32[1,96,768]{2,1,0:T(8,128)S(1)}, u32[]{:S(2)}, u32[]{:S(2)}) collective-permute-start(f32[1,96,768]{2,1,0:T(8,128)S(1)} %copy-done.11), channel_id=1, source_target_pairs={{0,16},{8,24},{16,0},{24,8},{1,17},{9,25},{17,1},{25,9},{2,18},{10... | collective-permute-start | bytes 884744 | tf_op jit(solution)/shard_map/ppermute | solution.py:23
  103.9 15.3 %collective-permute-done.10.refs_5_ = f32[1,96,768]{2,1,0:T(8,128)S(1)} collective-permute-done((f32[1,96,768]{2,1,0:T(8,128)S(1)}, f32[1,96,768]{2,1,0:T(8,128)S(1)}, u32[]{:S(2)}, u32[]{:S(2)}) %collective-permute-start.10) | collective-permute-done | bytes 294944 | tf_op jit(solution)/shard_map/ppermute | solution.py:23
  119.2 6.8 %shard_map.24 = (f32[2,64,768]{2,1,0:T(8,128)}, f32[2,64,768]{2,1,0:T(8,128)}) custom-call(s32[4]{0:T(128)} %add_xor_fusion.place, f32[2048,384]{1,0:T(8,128)} %own.9, f32[2048,384]{1,0:T(8,128)} %copy-done.12, f32[64,2048]{1,0:T(8,128)} %copy-done.7, f32[64,2048]{1,0:T(8,128)} %collective-permute-done.11.refs_1_, ...), custom_call_target="tpu_custom_call" | custom-call | flops 1 | bytes 1 | tf_op jit(solution)/shard_map/pallas_call | solution.py:105
  125.9 3.2 %collective-permute-start.18 = (f32[2,64,768]{2,1,0:T(8,128)}, f32[2,64,768]{2,1,0:T(8,128)S(1)}, u32[]{:S(2)}, u32[]{:S(2)}) collective-permute-start(f32[2,64,768]{2,1,0:T(8,128)} %get-tuple-element.137), channel_id=1, source_target_pairs={{0,8},{8,0},{16,24},{24,16},{1,9},{9,1},{17,25},{25,17},{2,10},{10... | collective-permute-start | bytes 1179656 | tf_op jit(solution)/shard_map/ppermute | solution.py:23
  131.3 3.3 %collective-permute-done.21.refs_3_ = f32[32,2048]{1,0:T(8,128)S(1)} collective-permute-done((f32[32,2048]{1,0:T(8,128)S(1)}, f32[32,2048]{1,0:T(8,128)S(1)}, u32[]{:S(2)}, u32[]{:S(2)}) %collective-permute-start.21) | collective-permute-done | bytes 262176 | tf_op jit(solution)/shard_map/ppermute | solution.py:182
  135.3 2.2 %collective-permute-done.20.refs_2_ = f32[32,2048]{1,0:T(8,128)} collective-permute-done((f32[32,2048]{1,0:T(8,128)}, f32[32,2048]{1,0:T(8,128)}, u32[]{:S(2)}, u32[]{:S(2)}) %collective-permute-start.20) | collective-permute-done | bytes 262176 | tf_op jit(solution)/shard_map/ppermute | solution.py:182
  137.5 5.4 %shard_map.26 = (f32[2,32,768]{2,1,0:T(8,128)}, f32[2,32,768]{2,1,0:T(8,128)}) custom-call(s32[4]{0:T(128)} %add_xor_fusion.place, f32[2048,384]{1,0:T(8,128)} %own.9, f32[2048,384]{1,0:T(8,128)} %copy-done.12, f32[32,2048]{1,0:T(8,128)} %get-tuple-element.141.refs_0_, f32[32,2048]{1,0:T(8,128)} %copy-done.16, f32[32,2048]{1,0:T(8,128)} %collective-permute-done.20.refs_2_, ...), custom_call_target="tpu_custom_call" | custom-call | flops 1 | bytes 1 | tf_op jit(solution)/shard_map/pallas_call | solution.py:105
  145.5 6.0 %collective-permute-done.22.came = f32[2,32,768]{2,1,0:T(8,128)S(1)} collective-permute-done((f32[2,32,768]{2,1,0:T(8,128)}, f32[2,32,768]{2,1,0:T(8,128)S(1)}, u32[]{:S(2)}, u32[]{:S(2)}) %collective-permute-start.22) | collective-permute-done | bytes 196640 | tf_op jit(solution)/shard_map/ppermute | solution.py:23
  152.5 15.6 %collective-permute-done.24.refs_8_ = f32[1,64,768]{2,1,0:T(8,128)S(1)} collective-permute-done((f32[1,64,768]{2,1,0:T(8,128)S(1)}, f32[1,64,768]{2,1,0:T(8,128)S(1)}, u32[]{:S(2)}, u32[]{:S(2)}) %collective-permute-start.24) | collective-permute-done | bytes 196640 | tf_op jit(solution)/shard_map/ppermute | solution.py:23
  170.6 2.3 %collective-permute-start.26 = (f32[384,384]{0,1:T(8,128)S(1)}, f32[384,384]{0,1:T(8,128)S(1)}, u32[]{:S(2)}, u32[]{:S(2)}) collective-permute-start(f32[384,384]{0,1:T(8,128)S(1)} %copy.2), channel_id=1, source_target_pairs={{0,1},{1,0},{2,3},{3,2},{4,5},{5,4},{6,7},{7,6},{8,9},{9,8},{10,11... | collective-permute-start | bytes 1769480 | tf_op jit(solution)/shard_map/ppermute | solution.py:23
  176.0 2.3 %collective-permute-start.27 = (f32[16,768]{1,0:T(8,128)S(1)}, f32[16,768]{1,0:T(8,128)S(1)}, u32[]{:S(2)}, u32[]{:S(2)}) collective-permute-start(f32[16,768]{1,0:T(8,128)S(1)} %fusion.1), channel_id=1, source_target_pairs={{1,0},{2,1},{3,2},{4,3},{5,4},{6,5},{7,6},{9,8},{10,9},{11,10},{12... | collective-permute-start | bytes 147464 | tf_op jit(solution)/shard_map/ppermute | solution.py:29
  178.3 4.4 %collective-permute-done.28 = f32[16,384]{0,1:T(8,128)S(1)} collective-permute-done((f32[16,384]{0,1:T(8,128)S(1)}, f32[16,384]{0,1:T(8,128)S(1)}, u32[]{:S(2)}, u32[]{:S(2)}) %collective-permute-start.28) | collective-permute-done | bytes 24608 | tf_op jit(solution)/shard_map/ppermute | solution.py:29
  182.7 3.1 %collective-permute-start.29 = (f32[16,16]{1,0:T(8,128)S(1)}, f32[16,16]{1,0:T(8,128)S(1)}, u32[]{:S(2)}, u32[]{:S(2)}) collective-permute-start(f32[16,16]{1,0:T(8,128)S(1)} %slice.20), channel_id=1, source_target_pairs={{1,0},{2,1},{3,2},{4,3},{5,4},{6,5},{7,6},{9,8},{10,9},{11,10},{12... | collective-permute-start | bytes 3080 | tf_op jit(solution)/shard_map/ppermute | solution.py:29
  188.3 2.9 %shard_map.29 = f32[384,768]{1,0:T(8,128)} custom-call(f32[768,384]{1,0:T(8,128)S(1)} %copy.5.turned, f32[16,768]{1,0:T(8,128)S(1)} %collective-permute-done.27.below, f32[16,384]{1,0:T(8,128)S(1)} %copy.6.beside, f32[16,16]{1,0:T(8,128)S(1)} %collective-permute-done.29.corner), custom_call_target="tpu_custom_call" | custom-call | tf_op jit(solution)/shard_map/pallas_call | solution.py:137
  (96 shorter events, 37.4 us)
Async XLA Ops:
  0.0 22.9 %collective-permute-start.1 = (f32[2048,384]{1,0:T(8,128)}, f32[2048,384]{1,0:T(8,128)S(1)}, u32[]{:S(2)}, u32[]{:S(2)}) collective-permute-start(f32[2048,384]{1,0:T(8,128)} %own.9), channel_id=1, source_target_pairs={{0,1},{1,0},{2,3},{3,2},{4,5},{5,4},{6,7},{7,6},{8,9},{9,8},{10,11... | collective-permute-start | bytes 9437192 | tf_op jit(solution)/shard_map/ppermute | solution.py:23
  4.2 18.7 %collective-permute-start = (f32[96,2048]{1,0:T(8,128)S(1)}, f32[96,2048]{1,0:T(8,128)S(1)}, u32[]{:S(2)}, u32[]{:S(2)}) collective-permute-start(f32[96,2048]{1,0:T(8,128)S(1)} %get-tuple-element.97.refs_0_), channel_id=1, source_target_pairs={{0,2},{1,5},{2,0},{3,7},{4,6},{5,1},{6,4},{7,3},{8,10},{9,13},{10,... | collective-permute-start | bytes 2359304 | tf_op jit(solution)/shard_map/ppermute | solution.py:182
  6.9 19.7 %collective-permute-start.2 = (f32[96,2048]{1,0:T(8,128)S(1)}, f32[96,2048]{1,0:T(8,128)}, u32[]{:S(2)}, u32[]{:S(2)}) collective-permute-start(f32[96,2048]{1,0:T(8,128)S(1)} %get-tuple-element.97.refs_0_), channel_id=1, source_target_pairs={{0,4},{1,3},{2,6},{3,1},{4,0},{5,7},{6,2},{7,5},{8,12},{9,11},{10,... | collective-permute-start | bytes 2359304 | tf_op jit(solution)/shard_map/ppermute | solution.py:182
  8.1 30.3 %collective-permute-start.3 = (f32[96,2048]{1,0:T(8,128)S(1)}, f32[96,2048]{1,0:T(8,128)}, u32[]{:S(2)}, u32[]{:S(2)}) collective-permute-start(f32[96,2048]{1,0:T(8,128)S(1)} %get-tuple-element.122.refs_0_), channel_id=1, source_target_pairs={{0,2},{1,5},{2,0},{3,7},{4,6},{5,1},{6,4},{7,3},{8,10},{9,13},{10,... | collective-permute-start | bytes 2359304 | tf_op jit(solution)/shard_map/ppermute | solution.py:182
  22.9 19.1 %collective-permute-start.4 = (f32[96,2048]{1,0:T(8,128)S(1)}, f32[96,2048]{1,0:T(8,128)S(1)}, u32[]{:S(2)}, u32[]{:S(2)}) collective-permute-start(f32[96,2048]{1,0:T(8,128)S(1)} %collective-permute-done.refs_1_), channel_id=1, source_target_pairs={{0,4},{1,3},{2,6},{3,1},{4,0},{5,7},{6,2},{7,5},{8,12},{9,11},{10,... | collective-permute-start | bytes 2359304 | tf_op jit(solution)/shard_map/ppermute | solution.py:182
  26.6 30.7 %collective-permute-start.5 = (f32[96,2048]{1,0:T(8,128)S(1)}, f32[96,2048]{1,0:T(8,128)S(1)}, u32[]{:S(2)}, u32[]{:S(2)}) collective-permute-start(f32[96,2048]{1,0:T(8,128)S(1)} %get-tuple-element.122.refs_0_), channel_id=1, source_target_pairs={{0,4},{1,3},{2,6},{3,1},{4,0},{5,7},{6,2},{7,5},{8,12},{9,11},{10,... | collective-permute-start | bytes 2359304 | tf_op jit(solution)/shard_map/ppermute | solution.py:182
  38.5 30.1 %collective-permute-start.6 = (f32[96,2048]{1,0:T(8,128)S(1)}, f32[96,2048]{1,0:T(8,128)}, u32[]{:S(2)}, u32[]{:S(2)}) collective-permute-start(f32[96,2048]{1,0:T(8,128)S(1)} %get-tuple-element.107.refs_0_), channel_id=1, source_target_pairs={{0,2},{1,5},{2,0},{3,7},{4,6},{5,1},{6,4},{7,3},{8,10},{9,13},{10,... | collective-permute-start | bytes 2359304 | tf_op jit(solution)/shard_map/ppermute | solution.py:182
  39.6 31.1 %collective-permute-start.7 = (f32[96,2048]{1,0:T(8,128)}, f32[96,2048]{1,0:T(8,128)}, u32[]{:S(2)}, u32[]{:S(2)}) collective-permute-start(f32[96,2048]{1,0:T(8,128)} %collective-permute-done.3.refs_1_), channel_id=1, source_target_pairs={{0,4},{1,3},{2,6},{3,1},{4,0},{5,7},{6,2},{7,5},{8,12},{9,11},{10,... | collective-permute-start | bytes 2359304 | tf_op jit(solution)/shard_map/ppermute | solution.py:182
  57.3 24.6 %collective-permute-start.8 = (f32[96,2048]{1,0:T(8,128)S(1)}, f32[96,2048]{1,0:T(8,128)}, u32[]{:S(2)}, u32[]{:S(2)}) collective-permute-start(f32[96,2048]{1,0:T(8,128)S(1)} %get-tuple-element.107.refs_0_), channel_id=1, source_target_pairs={{0,4},{1,3},{2,6},{3,1},{4,0},{5,7},{6,2},{7,5},{8,12},{9,11},{10,... | collective-permute-start | bytes 2359304 | tf_op jit(solution)/shard_map/ppermute | solution.py:182
  67.8 13.4 %collective-permute-start.9 = (f32[2,96,768]{2,1,0:T(8,128)}, f32[2,96,768]{2,1,0:T(8,128)S(1)}, u32[]{:S(2)}, u32[]{:S(2)}) collective-permute-start(f32[2,96,768]{2,1,0:T(8,128)} %get-tuple-element.101), channel_id=1, source_target_pairs={{0,8},{8,0},{16,24},{24,16},{1,9},{9,1},{17,25},{25,17},{2,10},{10... | collective-permute-start | bytes 1769480 | tf_op jit(solution)/shard_map/ppermute | solution.py:23
  68.6 21.3 %collective-permute-start.12 = (f32[96,2048]{1,0:T(8,128)}, f32[96,2048]{1,0:T(8,128)}, u32[]{:S(2)}, u32[]{:S(2)}) collective-permute-start(f32[96,2048]{1,0:T(8,128)} %collective-permute-done.6.refs_1_), channel_id=1, source_target_pairs={{0,4},{1,3},{2,6},{3,1},{4,0},{5,7},{6,2},{7,5},{8,12},{9,11},{10,... | collective-permute-start | bytes 2359304 | tf_op jit(solution)/shard_map/ppermute | solution.py:182
  69.5 14.1 %collective-permute-start.11 = (f32[64,2048]{1,0:T(8,128)S(1)}, f32[64,2048]{1,0:T(8,128)}, u32[]{:S(2)}, u32[]{:S(2)}) collective-permute-start(f32[64,2048]{1,0:T(8,128)S(1)} %get-tuple-element.133.refs_0_), channel_id=1, source_target_pairs={{0,2},{1,5},{2,0},{3,7},{4,6},{5,1},{6,4},{7,3},{8,10},{9,13},{10,... | collective-permute-start | bytes 1572872 | tf_op jit(solution)/shard_map/ppermute | solution.py:182
  78.8 23.2 %collective-permute-start.15 = (f32[2,96,768]{2,1,0:T(8,128)}, f32[2,96,768]{2,1,0:T(8,128)S(1)}, u32[]{:S(2)}, u32[]{:S(2)}) collective-permute-start(f32[2,96,768]{2,1,0:T(8,128)} %get-tuple-element.126), channel_id=1, source_target_pairs={{0,8},{8,0},{16,24},{24,16},{1,9},{9,1},{17,25},{25,17},{2,10},{10... | collective-permute-start | bytes 1769480 | tf_op jit(solution)/shard_map/ppermute | solution.py:23
  81.9 21.9 %collective-permute-start.14 = (f32[64,2048]{1,0:T(8,128)S(1)}, f32[64,2048]{1,0:T(8,128)}, u32[]{:S(2)}, u32[]{:S(2)}) collective-permute-start(f32[64,2048]{1,0:T(8,128)S(1)} %get-tuple-element.133.refs_0_), channel_id=1, source_target_pairs={{0,4},{1,3},{2,6},{3,1},{4,0},{5,7},{6,2},{7,5},{8,12},{9,11},{10,... | collective-permute-start | bytes 1572872 | tf_op jit(solution)/shard_map/ppermute | solution.py:182
  83.7 35.5 %collective-permute-start.17 = (f32[64,2048]{1,0:T(8,128)}, f32[64,2048]{1,0:T(8,128)}, u32[]{:S(2)}, u32[]{:S(2)}) collective-permute-start(f32[64,2048]{1,0:T(8,128)} %collective-permute-done.11.refs_1_), channel_id=1, source_target_pairs={{0,4},{1,3},{2,6},{3,1},{4,0},{5,7},{6,2},{7,5},{8,12},{9,11},{10,... | collective-permute-start | bytes 1572872 | tf_op jit(solution)/shard_map/ppermute | solution.py:182
  97.9 32.6 %collective-permute-start.13 = (f32[2,96,768]{2,1,0:T(8,128)}, f32[2,96,768]{2,1,0:T(8,128)S(1)}, u32[]{:S(2)}, u32[]{:S(2)}) collective-permute-start(f32[2,96,768]{2,1,0:T(8,128)} %get-tuple-element.116), channel_id=1, source_target_pairs={{0,8},{8,0},{16,24},{24,16},{1,9},{9,1},{17,25},{25,17},{2,10},{10... | collective-permute-start | bytes 1769480 | tf_op jit(solution)/shard_map/ppermute | solution.py:23
  99.7 19.4 %collective-permute-start.10 = (f32[1,96,768]{2,1,0:T(8,128)S(1)}, f32[1,96,768]{2,1,0:T(8,128)S(1)}, u32[]{:S(2)}, u32[]{:S(2)}) collective-permute-start(f32[1,96,768]{2,1,0:T(8,128)S(1)} %copy-done.11), channel_id=1, source_target_pairs={{0,16},{8,24},{16,0},{24,8},{1,17},{9,25},{17,1},{25,9},{2,18},{10... | collective-permute-start | bytes 884744 | tf_op jit(solution)/shard_map/ppermute | solution.py:23
  102.0 27.0 %collective-permute-start.19 = (f32[32,2048]{1,0:T(8,128)}, f32[32,2048]{1,0:T(8,128)S(1)}, u32[]{:S(2)}, u32[]{:S(2)}) collective-permute-start(f32[32,2048]{1,0:T(8,128)} %get-tuple-element.141.refs_0_), channel_id=1, source_target_pairs={{0,2},{1,5},{2,0},{3,7},{4,6},{5,1},{6,4},{7,3},{8,10},{9,13},{10,... | collective-permute-start | bytes 786440 | tf_op jit(solution)/shard_map/ppermute | solution.py:182
  103.8 27.5 %collective-permute-start.16 = (f32[1,96,768]{2,1,0:T(8,128)}, f32[1,96,768]{2,1,0:T(8,128)S(1)}, u32[]{:S(2)}, u32[]{:S(2)}) collective-permute-start(f32[1,96,768]{2,1,0:T(8,128)} %get-tuple-element.130), channel_id=1, source_target_pairs={{0,16},{8,24},{16,0},{24,8},{1,17},{9,25},{17,1},{25,9},{2,18},{10... | collective-permute-start | bytes 884744 | tf_op jit(solution)/shard_map/ppermute | solution.py:23
  125.9 18.4 %collective-permute-start.18 = (f32[2,64,768]{2,1,0:T(8,128)}, f32[2,64,768]{2,1,0:T(8,128)S(1)}, u32[]{:S(2)}, u32[]{:S(2)}) collective-permute-start(f32[2,64,768]{2,1,0:T(8,128)} %get-tuple-element.137), channel_id=1, source_target_pairs={{0,8},{8,0},{16,24},{24,16},{1,9},{9,1},{17,25},{25,17},{2,10},{10... | collective-permute-start | bytes 1179656 | tf_op jit(solution)/shard_map/ppermute | solution.py:23
  143.0 27.3 %collective-permute-start.23 = (f32[1,96,768]{2,1,0:T(8,128)}, f32[1,96,768]{2,1,0:T(8,128)S(1)}, u32[]{:S(2)}, u32[]{:S(2)}) collective-permute-start(f32[1,96,768]{2,1,0:T(8,128)} %get-tuple-element.148), channel_id=1, source_target_pairs={{0,16},{8,24},{16,0},{24,8},{1,17},{9,25},{17,1},{25,9},{2,18},{10... | collective-permute-start | bytes 884744 | tf_op jit(solution)/shard_map/ppermute | solution.py:23
  144.4 23.8 %collective-permute-start.24 = (f32[1,64,768]{2,1,0:T(8,128)S(1)}, f32[1,64,768]{2,1,0:T(8,128)S(1)}, u32[]{:S(2)}, u32[]{:S(2)}) collective-permute-start(f32[1,64,768]{2,1,0:T(8,128)S(1)} %get-tuple-element.149), channel_id=1, source_target_pairs={{0,16},{8,24},{16,0},{24,8},{1,17},{9,25},{17,1},{25,9},{2,18},{10... | collective-permute-start | bytes 589832 | tf_op jit(solution)/shard_map/ppermute | solution.py:23
  152.4 17.8 %collective-permute-start.25 = (f32[1,32,768]{2,1,0:T(8,128)S(1)}, f32[1,32,768]{2,1,0:T(8,128)S(1)}, u32[]{:S(2)}, u32[]{:S(2)}) collective-permute-start(f32[1,32,768]{2,1,0:T(8,128)S(1)} %get-tuple-element.150), channel_id=1, source_target_pairs={{0,16},{8,24},{16,0},{24,8},{1,17},{9,25},{17,1},{25,9},{2,18},{10... | collective-permute-start | bytes 294920 | tf_op jit(solution)/shard_map/ppermute | solution.py:23
  176.0 12.2 %collective-permute-start.27 = (f32[16,768]{1,0:T(8,128)S(1)}, f32[16,768]{1,0:T(8,128)S(1)}, u32[]{:S(2)}, u32[]{:S(2)}) collective-permute-start(f32[16,768]{1,0:T(8,128)S(1)} %fusion.1), channel_id=1, source_target_pairs={{1,0},{2,1},{3,2},{4,3},{5,4},{6,5},{7,6},{9,8},{10,9},{11,10},{12... | collective-permute-start | bytes 147464 | tf_op jit(solution)/shard_map/ppermute | solution.py:29
  (24 other events, 489.1 us)

commit v4 on v3

--- a/solution.py
+++ b/solution.py
@@ -56,14 +56,23 @@
     )(source)
 
 
-def multiply_kernel(steps, place, own, mate, *refs):
-    *pieces, keep, send, total = refs
+def multiply_kernel(steps, count, place, own, mate, *refs):
+    pieces, (*earlier, keep, send, total) = refs[:count], refs[count:]
     step = pl.program_id(0)
     left_high, left_low = split(jnp.concatenate([piece[...] for piece in pieces], 0))
     right_high, right_low = split(jnp.concatenate([own[...], mate[...]], 1))
     left = jnp.concatenate([left_high, left_low, left_high], 1)
     right = jnp.concatenate([right_high, right_high, right_low], 0)
     partial = jnp.dot(left, right, preferred_element_type=jnp.float32)
+
+    if earlier:
+        kept, came, first, second = earlier
+
+        @pl.when(step == 0)
+        def _():
+            half = first.shape[0]
+            first[...] = kept[:half] + came[:half]
+            second[...] = kept[half:] + came[half:]
 
     @pl.when(step == 0)
     def _():
@@ -95,24 +104,27 @@
                 send[slot] = block
 
 
-def multiply(place, own, mate, pieces):
+def multiply(place, own, mate, pieces, earlier):
     depth, block = own.shape
     steps = depth // DEPTH
     width = pieces[0].shape[0]
     chips = sum(piece.shape[0] for piece in pieces) // width
     shape = (chips // 2, width, 2 * block)
+    shapes = [(array.shape[0] // 2,) + array.shape[1:] for array in earlier] + [shape] * 2
+    whole = lambda shape: pl.BlockSpec(shape, lambda k: (0, 0, 0))
     right = pl.BlockSpec((DEPTH, block), lambda k: (k, 0))
     return pl.pallas_call(
-        functools.partial(multiply_kernel, steps),
+        functools.partial(multiply_kernel, steps, len(pieces)),
         grid=(steps,),
         in_specs=[pl.BlockSpec(memory_space=pltpu.SMEM), right, right]
-        + [pl.BlockSpec((p.shape[0], DEPTH), lambda k: (0, k)) for p in pieces],
-        out_specs=[pl.BlockSpec(shape, lambda k: (0, 0, 0))] * 2,
-        out_shape=[jax.ShapeDtypeStruct(shape, jnp.float32)] * 2,
+        + [pl.BlockSpec((p.shape[0], DEPTH), lambda k: (0, k)) for p in pieces]
+        + [whole(array.shape) for array in earlier],
+        out_specs=[whole(shape) for shape in shapes],
+        out_shape=[jax.ShapeDtypeStruct(shape, jnp.float32) for shape in shapes],
         scratch_shapes=[pltpu.VMEM((chips * width, 2 * block), jnp.float32)],
         compiler_params=params(5),
         cost_estimate=pl.CostEstimate(flops=1, bytes_accessed=1, transcendentals=0),
-    )(place, own, mate, *pieces)
+    )(place, own, mate, *pieces, *earlier)
 
 
 def window_kernel(scale, turned, below, beside, corner, out, wide):
@@ -200,20 +212,18 @@
     count = len(chunks)
     steps = [(0, 0)] + [(j + (step == 0), step) for j in range(count) for step in (1, 0, 2)]
     steps.remove((count, 0))
-    got, firsts, halved, seconds = {}, {}, {}, {}
-
-    def product(j):
+    got, firsts, seconds = {}, {}, {}
+
+    def product(j, earlier=()):
         pieces = [chunks[j]] + [got[j, step] for step in range(3)]
         bit = 4
         while bit < chips:
             pieces += [swapped(piece, 2 * bit) for piece in pieces]
             bit *= 2
-        keep, send = multiply(place, snapshots, mate, pieces)
+        *halved, keep, send = multiply(place, snapshots, mate, pieces, earlier)
         firsts[j] = keep, swapped(send, 1, "space")
-
-    def halving(j):
-        keep, send = halved[j]
-        seconds[j] = keep, swapped(send, 2, "space")
+        if halved:
+            seconds[j - 1] = halved[0], swapped(halved[1], 2, "space")
 
     for k, (j, step) in enumerate(steps):
         tied = {"chunk": chunks[j]}
@@ -225,23 +235,12 @@
                 tied["mate"] = mate
             if k > FLIGHT:
                 tied["before"] = chunks[steps[k - 1][0]]
-            ready = last[0] if last[1] == 2 else -1
-            half = len(firsts) - 2 if steps[k - FLIGHT - 1][1] == 2 and k > FLIGHT else -1
-            late = -1
-            if half in firsts:
-                tied["halved"] = halve(*firsts[half])
-            if late in seconds:
-                tied["second"] = seconds[late]
+            ready = k // FLIGHT - 2 if k % FLIGHT == FLIGHT - 1 else -1
             tied = lax.optimization_barrier(tied)
             if k > FLIGHT:
                 chunks[steps[k - 1][0]] = tied["before"]
             chunks[j], got[last] = tied["chunk"], tied["got"]
             mate = tied.get("mate", mate)
-            if half in firsts:
-                halved[half] = tied["halved"]
-                halving(half)
-            if late in seconds:
-                seconds[late] = tied["second"]
         if step == 0:
             got[j, 0] = routed(chunks[j], (0, 1))
         elif step == 1:
@@ -249,25 +248,15 @@
         else:
             got[j, 2] = routed(got[j, 0], (1, 0))
         if ready >= 0:
-            product(ready)
+            product(ready, firsts.get(ready - 1, ()))
     for i in range(len(firsts), count):
-        tied = {"place": place}
-        if i - 2 not in halved:
-            tied["halved"] = halve(*firsts[i - 2])
-        if i - 3 in seconds:
-            tied["second"] = seconds[i - 3]
-        tied = lax.optimization_barrier(tied)
-        place = tied["place"]
-        if i - 2 not in halved:
-            halved[i - 2] = tied["halved"]
-            halving(i - 2)
-        if i - 3 in seconds:
-            seconds[i - 3] = tied["second"]
-        product(i)
+        if i == count - 1:
+            place, seconds = lax.optimization_barrier((place, seconds))
+        product(i, firsts[i - 1] if i == 2 else ())
     for i in range(count):
-        if i not in halved:
-            halved[i] = halve(*firsts[i])
-            halving(i)
+        if i not in seconds:
+            keep, send = halve(*firsts[i])
+            seconds[i] = keep, swapped(send, 2, "space")
     for i, (keep, came) in seconds.items():
         bit = 2
         while keep.shape[0] > 1:

time: 192 us -> 182 us (0.948)
  waiting for transfers between devices: 103 us -> 84.7 us
  starting transfers between devices: 38.5 us -> 47.1 us
    ppermute x12, waiting for transfers between devices: 42.5 us -> 29.8 us  [swapped(): return lax.ppermute(block, axis, [(i, i ^ bit) for i in range(size)])]
    ppermute x12, starting transfers between devices: 13.3 us -> 21.9 us  [swapped(): return lax.ppermute(block, axis, [(i, i ^ bit) for i in range(size)])]
    ppermute x15, waiting for transfers between devices: 54.4 us -> 48.7 us  [routed(): lax.ppermute(block, 'tm', [(i, i ^ 2 << ways[i % 2]) for i in range(size)])]
    pallas_call x5, Pallas kernels: 36.3 us -> 38.2 us  [multiply(): pl.pallas_call(functools.partial(multiply_kernel, steps, len(pieces)), gr...]
    unnamed x36 -> x40, local copies, waits for them, and re-layouts: 4.3 us -> 4.95 us
  transfers between devices with their start and end apart: 30 -> 30, of which waited for: 17 -> 16; matrix products, arithmetic and copies ran while one was open for 1% -> 1% of each run, Pallas kernels for 21% -> 22%
where the time goes in v4:
time: 182 us; the launch traced here: 181 us
  waiting for transfers between devices  84.7 us (47%)
  starting transfers between devices  47.1 us (26%)
  Pallas kernels  42.7 us (23%)
  local copies, waits for them, and re-layouts  5.88 us (3%)
    ppermute x15, waiting for transfers between devices, routed(): lax.ppermute(block, 'tm', [(i, i ^ 2 << ways[i % 2]) for i in range(size)])  48.7 us
    pallas_call x5, Pallas kernels, multiply(): pl.pallas_call(functools.partial(multiply_kernel, steps, len(pieces)), gr...  38.2 us
    ppermute x12, waiting for transfers between devices, swapped(): return lax.ppermute(block, axis, [(i, i ^ bit) for i in range(size)])  29.8 us
    ppermute x12, starting transfers between devices, swapped(): return lax.ppermute(block, axis, [(i, i ^ bit) for i in range(size)])  21.9 us
    ppermute x15, starting transfers between devices, routed(): lax.ppermute(block, 'tm', [(i, i ^ 2 << ways[i % 2]) for i in range(size)])  18.5 us
    ppermute x3, starting transfers between devices, shifted(): return lax.ppermute(block, axis, route)  6.68 us
    ppermute x3, waiting for transfers between devices, shifted(): return lax.ppermute(block, axis, route)  6.27 us
    unnamed x40, local copies, waits for them, and re-layouts  4.95 us
  transfers between devices with their start and end apart: 30, of which 16 were waited for; matrix products, arithmetic and copies ran while one was open for 1% of the time, Pallas kernels for 22%

profile of v4, /device:TPU:1, one launch (start us, length us, event | category | flops | bytes accessed | tf_op | source)
XLA Modules:
  0.0 181.4 jit_solution(10361568517793678188)
XLA Ops:
  3.3 2.8 %collective-permute-start = (f32[96,2048]{1,0:T(8,128)S(1)}, f32[96,2048]{1,0:T(8,128)}, u32[]{:S(2)}, u32[]{:S(2)}) collective-permute-start(f32[96,2048]{1,0:T(8,128)S(1)} %get-tuple-element.91.refs_0_), channel_id=1, source_target_pairs={{0,2},{1,5},{2,0},{3,7},{4,6},{5,1},{6,4},{7,3},{8,10},{9,13},{10,... | collective-permute-start | bytes 2359304 | tf_op jit(solution)/shard_map/ppermute | solution.py:194
  7.5 14.5 %collective-permute-done.refs_1_ = f32[96,2048]{1,0:T(8,128)} collective-permute-done((f32[96,2048]{1,0:T(8,128)S(1)}, f32[96,2048]{1,0:T(8,128)}, u32[]{:S(2)}, u32[]{:S(2)}) %collective-permute-start) | collective-permute-done | bytes 786464 | tf_op jit(solution)/shard_map/ppermute | solution.py:194
  22.0 3.2 %collective-permute-start.4 = (f32[96,2048]{1,0:T(8,128)}, f32[96,2048]{1,0:T(8,128)}, u32[]{:S(2)}, u32[]{:S(2)}) collective-permute-start(f32[96,2048]{1,0:T(8,128)} %collective-permute-done.refs_1_), channel_id=1, source_target_pairs={{0,4},{1,3},{2,6},{3,1},{4,0},{5,7},{6,2},{7,5},{8,12},{9,11},{10,... | collective-permute-start | bytes 2359304 | tf_op jit(solution)/shard_map/ppermute | solution.py:194
  26.9 10.5 %collective-permute-done.3.refs_1_ = f32[96,2048]{1,0:T(8,128)} collective-permute-done((f32[96,2048]{1,0:T(8,128)S(1)}, f32[96,2048]{1,0:T(8,128)}, u32[]{:S(2)}, u32[]{:S(2)}) %collective-permute-start.3) | collective-permute-done | bytes 786464 | tf_op jit(solution)/shard_map/ppermute | solution.py:194
  41.3 8.0 %shard_map.18 = (f32[2,96,768]{2,1,0:T(8,128)}, f32[2,96,768]{2,1,0:T(8,128)}) custom-call(s32[4]{0:T(128)} %add_xor_fusion.place, f32[2048,384]{1,0:T(8,128)} %own.9, f32[2048,384]{1,0:T(8,128)} %copy-done.11, f32[96,2048]{1,0:T(8,128)} %copy-done.1, f32[96,2048]{1,0:T(8,128)} %collective-permute-done.refs_1_, f32[96,2048]{1,0:T(8,128)} %copy-done.12, ...), custom_call_target="tpu_custom_call" | custom-call | flops 1 | bytes 1 | tf_op jit(solution)/shard_map/pallas_call | solution.py:116
  51.2 5.4 %collective-permute-done.5.refs_2_ = f32[96,2048]{1,0:T(8,128)} collective-permute-done((f32[96,2048]{1,0:T(8,128)S(1)}, f32[96,2048]{1,0:T(8,128)}, u32[]{:S(2)}, u32[]{:S(2)}) %collective-permute-start.5) | collective-permute-done | bytes 786464 | tf_op jit(solution)/shard_map/ppermute | solution.py:194
  59.3 8.3 %collective-permute-done.7.refs_3_ = f32[96,2048]{1,0:T(8,128)} collective-permute-done((f32[96,2048]{1,0:T(8,128)}, f32[96,2048]{1,0:T(8,128)}, u32[]{:S(2)}, u32[]{:S(2)}) %collective-permute-start.7) | collective-permute-done | bytes 786464 | tf_op jit(solution)/shard_map/ppermute | solution.py:194
  67.6 9.1 %shard_map.19 = (f32[1,96,768]{2,1,0:T(8,128)}, f32[1,96,768]{2,1,0:T(8,128)}, f32[2,96,768]{2,1,0:T(8,128)}, f32[2,96,768]{2,1,0:T(8,128)}) custom-call(s32[4]{0:T(128)} %add_xor_fusion.place, f32[2048,384]{1,0:T(8,128)} %own.9, f32[2048,384]{1,0:T(8,128)} %copy-done.11, f32[96,2048]{1,0:T(8,128)} %copy-done.3, f32[96,2048]{1,0:T(8,128)} %collective-permute-done.3.refs_1_, ...), custom_call_target="tpu_custom_call" | custom-call | flops 1 | bytes 1 | tf_op jit(solution)/shard_map/pallas_call | solution.py:116
  82.3 6.7 %collective-permute-done.12.refs_3_ = f32[96,2048]{1,0:T(8,128)S(1)} collective-permute-done((f32[96,2048]{1,0:T(8,128)}, f32[96,2048]{1,0:T(8,128)S(1)}, u32[]{:S(2)}, u32[]{:S(2)}) %collective-permute-start.12) | collective-permute-done | bytes 786464 | tf_op jit(solution)/shard_map/ppermute | solution.py:194
  89.9 9.0 %shard_map.20 = (f32[1,96,768]{2,1,0:T(8,128)}, f32[1,96,768]{2,1,0:T(8,128)}, f32[2,96,768]{2,1,0:T(8,128)}, f32[2,96,768]{2,1,0:T(8,128)}) custom-call(s32[4]{0:T(128)} %add_xor_fusion.place, f32[2048,384]{1,0:T(8,128)} %own.9, f32[2048,384]{1,0:T(8,128)} %copy-done.11, f32[96,2048]{1,0:T(8,128)} %copy-done.2, f32[96,2048]{1,0:T(8,128)} %collective-permute-done.6.refs_1_, ...), custom_call_target="tpu_custom_call" | custom-call | flops 1 | bytes 1 | tf_op jit(solution)/shard_map/pallas_call | solution.py:116
  100.8 2.3 %collective-permute-start.9 = (f32[1,96,768]{2,1,0:T(8,128)S(1)}, f32[1,96,768]{2,1,0:T(8,128)S(1)}, u32[]{:S(2)}, u32[]{:S(2)}) collective-permute-start(f32[1,96,768]{2,1,0:T(8,128)S(1)} %copy-done.19), channel_id=1, source_target_pairs={{0,16},{8,24},{16,0},{24,8},{1,17},{9,25},{17,1},{25,9},{2,18},{10... | collective-permute-start | bytes 884744 | tf_op jit(solution)/shard_map/ppermute | solution.py:23
  104.9 6.8 %shard_map.22 = (f32[2,64,768]{2,1,0:T(8,128)}, f32[2,64,768]{2,1,0:T(8,128)}) custom-call(s32[4]{0:T(128)} %add_xor_fusion.place, f32[2048,384]{1,0:T(8,128)} %own.9, f32[2048,384]{1,0:T(8,128)} %copy-done.11, f32[64,2048]{1,0:T(8,128)} %copy-done.5, f32[64,2048]{1,0:T(8,128)} %collective-permute-done.11.refs_1_, f32[64,2048]{1,0:T(8,128)} %copy-done.15, ...), custom_call_target="tpu_custom_call" | custom-call | flops 1 | bytes 1 | tf_op jit(solution)/shard_map/pallas_call | solution.py:116
  113.0 3.8 %collective-permute-done.9.refs_5_ = f32[1,96,768]{2,1,0:T(8,128)S(1)} collective-permute-done((f32[1,96,768]{2,1,0:T(8,128)S(1)}, f32[1,96,768]{2,1,0:T(8,128)S(1)}, u32[]{:S(2)}, u32[]{:S(2)}) %collective-permute-start.9) | collective-permute-done | bytes 294944 | tf_op jit(solution)/shard_map/ppermute | solution.py:23
  117.8 5.5 %collective-permute-done.14.refs_6_ = f32[1,96,768]{2,1,0:T(8,128)S(1)} collective-permute-done((f32[1,96,768]{2,1,0:T(8,128)}, f32[1,96,768]{2,1,0:T(8,128)S(1)}, u32[]{:S(2)}, u32[]{:S(2)}) %collective-permute-start.14) | collective-permute-done | bytes 294944 | tf_op jit(solution)/shard_map/ppermute | solution.py:23
  124.7 5.4 %shard_map.24 = (f32[2,32,768]{2,1,0:T(8,128)}, f32[2,32,768]{2,1,0:T(8,128)}) custom-call(s32[4]{0:T(128)} %add_xor_fusion.place, f32[2048,384]{1,0:T(8,128)} %own.9, f32[2048,384]{1,0:T(8,128)} %copy-done.11, f32[32,2048]{1,0:T(8,128)} %copy-done.9, f32[32,2048]{1,0:T(8,128)} %copy-done.16, f32[32,2048]{1,0:T(8,128)} %copy-done.18, f32[32,2048]{1,0:T(8,128)} %copy-done.17), custom_call_target="tpu_custom_call" | custom-call | flops 1 | bytes 1 | tf_op jit(solution)/shard_map/pallas_call | solution.py:116
  130.1 3.2 %collective-permute-start.22 = (f32[2,32,768]{2,1,0:T(8,128)}, f32[2,32,768]{2,1,0:T(8,128)S(1)}, u32[]{:S(2)}, u32[]{:S(2)}) collective-permute-start(f32[2,32,768]{2,1,0:T(8,128)} %get-tuple-element.130), channel_id=1, source_target_pairs={{0,8},{8,0},{16,24},{24,16},{1,9},{9,1},{17,25},{25,17},{2,10},{10... | collective-permute-start | bytes 589832 | tf_op jit(solution)/shard_map/ppermute | solution.py:23
  133.7 3.0 %collective-permute-start.24 = (f32[1,64,768]{2,1,0:T(8,128)S(1)}, f32[1,64,768]{2,1,0:T(8,128)S(1)}, u32[]{:S(2)}, u32[]{:S(2)}) collective-permute-start(f32[1,64,768]{2,1,0:T(8,128)S(1)} %get-tuple-element.135), channel_id=1, source_target_pairs={{0,16},{8,24},{16,0},{24,8},{1,17},{9,25},{17,1},{25,9},{2,18},{10... | collective-permute-start | bytes 589832 | tf_op jit(solution)/shard_map/ppermute | solution.py:23
  136.6 4.3 %collective-permute-done.22.came = f32[2,32,768]{2,1,0:T(8,128)S(1)} collective-permute-done((f32[2,32,768]{2,1,0:T(8,128)}, f32[2,32,768]{2,1,0:T(8,128)S(1)}, u32[]{:S(2)}, u32[]{:S(2)}) %collective-permute-start.22) | collective-permute-done | bytes 196640 | tf_op jit(solution)/shard_map/ppermute | solution.py:23
  141.0 2.8 %collective-permute-start.25 = (f32[1,32,768]{2,1,0:T(8,128)S(1)}, f32[1,32,768]{2,1,0:T(8,128)S(1)}, u32[]{:S(2)}, u32[]{:S(2)}) collective-permute-start(f32[1,32,768]{2,1,0:T(8,128)S(1)} %get-tuple-element.136), channel_id=1, source_target_pairs={{0,16},{8,24},{16,0},{24,8},{1,17},{9,25},{17,1},{25,9},{2,18},{10... | collective-permute-start | bytes 294920 | tf_op jit(solution)/shard_map/ppermute | solution.py:23
  143.8 14.6 %collective-permute-done.25.refs_9_ = f32[1,32,768]{2,1,0:T(8,128)S(1)} collective-permute-done((f32[1,32,768]{2,1,0:T(8,128)S(1)}, f32[1,32,768]{2,1,0:T(8,128)S(1)}, u32[]{:S(2)}, u32[]{:S(2)}) %collective-permute-start.25) | collective-permute-done | bytes 98336 | tf_op jit(solution)/shard_map/ppermute | solution.py:23
  158.8 4.4 %collective-permute-start.26 = (f32[384,384]{0,1:T(8,128)S(1)}, f32[384,384]{0,1:T(8,128)S(1)}, u32[]{:S(2)}, u32[]{:S(2)}) collective-permute-start(f32[384,384]{0,1:T(8,128)S(1)} %copy.2), channel_id=1, source_target_pairs={{0,1},{1,0},{2,3},{3,2},{4,5},{5,4},{6,7},{7,6},{8,9},{9,8},{10,11... | collective-permute-start | bytes 1769480 | tf_op jit(solution)/shard_map/ppermute | solution.py:23
  168.6 4.4 %collective-permute-done.28 = f32[16,384]{0,1:T(8,128)S(1)} collective-permute-done((f32[16,384]{0,1:T(8,128)S(1)}, f32[16,384]{0,1:T(8,128)S(1)}, u32[]{:S(2)}, u32[]{:S(2)}) %collective-permute-start.28) | collective-permute-done | bytes 24608 | tf_op jit(solution)/shard_map/ppermute | solution.py:29
  173.0 3.1 %collective-permute-start.29 = (f32[16,16]{1,0:T(8,128)S(1)}, f32[16,16]{1,0:T(8,128)S(1)}, u32[]{:S(2)}, u32[]{:S(2)}) collective-permute-start(f32[16,16]{1,0:T(8,128)S(1)} %slice.20), channel_id=1, source_target_pairs={{1,0},{2,1},{3,2},{4,3},{5,4},{6,5},{7,6},{9,8},{10,9},{11,10},{12... | collective-permute-start | bytes 3080 | tf_op jit(solution)/shard_map/ppermute | solution.py:29
  178.5 2.9 %shard_map.27 = f32[384,768]{1,0:T(8,128)} custom-call(f32[768,384]{1,0:T(8,128)S(1)} %copy.5.turned, f32[16,768]{1,0:T(8,128)S(1)} %collective-permute-done.27.below, f32[16,384]{1,0:T(8,128)S(1)} %copy.6.beside, f32[16,16]{1,0:T(8,128)S(1)} %collective-permute-done.29.corner), custom_call_target="tpu_custom_call" | custom-call | tf_op jit(solution)/shard_map/pallas_call | solution.py:149
  (98 shorter events, 37.2 us)
Async XLA Ops:
  0.0 22.0 %collective-permute-start.1 = (f32[2048,384]{1,0:T(8,128)}, f32[2048,384]{1,0:T(8,128)S(1)}, u32[]{:S(2)}, u32[]{:S(2)}) collective-permute-start(f32[2048,384]{1,0:T(8,128)} %own.9), channel_id=1, source_target_pairs={{0,1},{1,0},{2,3},{3,2},{4,5},{5,4},{6,7},{7,6},{8,9},{9,8},{10,11... | collective-permute-start | bytes 9437192 | tf_op jit(solution)/shard_map/ppermute | solution.py:23
  3.3 18.7 %collective-permute-start = (f32[96,2048]{1,0:T(8,128)S(1)}, f32[96,2048]{1,0:T(8,128)}, u32[]{:S(2)}, u32[]{:S(2)}) collective-permute-start(f32[96,2048]{1,0:T(8,128)S(1)} %get-tuple-element.91.refs_0_), channel_id=1, source_target_pairs={{0,2},{1,5},{2,0},{3,7},{4,6},{5,1},{6,4},{7,3},{8,10},{9,13},{10,... | collective-permute-start | bytes 2359304 | tf_op jit(solution)/shard_map/ppermute | solution.py:194
  6.1 19.7 %collective-permute-start.2 = (f32[96,2048]{1,0:T(8,128)S(1)}, f32[96,2048]{1,0:T(8,128)S(1)}, u32[]{:S(2)}, u32[]{:S(2)}) collective-permute-start(f32[96,2048]{1,0:T(8,128)S(1)} %get-tuple-element.91.refs_0_), channel_id=1, source_target_pairs={{0,4},{1,3},{2,6},{3,1},{4,0},{5,7},{6,2},{7,5},{8,12},{9,11},{10,... | collective-permute-start | bytes 2359304 | tf_op jit(solution)/shard_map/ppermute | solution.py:194
  7.3 30.1 %collective-permute-start.3 = (f32[96,2048]{1,0:T(8,128)S(1)}, f32[96,2048]{1,0:T(8,128)}, u32[]{:S(2)}, u32[]{:S(2)}) collective-permute-start(f32[96,2048]{1,0:T(8,128)S(1)} %get-tuple-element.83.refs_0_), channel_id=1, source_target_pairs={{0,2},{1,5},{2,0},{3,7},{4,6},{5,1},{6,4},{7,3},{8,10},{9,13},{10,... | collective-permute-start | bytes 2359304 | tf_op jit(solution)/shard_map/ppermute | solution.py:194
  22.0 19.2 %collective-permute-start.4 = (f32[96,2048]{1,0:T(8,128)}, f32[96,2048]{1,0:T(8,128)}, u32[]{:S(2)}, u32[]{:S(2)}) collective-permute-start(f32[96,2048]{1,0:T(8,128)} %collective-permute-done.refs_1_), channel_id=1, source_target_pairs={{0,4},{1,3},{2,6},{3,1},{4,0},{5,7},{6,2},{7,5},{8,12},{9,11},{10,... | collective-permute-start | bytes 2359304 | tf_op jit(solution)/shard_map/ppermute | solution.py:194
  25.8 30.8 %collective-permute-start.5 = (f32[96,2048]{1,0:T(8,128)S(1)}, f32[96,2048]{1,0:T(8,128)}, u32[]{:S(2)}, u32[]{:S(2)}) collective-permute-start(f32[96,2048]{1,0:T(8,128)S(1)} %get-tuple-element.83.refs_0_), channel_id=1, source_target_pairs={{0,4},{1,3},{2,6},{3,1},{4,0},{5,7},{6,2},{7,5},{8,12},{9,11},{10,... | collective-permute-start | bytes 2359304 | tf_op jit(solution)/shard_map/ppermute | solution.py:194
  37.4 20.9 %collective-permute-start.6 = (f32[96,2048]{1,0:T(8,128)S(1)}, f32[96,2048]{1,0:T(8,128)}, u32[]{:S(2)}, u32[]{:S(2)}) collective-permute-start(f32[96,2048]{1,0:T(8,128)S(1)} %get-tuple-element.100.refs_0_), channel_id=1, source_target_pairs={{0,2},{1,5},{2,0},{3,7},{4,6},{5,1},{6,4},{7,3},{8,10},{9,13},{10,... | collective-permute-start | bytes 2359304 | tf_op jit(solution)/shard_map/ppermute | solution.py:194
  38.6 29.1 %collective-permute-start.7 = (f32[96,2048]{1,0:T(8,128)}, f32[96,2048]{1,0:T(8,128)}, u32[]{:S(2)}, u32[]{:S(2)}) collective-permute-start(f32[96,2048]{1,0:T(8,128)} %collective-permute-done.3.refs_1_), channel_id=1, source_target_pairs={{0,4},{1,3},{2,6},{3,1},{4,0},{5,7},{6,2},{7,5},{8,12},{9,11},{10,... | collective-permute-start | bytes 2359304 | tf_op jit(solution)/shard_map/ppermute | solution.py:194
  49.3 18.3 %collective-permute-start.8 = (f32[2,96,768]{2,1,0:T(8,128)}, f32[2,96,768]{2,1,0:T(8,128)}, u32[]{:S(2)}, u32[]{:S(2)}) collective-permute-start(f32[2,96,768]{2,1,0:T(8,128)} %get-tuple-element.95), channel_id=1, source_target_pairs={{0,8},{8,0},{16,24},{24,16},{1,9},{9,1},{17,25},{25,17},{2,10},{10... | collective-permute-start | bytes 1769480 | tf_op jit(solution)/shard_map/ppermute | solution.py:23
  56.6 23.9 %collective-permute-start.10 = (f32[96,2048]{1,0:T(8,128)S(1)}, f32[96,2048]{1,0:T(8,128)S(1)}, u32[]{:S(2)}, u32[]{:S(2)}) collective-permute-start(f32[96,2048]{1,0:T(8,128)S(1)} %get-tuple-element.100.refs_0_), channel_id=1, source_target_pairs={{0,4},{1,3},{2,6},{3,1},{4,0},{5,7},{6,2},{7,5},{8,12},{9,11},{10,... | collective-permute-start | bytes 2359304 | tf_op jit(solution)/shard_map/ppermute | solution.py:194
  58.3 30.7 %collective-permute-start.12 = (f32[96,2048]{1,0:T(8,128)}, f32[96,2048]{1,0:T(8,128)S(1)}, u32[]{:S(2)}, u32[]{:S(2)}) collective-permute-start(f32[96,2048]{1,0:T(8,128)} %collective-permute-done.6.refs_1_), channel_id=1, source_target_pairs={{0,4},{1,3},{2,6},{3,1},{4,0},{5,7},{6,2},{7,5},{8,12},{9,11},{10,... | collective-permute-start | bytes 2359304 | tf_op jit(solution)/shard_map/ppermute | solution.py:194
  58.6 23.6 %collective-permute-start.11 = (f32[64,2048]{1,0:T(8,128)S(1)}, f32[64,2048]{1,0:T(8,128)}, u32[]{:S(2)}, u32[]{:S(2)}) collective-permute-start(f32[64,2048]{1,0:T(8,128)S(1)} %get-tuple-element.119.refs_0_), channel_id=1, source_target_pairs={{0,2},{1,5},{2,0},{3,7},{4,6},{5,1},{6,4},{7,3},{8,10},{9,13},{10,... | collective-permute-start | bytes 1572872 | tf_op jit(solution)/shard_map/ppermute | solution.py:194
  76.7 12.4 %collective-permute-start.13 = (f32[2,96,768]{2,1,0:T(8,128)}, f32[2,96,768]{2,1,0:T(8,128)}, u32[]{:S(2)}, u32[]{:S(2)}) collective-permute-start(f32[2,96,768]{2,1,0:T(8,128)} %get-tuple-element.109), channel_id=1, source_target_pairs={{0,8},{8,0},{16,24},{24,16},{1,9},{9,1},{17,25},{25,17},{2,10},{10... | collective-permute-start | bytes 1769480 | tf_op jit(solution)/shard_map/ppermute | solution.py:23
  80.5 23.6 %collective-permute-start.16 = (f32[64,2048]{1,0:T(8,128)S(1)}, f32[64,2048]{1,0:T(8,128)S(1)}, u32[]{:S(2)}, u32[]{:S(2)}) collective-permute-start(f32[64,2048]{1,0:T(8,128)S(1)} %get-tuple-element.119.refs_0_), channel_id=1, source_target_pairs={{0,4},{1,3},{2,6},{3,1},{4,0},{5,7},{6,2},{7,5},{8,12},{9,11},{10,... | collective-permute-start | bytes 1572872 | tf_op jit(solution)/shard_map/ppermute | solution.py:194
  82.2 21.9 %collective-permute-start.17 = (f32[64,2048]{1,0:T(8,128)}, f32[64,2048]{1,0:T(8,128)}, u32[]{:S(2)}, u32[]{:S(2)}) collective-permute-start(f32[64,2048]{1,0:T(8,128)} %collective-permute-done.11.refs_1_), channel_id=1, source_target_pairs={{0,4},{1,3},{2,6},{3,1},{4,0},{5,7},{6,2},{7,5},{8,12},{9,11},{10,... | collective-permute-start | bytes 1572872 | tf_op jit(solution)/shard_map/ppermute | solution.py:194
  98.9 34.4 %collective-permute-start.15 = (f32[2,96,768]{2,1,0:T(8,128)}, f32[2,96,768]{2,1,0:T(8,128)S(1)}, u32[]{:S(2)}, u32[]{:S(2)}) collective-permute-start(f32[2,96,768]{2,1,0:T(8,128)} %get-tuple-element.115), channel_id=1, source_target_pairs={{0,8},{8,0},{16,24},{24,16},{1,9},{9,1},{17,25},{25,17},{2,10},{10... | collective-permute-start | bytes 1769480 | tf_op jit(solution)/shard_map/ppermute | solution.py:23
  100.8 16.1 %collective-permute-start.9 = (f32[1,96,768]{2,1,0:T(8,128)S(1)}, f32[1,96,768]{2,1,0:T(8,128)S(1)}, u32[]{:S(2)}, u32[]{:S(2)}) collective-permute-start(f32[1,96,768]{2,1,0:T(8,128)S(1)} %copy-done.19), channel_id=1, source_target_pairs={{0,16},{8,24},{16,0},{24,8},{1,17},{9,25},{17,1},{25,9},{2,18},{10... | collective-permute-start | bytes 884744 | tf_op jit(solution)/shard_map/ppermute | solution.py:23
  104.1 19.2 %collective-permute-start.14 = (f32[1,96,768]{2,1,0:T(8,128)}, f32[1,96,768]{2,1,0:T(8,128)S(1)}, u32[]{:S(2)}, u32[]{:S(2)}) collective-permute-start(f32[1,96,768]{2,1,0:T(8,128)} %get-tuple-element.111), channel_id=1, source_target_pairs={{0,16},{8,24},{16,0},{24,8},{1,17},{9,25},{17,1},{25,9},{2,18},{10... | collective-permute-start | bytes 884744 | tf_op jit(solution)/shard_map/ppermute | solution.py:23
  111.6 22.0 %collective-permute-start.18 = (f32[2,64,768]{2,1,0:T(8,128)}, f32[2,64,768]{2,1,0:T(8,128)S(1)}, u32[]{:S(2)}, u32[]{:S(2)}) collective-permute-start(f32[2,64,768]{2,1,0:T(8,128)} %get-tuple-element.123), channel_id=1, source_target_pairs={{0,8},{8,0},{16,24},{24,16},{1,9},{9,1},{17,25},{25,17},{2,10},{10... | collective-permute-start | bytes 1179656 | tf_op jit(solution)/shard_map/ppermute | solution.py:23
  111.8 11.5 %collective-permute-start.21 = (f32[32,2048]{1,0:T(8,128)S(1)}, f32[32,2048]{1,0:T(8,128)S(1)}, u32[]{:S(2)}, u32[]{:S(2)}) collective-permute-start(f32[32,2048]{1,0:T(8,128)S(1)} %collective-permute-done.19.refs_1_), channel_id=1, source_target_pairs={{0,4},{1,3},{2,6},{3,1},{4,0},{5,7},{6,2},{7,5},{8,12},{9,11},{10,... | collective-permute-start | bytes 786440 | tf_op jit(solution)/shard_map/ppermute | solution.py:194
  133.4 25.0 %collective-permute-start.23 = (f32[1,96,768]{2,1,0:T(8,128)S(1)}, f32[1,96,768]{2,1,0:T(8,128)S(1)}, u32[]{:S(2)}, u32[]{:S(2)}) collective-permute-start(f32[1,96,768]{2,1,0:T(8,128)S(1)} %get-tuple-element.134), channel_id=1, source_target_pairs={{0,16},{8,24},{16,0},{24,8},{1,17},{9,25},{17,1},{25,9},{2,18},{10... | collective-permute-start | bytes 884744 | tf_op jit(solution)/shard_map/ppermute | solution.py:23
  133.7 24.8 %collective-permute-start.24 = (f32[1,64,768]{2,1,0:T(8,128)S(1)}, f32[1,64,768]{2,1,0:T(8,128)S(1)}, u32[]{:S(2)}, u32[]{:S(2)}) collective-permute-start(f32[1,64,768]{2,1,0:T(8,128)S(1)} %get-tuple-element.135), channel_id=1, source_target_pairs={{0,16},{8,24},{16,0},{24,8},{1,17},{9,25},{17,1},{25,9},{2,18},{10... | collective-permute-start | bytes 589832 | tf_op jit(solution)/shard_map/ppermute | solution.py:23
  141.0 17.4 %collective-permute-start.25 = (f32[1,32,768]{2,1,0:T(8,128)S(1)}, f32[1,32,768]{2,1,0:T(8,128)S(1)}, u32[]{:S(2)}, u32[]{:S(2)}) collective-permute-start(f32[1,32,768]{2,1,0:T(8,128)S(1)} %get-tuple-element.136), channel_id=1, source_target_pairs={{0,16},{8,24},{16,0},{24,8},{1,17},{9,25},{17,1},{25,9},{2,18},{10... | collective-permute-start | bytes 294920 | tf_op jit(solution)/shard_map/ppermute | solution.py:23
  166.3 12.2 %collective-permute-start.27 = (f32[16,768]{1,0:T(8,128)S(1)}, f32[16,768]{1,0:T(8,128)S(1)}, u32[]{:S(2)}, u32[]{:S(2)}) collective-permute-start(f32[16,768]{1,0:T(8,128)S(1)} %fusion.1), channel_id=1, source_target_pairs={{1,0},{2,1},{3,2},{4,3},{5,4},{6,5},{7,6},{9,8},{10,9},{11,10},{12... | collective-permute-start | bytes 147464 | tf_op jit(solution)/shard_map/ppermute | solution.py:29
  (26 other events, 511.2 us)

commit v5 on v4

--- a/solution.py
+++ b/solution.py
@@ -127,13 +127,30 @@
     )(place, own, mate, *pieces, *earlier)
 
 
-def window_kernel(scale, turned, below, beside, corner, out, wide):
+def window_kernel(scale, core, own, swap, near, first, second, rim, out, wide):
     rows, columns = out.shape
-    wide[:rows, :columns] = turned[...].T
-    wide[rows:, :columns] = below[...]
-    edge = jnp.concatenate([beside[...].T, corner[:, :WINDOW]], 0)
+    block = columns // 2
+
+    @pl.when(core[0] == 0)
+    def _():
+        wide[:rows, :block] = own[...].T
+        wide[:rows, block:columns] = swap[:, :block].T
+        wide[rows:, :block] = near[...]
+        wide[rows:, block:columns] = swap[:, block:].T[:WINDOW]
+
+    @pl.when(core[0] == 1)
+    def _():
+        wide[:rows, :block] = swap[:, :block].T
+        wide[:rows, block:columns] = own[...].T
+        wide[rows:, :block] = first[...]
+        wide[rows:, block:columns] = second[...]
+
     wide[:, columns:] = jnp.concatenate(
-        [edge, jnp.zeros((rows + WINDOW, 128 - WINDOW), jnp.float32)], 1
+        [
+            rim[...].T[: rows + WINDOW],
+            jnp.zeros((rows + WINDOW, 128 - WINDOW), jnp.float32),
+        ],
+        1,
     )
     total = wide[...] * scale
     distance = 1
@@ -144,14 +161,16 @@
     out[...] = total[:rows, :columns]
 
 
-def window(scale, turned, below, beside, corner):
-    columns, rows = turned.shape
+def window(scale, core, own, *parts):
+    columns, rows = own.shape
     return pl.pallas_call(
         functools.partial(window_kernel, scale),
-        out_shape=jax.ShapeDtypeStruct((rows, columns), jnp.float32),
-        scratch_shapes=[pltpu.VMEM((rows + WINDOW, columns + 128), jnp.float32)],
+        in_specs=[pl.BlockSpec(memory_space=pltpu.SMEM)]
+        + [pl.BlockSpec(memory_space=pltpu.VMEM)] * (1 + len(parts)),
+        out_shape=jax.ShapeDtypeStruct((rows, 2 * columns), jnp.float32),
+        scratch_shapes=[pltpu.VMEM((rows + WINDOW, 2 * columns + 128), jnp.float32)],
         compiler_params=params(),
-    )(turned, below, beside, corner)
+    )(core, own, *parts)
 
 
 def halve_kernel(keep, came, first, second):
@@ -170,23 +189,59 @@
 
 
 def collect_kernel(count, *refs):
-    own, other = refs[2 * count :]
+    own, swap, near, far = refs[2 * count :]
+    block = own.shape[1]
     start = 0
     for keep, came in zip(refs[:count], refs[count : 2 * count]):
         total = keep[0] + came[0]
         rows = pl.ds(start, total.shape[0])
-        own[rows, :], other[rows, :] = total[:, : own.shape[1]], total[:, own.shape[1] :]
+        own[rows, :] = total[:, :block]
+        swap[rows, :block] = total[:, block:]
         start += total.shape[0]
+    swap[:, block:] = own[:, :128]
+    near[...] = swap[:, :128].T[:WINDOW]
+    far[...] = own[:, :128].T[:WINDOW]
 
 
 def collect(keeps, cames):
     columns = sum(keep.shape[1] for keep in keeps)
-    shape = jax.ShapeDtypeStruct((columns, keeps[0].shape[2] // 2), jnp.float32)
+    block = keeps[0].shape[2] // 2
+    shapes = [(columns, block), (columns, block + 128)] + [(WINDOW, columns)] * 2
     return pl.pallas_call(
         functools.partial(collect_kernel, len(keeps)),
-        out_shape=[shape] * 2,
+        out_shape=[jax.ShapeDtypeStruct(shape, jnp.float32) for shape in shapes],
         compiler_params=params(),
     )(*keeps, *cames)
+
+
+def moved(value, planes, size, source, target):
+    pairs = []
+    for chip in range(size // 2):
+        start, end = source(chip), target(chip)
+        if start < size:
+            pairs += [((z + 1) * size + start, z * size + end) for z in range(planes - 1)]
+    return lax.ppermute(value, ("space", "tm"), pairs)
+
+
+def rimmed(edge, core, planes, size):
+    block = edge.shape[1] // 2
+    zero = moved(edge, planes, size, lambda chip: 2 * chip, lambda chip: 2 * chip)
+    one = moved(edge, planes, size, lambda chip: 2 * chip, lambda chip: 2 * chip + 1)
+    next_ = moved(
+        edge[:, :128], planes, size, lambda chip: 2 * chip + 2, lambda chip: 2 * chip + 1
+    )
+    return jnp.where(
+        core == 0, zero[:, : block + 128], jnp.concatenate([one[:, block:], next_], 1)
+    )
+
+
+def finished(keep, came):
+    bit = 2
+    while keep.shape[0] > 1:
+        bit *= 2
+        keep, send = halve(keep, came)
+        came = swapped(send, bit, "space")
+    return keep, came
 
 
 def routed(block, ways):
@@ -257,24 +312,21 @@
         if i not in seconds:
             keep, send = halve(*firsts[i])
             seconds[i] = keep, swapped(send, 2, "space")
-    for i, (keep, came) in seconds.items():
-        bit = 2
-        while keep.shape[0] > 1:
-            bit *= 2
-            keep, send = halve(keep, came)
-            came = swapped(send, bit, "space")
-        seconds[i] = keep, came
-    own, other = collect(
+    seconds = {i: finished(*seconds[i]) for i in seconds}
+    edge = (seconds[0][0] + seconds[0][1])[0, :WINDOW]
+    last, came = seconds[count - 1]
+    edge, last = lax.optimization_barrier((edge, last))
+    rim = rimmed(edge, core, planes, 2 * chips)
+    rim, came = lax.optimization_barrier((rim, came))
+    seconds[count - 1] = last, came
+    own, swap, near, far = collect(
         [seconds[j][0] for j in range(count)], [seconds[j][1] for j in range(count)]
     )
-    other = swapped(other, 1)
-    turned = jnp.concatenate(
-        [jnp.where(core == 0, own, other), jnp.where(core == 0, other, own)], 0
-    )
-    below = shifted(turned[:, :WINDOW].T, "tm", -1)
-    beside = shifted(turned[:WINDOW], "space", -1)
-    corner = shifted(beside[:, :128].T[:WINDOW], "tm", -1)
-    return window(scale, turned, below, beside, corner)
+    size = 2 * chips
+    swap = swapped(swap, 1)
+    first = lax.ppermute(far, "tm", [(i + 1, i) for i in range(1, size - 1, 2)])
+    second = lax.ppermute(near, "tm", [(i + 2, i) for i in range(1, size - 2, 2)])
+    return window(scale, core.reshape(1), own, swap, near, first, second, rim)
 
 
 def solution(mesh):

time: 182 us -> 175 us (0.962)
  waiting for transfers between devices: 84.7 us -> 78.7 us
    ppermute x12, waiting for transfers between devices: 29.8 us -> 18.3 us  [swapped(): return lax.ppermute(block, axis, [(i, i ^ bit) for i in range(size)])]
    ppermute x3 -> x5, waiting for transfers between devices: 6.27 us -> 9.85 us  [the longest x3 6.48 us: moved(): return lax.ppermute(value, ('space', 'tm'), pairs)]
    ppermute x12, starting transfers between devices: 21.9 us -> 23.8 us  [swapped(): return lax.ppermute(block, axis, [(i, i ^ bit) for i in range(size)])]
    ppermute x15, waiting for transfers between devices: 48.7 us -> 50.5 us  [routed(): lax.ppermute(block, 'tm', [(i, i ^ 2 << ways[i % 2]) for i in range(size)])]
    ppermute x3 -> x5, starting transfers between devices: 6.68 us -> 5.82 us  [the longest x3 3.25 us: moved(): return lax.ppermute(value, ('space', 'tm'), pairs)]
    unnamed x40 -> x36, local copies, waits for them, and re-layouts: 4.95 us -> 4.43 us
  transfers between devices with their start and end apart: 30 -> 32, of which waited for: 16 -> 17; matrix products, arithmetic and copies ran while one was open for 1% -> 0% of each run, Pallas kernels for 22% -> 23%
where the time goes in v5:
time: 175 us; the launch traced here: 174 us
  waiting for transfers between devices  78.7 us (45%)
  starting transfers between devices  47.5 us (27%)
  Pallas kernels  42.8 us (24%)
  local copies, waits for them, and re-layouts  4.44 us (3%)
    ppermute x15, waiting for transfers between devices, routed(): lax.ppermute(block, 'tm', [(i, i ^ 2 << ways[i % 2]) for i in range(size)])  50.5 us
    pallas_call x5, Pallas kernels, multiply(): pl.pallas_call(functools.partial(multiply_kernel, steps, len(pieces)), gr...  38.2 us
    ppermute x12, starting transfers between devices, swapped(): return lax.ppermute(block, axis, [(i, i ^ bit) for i in range(size)])  23.8 us
    ppermute x12, waiting for transfers between devices, swapped(): return lax.ppermute(block, axis, [(i, i ^ bit) for i in range(size)])  18.3 us
    ppermute x15, starting transfers between devices, routed(): lax.ppermute(block, 'tm', [(i, i ^ 2 << ways[i % 2]) for i in range(size)])  17.8 us
    ppermute x3, waiting for transfers between devices, moved(): return lax.ppermute(value, ('space', 'tm'), pairs)  6.48 us
    unnamed x36, local copies, waits for them, and re-layouts  4.43 us
  transfers between devices with their start and end apart: 32, of which 17 were waited for; matrix products, arithmetic and copies ran while one was open for 0% of the time, Pallas kernels for 23%

profile of v5, /device:TPU:1, one launch (start us, length us, event | category | flops | bytes accessed | tf_op | source)
XLA Modules:
  0.0 174.2 jit_solution(3563509101967415887)
XLA Ops:
  3.3 2.8 %collective-permute-start = (f32[96,2048]{1,0:T(8,128)S(1)}, f32[96,2048]{1,0:T(8,128)}, u32[]{:S(2)}, u32[]{:S(2)}) collective-permute-start(f32[96,2048]{1,0:T(8,128)S(1)} %get-tuple-element.97.refs_0_), channel_id=1, source_target_pairs={{0,2},{1,5},{2,0},{3,7},{4,6},{5,1},{6,4},{7,3},{8,10},{9,13},{10,... | collective-permute-start | bytes 2359304 | tf_op jit(solution)/shard_map/ppermute | solution.py:249
  7.5 14.5 %collective-permute-done.refs_1_ = f32[96,2048]{1,0:T(8,128)} collective-permute-done((f32[96,2048]{1,0:T(8,128)S(1)}, f32[96,2048]{1,0:T(8,128)}, u32[]{:S(2)}, u32[]{:S(2)}) %collective-permute-start) | collective-permute-done | bytes 786464 | tf_op jit(solution)/shard_map/ppermute | solution.py:249
  22.0 3.2 %collective-permute-start.4 = (f32[96,2048]{1,0:T(8,128)}, f32[96,2048]{1,0:T(8,128)}, u32[]{:S(2)}, u32[]{:S(2)}) collective-permute-start(f32[96,2048]{1,0:T(8,128)} %collective-permute-done.refs_1_), channel_id=1, source_target_pairs={{0,4},{1,3},{2,6},{3,1},{4,0},{5,7},{6,2},{7,5},{8,12},{9,11},{10,... | collective-permute-start | bytes 2359304 | tf_op jit(solution)/shard_map/ppermute | solution.py:249
  26.9 10.5 %collective-permute-done.3.refs_1_ = f32[96,2048]{1,0:T(8,128)} collective-permute-done((f32[96,2048]{1,0:T(8,128)S(1)}, f32[96,2048]{1,0:T(8,128)}, u32[]{:S(2)}, u32[]{:S(2)}) %collective-permute-start.3) | collective-permute-done | bytes 786464 | tf_op jit(solution)/shard_map/ppermute | solution.py:249
  41.3 8.0 %shard_map.18 = (f32[2,96,768]{2,1,0:T(8,128)}, f32[2,96,768]{2,1,0:T(8,128)}) custom-call(s32[4]{0:T(128)} %add_xor_fusion.place, f32[2048,384]{1,0:T(8,128)} %own.9, f32[2048,384]{1,0:T(8,128)} %copy-done.11, f32[96,2048]{1,0:T(8,128)} %copy-done.1, f32[96,2048]{1,0:T(8,128)} %collective-permute-done.refs_1_, f32[96,2048]{1,0:T(8,128)} %copy-done.12, ...), custom_call_target="tpu_custom_call" | custom-call | flops 1 | bytes 1 | tf_op jit(solution)/shard_map/pallas_call | solution.py:116
  51.2 5.4 %collective-permute-done.5.refs_2_ = f32[96,2048]{1,0:T(8,128)} collective-permute-done((f32[96,2048]{1,0:T(8,128)S(1)}, f32[96,2048]{1,0:T(8,128)}, u32[]{:S(2)}, u32[]{:S(2)}) %collective-permute-start.5) | collective-permute-done | bytes 786464 | tf_op jit(solution)/shard_map/ppermute | solution.py:249
  59.3 8.3 %collective-permute-done.7.refs_3_ = f32[96,2048]{1,0:T(8,128)} collective-permute-done((f32[96,2048]{1,0:T(8,128)}, f32[96,2048]{1,0:T(8,128)}, u32[]{:S(2)}, u32[]{:S(2)}) %collective-permute-start.7) | collective-permute-done | bytes 786464 | tf_op jit(solution)/shard_map/ppermute | solution.py:249
  67.6 9.0 %shard_map.19 = (f32[1,96,768]{2,1,0:T(8,128)}, f32[1,96,768]{2,1,0:T(8,128)}, f32[2,96,768]{2,1,0:T(8,128)}, f32[2,96,768]{2,1,0:T(8,128)}) custom-call(s32[4]{0:T(128)} %add_xor_fusion.place, f32[2048,384]{1,0:T(8,128)} %own.9, f32[2048,384]{1,0:T(8,128)} %copy-done.11, f32[96,2048]{1,0:T(8,128)} %copy-done.3, f32[96,2048]{1,0:T(8,128)} %collective-permute-done.3.refs_1_, ...), custom_call_target="tpu_custom_call" | custom-call | flops 1 | bytes 1 | tf_op jit(solution)/shard_map/pallas_call | solution.py:116
  82.3 6.7 %collective-permute-done.12.refs_3_ = f32[96,2048]{1,0:T(8,128)S(1)} collective-permute-done((f32[96,2048]{1,0:T(8,128)}, f32[96,2048]{1,0:T(8,128)S(1)}, u32[]{:S(2)}, u32[]{:S(2)}) %collective-permute-start.12) | collective-permute-done | bytes 786464 | tf_op jit(solution)/shard_map/ppermute | solution.py:249
  89.9 9.0 %shard_map.20 = (f32[1,96,768]{2,1,0:T(8,128)}, f32[1,96,768]{2,1,0:T(8,128)}, f32[2,96,768]{2,1,0:T(8,128)}, f32[2,96,768]{2,1,0:T(8,128)}) custom-call(s32[4]{0:T(128)} %add_xor_fusion.place, f32[2048,384]{1,0:T(8,128)} %own.9, f32[2048,384]{1,0:T(8,128)} %copy-done.11, f32[96,2048]{1,0:T(8,128)} %copy-done.2, f32[96,2048]{1,0:T(8,128)} %collective-permute-done.6.refs_1_, ...), custom_call_target="tpu_custom_call" | custom-call | flops 1 | bytes 1 | tf_op jit(solution)/shard_map/pallas_call | solution.py:116
  107.5 6.7 %shard_map.22 = (f32[2,64,768]{2,1,0:T(8,128)}, f32[2,64,768]{2,1,0:T(8,128)}) custom-call(s32[4]{0:T(128)} %add_xor_fusion.place, f32[2048,384]{1,0:T(8,128)} %own.9, f32[2048,384]{1,0:T(8,128)} %copy-done.11, f32[64,2048]{1,0:T(8,128)} %copy-done.5, f32[64,2048]{1,0:T(8,128)} %collective-permute-done.11.refs_1_, ...), custom_call_target="tpu_custom_call" | custom-call | flops 1 | bytes 1 | tf_op jit(solution)/shard_map/pallas_call | solution.py:116
  114.2 2.7 %collective-permute-done.9.refs_5_ = f32[1,96,768]{2,1,0:T(8,128)S(1)} collective-permute-done((f32[1,96,768]{2,1,0:T(8,128)S(1)}, f32[1,96,768]{2,1,0:T(8,128)S(1)}, u32[]{:S(2)}, u32[]{:S(2)}) %collective-permute-start.9) | collective-permute-done | bytes 294944 | tf_op jit(solution)/shard_map/ppermute | solution.py:23
  116.9 2.9 %collective-permute-start.18 = (f32[2,64,768]{2,1,0:T(8,128)}, f32[2,64,768]{2,1,0:T(8,128)S(1)}, u32[]{:S(2)}, u32[]{:S(2)}) collective-permute-start(f32[2,64,768]{2,1,0:T(8,128)} %get-tuple-element.129), channel_id=1, source_target_pairs={{0,8},{8,0},{16,24},{24,16},{1,9},{9,1},{17,25},{25,17},{2,10},{10... | collective-permute-start | bytes 1179656 | tf_op jit(solution)/shard_map/ppermute | solution.py:23
  119.8 3.6 %collective-permute-done.14.refs_6_ = f32[1,96,768]{2,1,0:T(8,128)S(1)} collective-permute-done((f32[1,96,768]{2,1,0:T(8,128)}, f32[1,96,768]{2,1,0:T(8,128)S(1)}, u32[]{:S(2)}, u32[]{:S(2)}) %collective-permute-start.14) | collective-permute-done | bytes 294944 | tf_op jit(solution)/shard_map/ppermute | solution.py:23
  124.0 5.4 %shard_map.24 = (f32[2,32,768]{2,1,0:T(8,128)}, f32[2,32,768]{2,1,0:T(8,128)}) custom-call(s32[4]{0:T(128)} %add_xor_fusion.place, f32[2048,384]{1,0:T(8,128)} %own.9, f32[2048,384]{1,0:T(8,128)} %copy-done.11, f32[32,2048]{1,0:T(8,128)} %copy-done.9, f32[32,2048]{1,0:T(8,128)} %copy-done.15, f32[32,2048]{1,0:T(8,128)} %copy-done.16, ...), custom_call_target="tpu_custom_call" | custom-call | flops 1 | bytes 1 | tf_op jit(solution)/shard_map/pallas_call | solution.py:116
  129.4 3.1 %collective-permute-start.22 = (f32[2,32,768]{2,1,0:T(8,128)}, f32[2,32,768]{2,1,0:T(8,128)S(1)}, u32[]{:S(2)}, u32[]{:S(2)}) collective-permute-start(f32[2,32,768]{2,1,0:T(8,128)} %get-tuple-element.137), channel_id=1, source_target_pairs={{0,8},{8,0},{16,24},{24,16},{1,9},{9,1},{17,25},{25,17},{2,10},{10... | collective-permute-start | bytes 589832 | tf_op jit(solution)/shard_map/ppermute | solution.py:23
  132.7 8.2 %collective-permute-done.22.came = f32[2,32,768]{2,1,0:T(8,128)S(1)} collective-permute-done((f32[2,32,768]{2,1,0:T(8,128)}, f32[2,32,768]{2,1,0:T(8,128)S(1)}, u32[]{:S(2)}, u32[]{:S(2)}) %collective-permute-start.22) | collective-permute-done | bytes 196640 | tf_op jit(solution)/shard_map/ppermute | solution.py:23
  147.3 2.9 %collective-permute-done.26 = f32[16,768]{1,0:T(8,128)S(1)} collective-permute-done((f32[16,768]{1,0:T(8,128)S(1)}, f32[16,768]{1,0:T(8,128)S(1)}, u32[]{:S(2)}, u32[]{:S(2)}) %collective-permute-start.26) | collective-permute-done | bytes 49184 | tf_op jit(solution)/shard_map/ppermute | solution.py:223
  150.2 3.0 %collective-permute-start.28 = (f32[1,32,768]{2,1,0:T(8,128)S(1)}, f32[1,32,768]{2,1,0:T(8,128)S(1)}, u32[]{:S(2)}, u32[]{:S(2)}) collective-permute-start(f32[1,32,768]{2,1,0:T(8,128)S(1)} %get-tuple-element.144), channel_id=1, source_target_pairs={{0,16},{8,24},{16,0},{24,8},{1,17},{9,25},{17,1},{25,9},{2,18},{10... | collective-permute-start | bytes 294920 | tf_op jit(solution)/shard_map/ppermute | solution.py:23
  153.1 3.6 %collective-permute-done.27 = f32[16,128]{1,0:T(8,128)S(1)} collective-permute-done((f32[16,128]{1,0:T(8,128)S(1)}, f32[16,128]{1,0:T(8,128)S(1)}, u32[]{:S(2)}, u32[]{:S(2)}) %collective-permute-start.27) | collective-permute-done | bytes 8224 | tf_op jit(solution)/shard_map/ppermute | solution.py:223
  156.8 3.8 %collective-permute-done.28.refs_9_ = f32[1,32,768]{2,1,0:T(8,128)S(1)} collective-permute-done((f32[1,32,768]{2,1,0:T(8,128)S(1)}, f32[1,32,768]{2,1,0:T(8,128)S(1)}, u32[]{:S(2)}, u32[]{:S(2)}) %collective-permute-start.28) | collective-permute-done | bytes 98336 | tf_op jit(solution)/shard_map/ppermute | solution.py:23
  160.8 4.5 %collective-permute-start.29 = (f32[384,512]{1,0:T(8,128)S(1)}, f32[384,512]{1,0:T(8,128)S(1)}, u32[]{:S(2)}, u32[]{:S(2)}) collective-permute-start(f32[384,512]{1,0:T(8,128)S(1)} %get-tuple-element.147), channel_id=1, source_target_pairs={{0,1},{1,0},{2,3},{3,2},{4,5},{5,4},{6,7},{7,6},{8,9},{9,8},{10,11... | collective-permute-start | bytes 2359304 | tf_op jit(solution)/shard_map/ppermute | solution.py:23
  167.9 2.5 %collective-permute-done.30.first = f32[16,384]{1,0:T(8,128)S(1)} collective-permute-done((f32[16,384]{1,0:T(8,128)S(1)}, f32[16,384]{1,0:T(8,128)S(1)}, u32[]{:S(2)}, u32[]{:S(2)}) %collective-permute-start.30) | collective-permute-done | bytes 24608 | tf_op jit(solution)/shard_map/ppermute | solution.py:327
  171.3 3.0 %shard_map.27 = f32[384,768]{1,0:T(8,128)} custom-call(s32[1]{0:T(128)} %bitcast.core, f32[384,384]{1,0:T(8,128)S(1)} %get-tuple-element.146.own, f32[384,512]{1,0:T(8,128)S(1)} %collective-permute-done.29.swap, f32[16,384]{1,0:T(8,128)S(1)} %get-tuple-element.148.near, f32[16,384]{1,0:T(8,128)S(1)} %collective-permute-done.30.first, ...), custom_call_target="tpu_custom_call" | custom-call | tf_op jit(solution)/shard_map/pallas_call | solution.py:166
  (92 shorter events, 40.8 us)
Async XLA Ops:
  0.0 22.0 %collective-permute-start.1 = (f32[2048,384]{1,0:T(8,128)}, f32[2048,384]{1,0:T(8,128)S(1)}, u32[]{:S(2)}, u32[]{:S(2)}) collective-permute-start(f32[2048,384]{1,0:T(8,128)} %own.9), channel_id=1, source_target_pairs={{0,1},{1,0},{2,3},{3,2},{4,5},{5,4},{6,7},{7,6},{8,9},{9,8},{10,11... | collective-permute-start | bytes 9437192 | tf_op jit(solution)/shard_map/ppermute | solution.py:23
  3.3 18.7 %collective-permute-start = (f32[96,2048]{1,0:T(8,128)S(1)}, f32[96,2048]{1,0:T(8,128)}, u32[]{:S(2)}, u32[]{:S(2)}) collective-permute-start(f32[96,2048]{1,0:T(8,128)S(1)} %get-tuple-element.97.refs_0_), channel_id=1, source_target_pairs={{0,2},{1,5},{2,0},{3,7},{4,6},{5,1},{6,4},{7,3},{8,10},{9,13},{10,... | collective-permute-start | bytes 2359304 | tf_op jit(solution)/shard_map/ppermute | solution.py:249
  6.1 19.7 %collective-permute-start.2 = (f32[96,2048]{1,0:T(8,128)S(1)}, f32[96,2048]{1,0:T(8,128)S(1)}, u32[]{:S(2)}, u32[]{:S(2)}) collective-permute-start(f32[96,2048]{1,0:T(8,128)S(1)} %get-tuple-element.97.refs_0_), channel_id=1, source_target_pairs={{0,4},{1,3},{2,6},{3,1},{4,0},{5,7},{6,2},{7,5},{8,12},{9,11},{10,... | collective-permute-start | bytes 2359304 | tf_op jit(solution)/shard_map/ppermute | solution.py:249
  7.3 30.1 %collective-permute-start.3 = (f32[96,2048]{1,0:T(8,128)S(1)}, f32[96,2048]{1,0:T(8,128)}, u32[]{:S(2)}, u32[]{:S(2)}) collective-permute-start(f32[96,2048]{1,0:T(8,128)S(1)} %get-tuple-element.89.refs_0_), channel_id=1, source_target_pairs={{0,2},{1,5},{2,0},{3,7},{4,6},{5,1},{6,4},{7,3},{8,10},{9,13},{10,... | collective-permute-start | bytes 2359304 | tf_op jit(solution)/shard_map/ppermute | solution.py:249
  22.0 19.2 %collective-permute-start.4 = (f32[96,2048]{1,0:T(8,128)}, f32[96,2048]{1,0:T(8,128)}, u32[]{:S(2)}, u32[]{:S(2)}) collective-permute-start(f32[96,2048]{1,0:T(8,128)} %collective-permute-done.refs_1_), channel_id=1, source_target_pairs={{0,4},{1,3},{2,6},{3,1},{4,0},{5,7},{6,2},{7,5},{8,12},{9,11},{10,... | collective-permute-start | bytes 2359304 | tf_op jit(solution)/shard_map/ppermute | solution.py:249
  25.8 30.8 %collective-permute-start.5 = (f32[96,2048]{1,0:T(8,128)S(1)}, f32[96,2048]{1,0:T(8,128)}, u32[]{:S(2)}, u32[]{:S(2)}) collective-permute-start(f32[96,2048]{1,0:T(8,128)S(1)} %get-tuple-element.89.refs_0_), channel_id=1, source_target_pairs={{0,4},{1,3},{2,6},{3,1},{4,0},{5,7},{6,2},{7,5},{8,12},{9,11},{10,... | collective-permute-start | bytes 2359304 | tf_op jit(solution)/shard_map/ppermute | solution.py:249
  37.4 20.9 %collective-permute-start.6 = (f32[96,2048]{1,0:T(8,128)S(1)}, f32[96,2048]{1,0:T(8,128)}, u32[]{:S(2)}, u32[]{:S(2)}) collective-permute-start(f32[96,2048]{1,0:T(8,128)S(1)} %get-tuple-element.106.refs_0_), channel_id=1, source_target_pairs={{0,2},{1,5},{2,0},{3,7},{4,6},{5,1},{6,4},{7,3},{8,10},{9,13},{10,... | collective-permute-start | bytes 2359304 | tf_op jit(solution)/shard_map/ppermute | solution.py:249
  38.6 29.1 %collective-permute-start.7 = (f32[96,2048]{1,0:T(8,128)}, f32[96,2048]{1,0:T(8,128)}, u32[]{:S(2)}, u32[]{:S(2)}) collective-permute-start(f32[96,2048]{1,0:T(8,128)} %collective-permute-done.3.refs_1_), channel_id=1, source_target_pairs={{0,4},{1,3},{2,6},{3,1},{4,0},{5,7},{6,2},{7,5},{8,12},{9,11},{10,... | collective-permute-start | bytes 2359304 | tf_op jit(solution)/shard_map/ppermute | solution.py:249
  49.3 18.3 %collective-permute-start.8 = (f32[2,96,768]{2,1,0:T(8,128)}, f32[2,96,768]{2,1,0:T(8,128)}, u32[]{:S(2)}, u32[]{:S(2)}) collective-permute-start(f32[2,96,768]{2,1,0:T(8,128)} %get-tuple-element.101), channel_id=1, source_target_pairs={{0,8},{8,0},{16,24},{24,16},{1,9},{9,1},{17,25},{25,17},{2,10},{10... | collective-permute-start | bytes 1769480 | tf_op jit(solution)/shard_map/ppermute | solution.py:23
  56.6 23.9 %collective-permute-start.10 = (f32[96,2048]{1,0:T(8,128)S(1)}, f32[96,2048]{1,0:T(8,128)S(1)}, u32[]{:S(2)}, u32[]{:S(2)}) collective-permute-start(f32[96,2048]{1,0:T(8,128)S(1)} %get-tuple-element.106.refs_0_), channel_id=1, source_target_pairs={{0,4},{1,3},{2,6},{3,1},{4,0},{5,7},{6,2},{7,5},{8,12},{9,11},{10,... | collective-permute-start | bytes 2359304 | tf_op jit(solution)/shard_map/ppermute | solution.py:249
  58.3 30.7 %collective-permute-start.12 = (f32[96,2048]{1,0:T(8,128)}, f32[96,2048]{1,0:T(8,128)S(1)}, u32[]{:S(2)}, u32[]{:S(2)}) collective-permute-start(f32[96,2048]{1,0:T(8,128)} %collective-permute-done.6.refs_1_), channel_id=1, source_target_pairs={{0,4},{1,3},{2,6},{3,1},{4,0},{5,7},{6,2},{7,5},{8,12},{9,11},{10,... | collective-permute-start | bytes 2359304 | tf_op jit(solution)/shard_map/ppermute | solution.py:249
  58.6 23.6 %collective-permute-start.11 = (f32[64,2048]{1,0:T(8,128)S(1)}, f32[64,2048]{1,0:T(8,128)}, u32[]{:S(2)}, u32[]{:S(2)}) collective-permute-start(f32[64,2048]{1,0:T(8,128)S(1)} %get-tuple-element.125.refs_0_), channel_id=1, source_target_pairs={{0,2},{1,5},{2,0},{3,7},{4,6},{5,1},{6,4},{7,3},{8,10},{9,13},{10,... | collective-permute-start | bytes 1572872 | tf_op jit(solution)/shard_map/ppermute | solution.py:249
  80.5 23.6 %collective-permute-start.16 = (f32[64,2048]{1,0:T(8,128)S(1)}, f32[64,2048]{1,0:T(8,128)}, u32[]{:S(2)}, u32[]{:S(2)}) collective-permute-start(f32[64,2048]{1,0:T(8,128)S(1)} %get-tuple-element.125.refs_0_), channel_id=1, source_target_pairs={{0,4},{1,3},{2,6},{3,1},{4,0},{5,7},{6,2},{7,5},{8,12},{9,11},{10,... | collective-permute-start | bytes 1572872 | tf_op jit(solution)/shard_map/ppermute | solution.py:249
  82.2 25.0 %collective-permute-start.17 = (f32[64,2048]{1,0:T(8,128)}, f32[64,2048]{1,0:T(8,128)}, u32[]{:S(2)}, u32[]{:S(2)}) collective-permute-start(f32[64,2048]{1,0:T(8,128)} %collective-permute-done.11.refs_1_), channel_id=1, source_target_pairs={{0,4},{1,3},{2,6},{3,1},{4,0},{5,7},{6,2},{7,5},{8,12},{9,11},{10,... | collective-permute-start | bytes 1572872 | tf_op jit(solution)/shard_map/ppermute | solution.py:249
  98.9 33.6 %collective-permute-start.15 = (f32[2,96,768]{2,1,0:T(8,128)}, f32[2,96,768]{2,1,0:T(8,128)S(1)}, u32[]{:S(2)}, u32[]{:S(2)}) collective-permute-start(f32[2,96,768]{2,1,0:T(8,128)} %get-tuple-element.121), channel_id=1, source_target_pairs={{0,8},{8,0},{16,24},{24,16},{1,9},{9,1},{17,25},{25,17},{2,10},{10... | collective-permute-start | bytes 1769480 | tf_op jit(solution)/shard_map/ppermute | solution.py:23
  101.8 15.1 %collective-permute-start.9 = (f32[1,96,768]{2,1,0:T(8,128)S(1)}, f32[1,96,768]{2,1,0:T(8,128)S(1)}, u32[]{:S(2)}, u32[]{:S(2)}) collective-permute-start(f32[1,96,768]{2,1,0:T(8,128)S(1)} %copy-done.17), channel_id=1, source_target_pairs={{0,16},{8,24},{16,0},{24,8},{1,17},{9,25},{17,1},{25,9},{2,18},{10... | collective-permute-start | bytes 884744 | tf_op jit(solution)/shard_map/ppermute | solution.py:23
  104.1 19.2 %collective-permute-start.14 = (f32[1,96,768]{2,1,0:T(8,128)}, f32[1,96,768]{2,1,0:T(8,128)S(1)}, u32[]{:S(2)}, u32[]{:S(2)}) collective-permute-start(f32[1,96,768]{2,1,0:T(8,128)} %get-tuple-element.117), channel_id=1, source_target_pairs={{0,16},{8,24},{16,0},{24,8},{1,17},{9,25},{17,1},{25,9},{2,18},{10... | collective-permute-start | bytes 884744 | tf_op jit(solution)/shard_map/ppermute | solution.py:23
  106.0 17.3 %collective-permute-start.20 = (f32[32,2048]{1,0:T(8,128)S(1)}, f32[32,2048]{1,0:T(8,128)S(1)}, u32[]{:S(2)}, u32[]{:S(2)}) collective-permute-start(f32[32,2048]{1,0:T(8,128)S(1)} %get-tuple-element.134.refs_0_), channel_id=1, source_target_pairs={{0,4},{1,3},{2,6},{3,1},{4,0},{5,7},{6,2},{7,5},{8,12},{9,11},{10,... | collective-permute-start | bytes 786440 | tf_op jit(solution)/shard_map/ppermute | solution.py:249
  107.2 16.1 %collective-permute-start.21 = (f32[32,2048]{1,0:T(8,128)S(1)}, f32[32,2048]{1,0:T(8,128)}, u32[]{:S(2)}, u32[]{:S(2)}) collective-permute-start(f32[32,2048]{1,0:T(8,128)S(1)} %collective-permute-done.19.refs_1_), channel_id=1, source_target_pairs={{0,4},{1,3},{2,6},{3,1},{4,0},{5,7},{6,2},{7,5},{8,12},{9,11},{10,... | collective-permute-start | bytes 786440 | tf_op jit(solution)/shard_map/ppermute | solution.py:249
  116.9 28.3 %collective-permute-start.18 = (f32[2,64,768]{2,1,0:T(8,128)}, f32[2,64,768]{2,1,0:T(8,128)S(1)}, u32[]{:S(2)}, u32[]{:S(2)}) collective-permute-start(f32[2,64,768]{2,1,0:T(8,128)} %get-tuple-element.129), channel_id=1, source_target_pairs={{0,8},{8,0},{16,24},{24,16},{1,9},{9,1},{17,25},{25,17},{2,10},{10... | collective-permute-start | bytes 1179656 | tf_op jit(solution)/shard_map/ppermute | solution.py:23
  132.6 28.0 %collective-permute-start.23 = (f32[1,96,768]{2,1,0:T(8,128)S(1)}, f32[1,96,768]{2,1,0:T(8,128)S(1)}, u32[]{:S(2)}, u32[]{:S(2)}) collective-permute-start(f32[1,96,768]{2,1,0:T(8,128)S(1)} %get-tuple-element.141), channel_id=1, source_target_pairs={{0,16},{8,24},{16,0},{24,8},{1,17},{9,25},{17,1},{25,9},{2,18},{10... | collective-permute-start | bytes 884744 | tf_op jit(solution)/shard_map/ppermute | solution.py:23
  143.2 13.6 %collective-permute-start.25 = (f32[16,768]{1,0:T(8,128)S(1)}, f32[16,768]{1,0:T(8,128)S(1)}, u32[]{:S(2)}, u32[]{:S(2)}) collective-permute-start(f32[16,768]{1,0:T(8,128)S(1)} %fusion), channel_id=1, source_target_pairs={{8,0},{16,8},{24,16},{10,2},{18,10},{26,18},{12,4},{20,12},{28,20}... | collective-permute-start | bytes 147464 | tf_op jit(solution)/shard_map/ppermute | solution.py:223
  143.9 12.9 %collective-permute-start.27 = (f32[16,128]{1,0:T(8,128)S(1)}, f32[16,128]{1,0:T(8,128)S(1)}, u32[]{:S(2)}, u32[]{:S(2)}) collective-permute-start(f32[16,128]{1,0:T(8,128)S(1)} %slice.15), channel_id=1, source_target_pairs={{10,1},{18,9},{26,17},{12,3},{20,11},{28,19},{14,5},{22,13},{30,21}} | collective-permute-start | bytes 24584 | tf_op jit(solution)/shard_map/ppermute | solution.py:223
  145.3 15.4 %collective-permute-start.24 = (f32[1,64,768]{2,1,0:T(8,128)S(1)}, f32[1,64,768]{2,1,0:T(8,128)S(1)}, u32[]{:S(2)}, u32[]{:S(2)}) collective-permute-start(f32[1,64,768]{2,1,0:T(8,128)S(1)} %get-tuple-element.142), channel_id=1, source_target_pairs={{0,16},{8,24},{16,0},{24,8},{1,17},{9,25},{17,1},{25,9},{2,18},{10... | collective-permute-start | bytes 589832 | tf_op jit(solution)/shard_map/ppermute | solution.py:23
  (26 other events, 523.1 us)

commit v6 on v5

--- a/solution.py
+++ b/solution.py
@@ -104,7 +104,7 @@
                 send[slot] = block
 
 
-def multiply(place, own, mate, pieces, earlier):
+def multiply(place, own, mate, pieces, earlier, flops):
     depth, block = own.shape
     steps = depth // DEPTH
     width = pieces[0].shape[0]
@@ -123,7 +123,7 @@
         out_shape=[jax.ShapeDtypeStruct(shape, jnp.float32) for shape in shapes],
         scratch_shapes=[pltpu.VMEM((chips * width, 2 * block), jnp.float32)],
         compiler_params=params(5),
-        cost_estimate=pl.CostEstimate(flops=1, bytes_accessed=1, transcendentals=0),
+        cost_estimate=pl.CostEstimate(flops=flops, bytes_accessed=1, transcendentals=0),
     )(place, own, mate, *pieces, *earlier)
 
 
@@ -269,13 +269,15 @@
     steps.remove((count, 0))
     got, firsts, seconds = {}, {}, {}
 
-    def product(j, earlier=()):
+    def product(j, earlier=(), flops=1):
         pieces = [chunks[j]] + [got[j, step] for step in range(3)]
         bit = 4
         while bit < chips:
             pieces += [swapped(piece, 2 * bit) for piece in pieces]
             bit *= 2
-        *halved, keep, send = multiply(place, snapshots, mate, pieces, earlier)
+        *halved, keep, send = multiply(
+            place, snapshots, mate, pieces, earlier, flops
+        )
         firsts[j] = keep, swapped(send, 1, "space")
         if halved:
             seconds[j - 1] = halved[0], swapped(halved[1], 2, "space")
@@ -306,8 +308,11 @@
             product(ready, firsts.get(ready - 1, ()))
     for i in range(len(firsts), count):
         if i == count - 1:
-            place, seconds = lax.optimization_barrier((place, seconds))
-        product(i, firsts[i - 1] if i == 2 else ())
+            keep, send = halve(*firsts[i - 2])
+            came = swapped(send, 2, "space")
+            place, seconds[0], keep = lax.optimization_barrier((place, seconds[0], keep))
+            seconds[i - 2] = keep, came
+        product(i, flops=1 if i == count - 1 else 1)
     for i in range(count):
         if i not in seconds:
             keep, send = halve(*firsts[i])

time: 175 us -> 178 us (1.017)
  waiting for transfers between devices: 78.7 us -> 92.8 us
  starting transfers between devices: 47.5 us -> 36 us
    ppermute x12, waiting for transfers between devices: 18.3 us -> 29.6 us  [swapped(): return lax.ppermute(block, axis, [(i, i ^ bit) for i in range(size)])]
    ppermute x12, starting transfers between devices: 23.8 us -> 12.5 us  [swapped(): return lax.ppermute(block, axis, [(i, i ^ bit) for i in range(size)])]
    ppermute x15, waiting for transfers between devices: 50.5 us -> 53.6 us  [routed(): lax.ppermute(block, 'tm', [(i, i ^ 2 << ways[i % 2]) for i in range(size)])]
  transfers between devices with their start and end apart: 32 -> 32, of which waited for: 17 -> 15; matrix products, arithmetic and copies ran while one was open for 0% -> 0% of each run, Pallas kernels for 23% -> 22%
where the time goes in v6:
time: 178 us
  waiting for transfers between devices  92.8 us (52%)
  Pallas kernels  42.8 us (24%)
  starting transfers between devices  36 us (20%)
  local copies, waits for them, and re-layouts  5.19 us (3%)
    ppermute x15, waiting for transfers between devices, routed(): lax.ppermute(block, 'tm', [(i, i ^ 2 << ways[i % 2]) for i in range(size)])  53.6 us
    pallas_call x5, Pallas kernels, multiply(): pl.pallas_call(functools.partial(multiply_kernel, steps, len(pieces)), gr...  38.2 us
    ppermute x12, waiting for transfers between devices, swapped(): return lax.ppermute(block, axis, [(i, i ^ bit) for i in range(size)])  29.6 us
    ppermute x15, starting transfers between devices, routed(): lax.ppermute(block, 'tm', [(i, i ^ 2 << ways[i % 2]) for i in range(size)])  17.6 us
    ppermute x12, starting transfers between devices, swapped(): return lax.ppermute(block, axis, [(i, i ^ bit) for i in range(size)])  12.5 us
    ppermute x3, waiting for transfers between devices, moved(): return lax.ppermute(value, ('space', 'tm'), pairs)  6.31 us
    unnamed x36, local copies, waits for them, and re-layouts  5.18 us
  transfers between devices with their start and end apart: 32, of which 15 were waited for; matrix products, arithmetic and copies ran while one was open for 0% of the time, Pallas kernels for 22%

profile of v6, /device:TPU:1, one launch (start us, length us, event | category | flops | bytes accessed | tf_op | source)
XLA Modules:
  0.0 177.7 jit_solution(9773522548576048310)
XLA Ops:
  0.1 1.9 %copy-done = f32[2048,384]{1,0:T(8,128)S(1)} copy-done((f32[2048,384]{1,0:T(8,128)S(1)}, f32[2048,384]{1,0:T(8,128)}, u32[]{:S(2)}) %copy-start) | copy-done | bytes 3145752
  3.3 2.8 %collective-permute-start = (f32[96,2048]{1,0:T(8,128)S(1)}, f32[96,2048]{1,0:T(8,128)}, u32[]{:S(2)}, u32[]{:S(2)}) collective-permute-start(f32[96,2048]{1,0:T(8,128)S(1)} %get-tuple-element.96.refs_0_), channel_id=1, source_target_pairs={{0,2},{1,5},{2,0},{3,7},{4,6},{5,1},{6,4},{7,3},{8,10},{9,13},{10,... | collective-permute-start | bytes 2359304 | tf_op jit(solution)/shard_map/ppermute | solution.py:249
  7.5 14.5 %collective-permute-done.refs_1_ = f32[96,2048]{1,0:T(8,128)} collective-permute-done((f32[96,2048]{1,0:T(8,128)S(1)}, f32[96,2048]{1,0:T(8,128)}, u32[]{:S(2)}, u32[]{:S(2)}) %collective-permute-start) | collective-permute-done | bytes 786464 | tf_op jit(solution)/shard_map/ppermute | solution.py:249
  22.0 3.2 %collective-permute-start.4 = (f32[96,2048]{1,0:T(8,128)}, f32[96,2048]{1,0:T(8,128)}, u32[]{:S(2)}, u32[]{:S(2)}) collective-permute-start(f32[96,2048]{1,0:T(8,128)} %collective-permute-done.refs_1_), channel_id=1, source_target_pairs={{0,4},{1,3},{2,6},{3,1},{4,0},{5,7},{6,2},{7,5},{8,12},{9,11},{10,... | collective-permute-start | bytes 2359304 | tf_op jit(solution)/shard_map/ppermute | solution.py:249
  26.9 10.5 %collective-permute-done.3.refs_1_ = f32[96,2048]{1,0:T(8,128)} collective-permute-done((f32[96,2048]{1,0:T(8,128)S(1)}, f32[96,2048]{1,0:T(8,128)}, u32[]{:S(2)}, u32[]{:S(2)}) %collective-permute-start.3) | collective-permute-done | bytes 786464 | tf_op jit(solution)/shard_map/ppermute | solution.py:249
  41.3 8.0 %shard_map.18 = (f32[2,96,768]{2,1,0:T(8,128)}, f32[2,96,768]{2,1,0:T(8,128)}) custom-call(s32[4]{0:T(128)} %add_xor_fusion.place, f32[2048,384]{1,0:T(8,128)} %own.9, f32[2048,384]{1,0:T(8,128)} %copy-done.11, f32[96,2048]{1,0:T(8,128)} %copy-done.1, f32[96,2048]{1,0:T(8,128)} %collective-permute-done.refs_1_, f32[96,2048]{1,0:T(8,128)} %copy-done.12, ...), custom_call_target="tpu_custom_call" | custom-call | flops 1 | bytes 1 | tf_op jit(solution)/shard_map/pallas_call | solution.py:116
  49.3 1.9 %collective-permute-start.8 = (f32[2,96,768]{2,1,0:T(8,128)}, f32[2,96,768]{2,1,0:T(8,128)}, u32[]{:S(2)}, u32[]{:S(2)}) collective-permute-start(f32[2,96,768]{2,1,0:T(8,128)} %get-tuple-element.100), channel_id=1, source_target_pairs={{0,8},{8,0},{16,24},{24,16},{1,9},{9,1},{17,25},{25,17},{2,10},{10... | collective-permute-start | bytes 1769480 | tf_op jit(solution)/shard_map/ppermute | solution.py:23
  51.2 5.4 %collective-permute-done.5.refs_2_ = f32[96,2048]{1,0:T(8,128)} collective-permute-done((f32[96,2048]{1,0:T(8,128)S(1)}, f32[96,2048]{1,0:T(8,128)}, u32[]{:S(2)}, u32[]{:S(2)}) %collective-permute-start.5) | collective-permute-done | bytes 786464 | tf_op jit(solution)/shard_map/ppermute | solution.py:249
  58.6 7.8 %collective-permute-done.7.refs_3_ = f32[96,2048]{1,0:T(8,128)} collective-permute-done((f32[96,2048]{1,0:T(8,128)}, f32[96,2048]{1,0:T(8,128)}, u32[]{:S(2)}, u32[]{:S(2)}) %collective-permute-start.7) | collective-permute-done | bytes 786464 | tf_op jit(solution)/shard_map/ppermute | solution.py:249
  66.5 9.1 %shard_map.19 = (f32[1,96,768]{2,1,0:T(8,128)}, f32[1,96,768]{2,1,0:T(8,128)}, f32[2,96,768]{2,1,0:T(8,128)}, f32[2,96,768]{2,1,0:T(8,128)}) custom-call(s32[4]{0:T(128)} %add_xor_fusion.place, f32[2048,384]{1,0:T(8,128)} %own.9, f32[2048,384]{1,0:T(8,128)} %copy-done.11, f32[96,2048]{1,0:T(8,128)} %copy-done.3, f32[96,2048]{1,0:T(8,128)} %collective-permute-done.3.refs_1_, ...), custom_call_target="tpu_custom_call" | custom-call | flops 1 | bytes 1 | tf_op jit(solution)/shard_map/pallas_call | solution.py:116
  79.6 11.8 %collective-permute-done.11.refs_1_ = f32[64,2048]{1,0:T(8,128)} collective-permute-done((f32[64,2048]{1,0:T(8,128)S(1)}, f32[64,2048]{1,0:T(8,128)}, u32[]{:S(2)}, u32[]{:S(2)}) %collective-permute-start.11) | collective-permute-done | bytes 524320 | tf_op jit(solution)/shard_map/ppermute | solution.py:249
  93.6 9.0 %shard_map.20 = (f32[1,96,768]{2,1,0:T(8,128)}, f32[1,96,768]{2,1,0:T(8,128)}, f32[2,96,768]{2,1,0:T(8,128)}, f32[2,96,768]{2,1,0:T(8,128)}) custom-call(s32[4]{0:T(128)} %add_xor_fusion.place, f32[2048,384]{1,0:T(8,128)} %own.9, f32[2048,384]{1,0:T(8,128)} %copy-done.11, f32[96,2048]{1,0:T(8,128)} %copy-done.2, f32[96,2048]{1,0:T(8,128)} %collective-permute-done.6.refs_1_, ...), custom_call_target="tpu_custom_call" | custom-call | flops 1 | bytes 1 | tf_op jit(solution)/shard_map/pallas_call | solution.py:116
  103.8 2.3 %collective-permute-start.9 = (f32[1,96,768]{2,1,0:T(8,128)}, f32[1,96,768]{2,1,0:T(8,128)S(1)}, u32[]{:S(2)}, u32[]{:S(2)}) collective-permute-start(f32[1,96,768]{2,1,0:T(8,128)} %get-tuple-element.102), channel_id=1, source_target_pairs={{0,16},{8,24},{16,0},{24,8},{1,17},{9,25},{17,1},{25,9},{2,18},{10... | collective-permute-start | bytes 884744 | tf_op jit(solution)/shard_map/ppermute | solution.py:23
  106.4 2.0 %collective-permute-done.18.refs_1_ = f32[32,2048]{1,0:T(8,128)} collective-permute-done((f32[32,2048]{1,0:T(8,128)S(1)}, f32[32,2048]{1,0:T(8,128)}, u32[]{:S(2)}, u32[]{:S(2)}) %collective-permute-start.18) | collective-permute-done | bytes 262176 | tf_op jit(solution)/shard_map/ppermute | solution.py:249
  108.4 6.8 %shard_map.22 = (f32[2,64,768]{2,1,0:T(8,128)}, f32[2,64,768]{2,1,0:T(8,128)}) custom-call(s32[4]{0:T(128)} %add_xor_fusion.place, f32[2048,384]{1,0:T(8,128)} %own.9, f32[2048,384]{1,0:T(8,128)} %copy-done.11, f32[64,2048]{1,0:T(8,128)} %copy-done.5, f32[64,2048]{1,0:T(8,128)} %collective-permute-done.11.refs_1_, f32[64,2048]{1,0:T(8,128)} %copy-done.15, ...), custom_call_target="tpu_custom_call" | custom-call | flops 1 | bytes 1 | tf_op jit(solution)/shard_map/pallas_call | solution.py:116
  116.6 5.8 %collective-permute-done.14.came = f32[2,96,768]{2,1,0:T(8,128)S(1)} collective-permute-done((f32[2,96,768]{2,1,0:T(8,128)}, f32[2,96,768]{2,1,0:T(8,128)S(1)}, u32[]{:S(2)}, u32[]{:S(2)}) %collective-permute-start.14) | collective-permute-done | bytes 589856 | tf_op jit(solution)/shard_map/ppermute | solution.py:23
  124.4 5.4 %shard_map.24 = (f32[2,32,768]{2,1,0:T(8,128)}, f32[2,32,768]{2,1,0:T(8,128)}) custom-call(s32[4]{0:T(128)} %add_xor_fusion.place, f32[2048,384]{1,0:T(8,128)} %own.9, f32[2048,384]{1,0:T(8,128)} %copy-done.11, f32[32,2048]{1,0:T(8,128)} %copy-done.9, f32[32,2048]{1,0:T(8,128)} %collective-permute-done.18.refs_1_, f32[32,2048]{1,0:T(8,128)} %copy-done.16, ...), custom_call_target="tpu_custom_call" | custom-call | flops 1 | bytes 1 | tf_op jit(solution)/shard_map/pallas_call | solution.py:116
  129.8 2.1 %collective-permute-start.21 = (f32[2,32,768]{2,1,0:T(8,128)}, f32[2,32,768]{2,1,0:T(8,128)S(1)}, u32[]{:S(2)}, u32[]{:S(2)}) collective-permute-start(f32[2,32,768]{2,1,0:T(8,128)} %get-tuple-element.135), channel_id=1, source_target_pairs={{0,8},{8,0},{16,24},{24,16},{1,9},{9,1},{17,25},{25,17},{2,10},{10... | collective-permute-start | bytes 589832 | tf_op jit(solution)/shard_map/ppermute | solution.py:23
  131.9 12.6 %collective-permute-done.21.came = f32[2,32,768]{2,1,0:T(8,128)S(1)} collective-permute-done((f32[2,32,768]{2,1,0:T(8,128)}, f32[2,32,768]{2,1,0:T(8,128)S(1)}, u32[]{:S(2)}, u32[]{:S(2)}) %collective-permute-start.21) | collective-permute-done | bytes 196640 | tf_op jit(solution)/shard_map/ppermute | solution.py:23
  148.9 4.7 %collective-permute-done.26 = f32[16,768]{1,0:T(8,128)S(1)} collective-permute-done((f32[16,768]{1,0:T(8,128)S(1)}, f32[16,768]{1,0:T(8,128)S(1)}, u32[]{:S(2)}, u32[]{:S(2)}) %collective-permute-start.26) | collective-permute-done | bytes 49184 | tf_op jit(solution)/shard_map/ppermute | solution.py:223
  155.2 2.3 %collective-permute-start.28 = (f32[1,32,768]{2,1,0:T(8,128)S(1)}, f32[1,32,768]{2,1,0:T(8,128)S(1)}, u32[]{:S(2)}, u32[]{:S(2)}) collective-permute-start(f32[1,32,768]{2,1,0:T(8,128)S(1)} %get-tuple-element.142), channel_id=1, source_target_pairs={{0,16},{8,24},{16,0},{24,8},{1,17},{9,25},{17,1},{25,9},{2,18},{10... | collective-permute-start | bytes 294920 | tf_op jit(solution)/shard_map/ppermute | solution.py:23
  157.5 11.1 %collective-permute-done.28.refs_9_ = f32[1,32,768]{2,1,0:T(8,128)S(1)} collective-permute-done((f32[1,32,768]{2,1,0:T(8,128)S(1)}, f32[1,32,768]{2,1,0:T(8,128)S(1)}, u32[]{:S(2)}, u32[]{:S(2)}) %collective-permute-start.28) | collective-permute-done | bytes 98336 | tf_op jit(solution)/shard_map/ppermute | solution.py:23
  171.5 2.5 %collective-permute-done.30.first = f32[16,384]{1,0:T(8,128)S(1)} collective-permute-done((f32[16,384]{1,0:T(8,128)S(1)}, f32[16,384]{1,0:T(8,128)S(1)}, u32[]{:S(2)}, u32[]{:S(2)}) %collective-permute-start.30) | collective-permute-done | bytes 24608 | tf_op jit(solution)/shard_map/ppermute | solution.py:332
  174.7 3.0 %shard_map.27 = f32[384,768]{1,0:T(8,128)} custom-call(s32[1]{0:T(128)} %bitcast.core, f32[384,384]{1,0:T(8,128)S(1)} %get-tuple-element.144.own, f32[384,512]{1,0:T(8,128)S(1)} %collective-permute-done.29.swap, f32[16,384]{1,0:T(8,128)S(1)} %get-tuple-element.146.near, f32[16,384]{1,0:T(8,128)S(1)} %collective-permute-done.30.first, ...), custom_call_target="tpu_custom_call" | custom-call | tf_op jit(solution)/shard_map/pallas_call | solution.py:166
  (92 shorter events, 31.0 us)
Async XLA Ops:
  0.0 22.0 %collective-permute-start.1 = (f32[2048,384]{1,0:T(8,128)}, f32[2048,384]{1,0:T(8,128)S(1)}, u32[]{:S(2)}, u32[]{:S(2)}) collective-permute-start(f32[2048,384]{1,0:T(8,128)} %own.9), channel_id=1, source_target_pairs={{0,1},{1,0},{2,3},{3,2},{4,5},{5,4},{6,7},{7,6},{8,9},{9,8},{10,11... | collective-permute-start | bytes 9437192 | tf_op jit(solution)/shard_map/ppermute | solution.py:23
  3.3 18.7 %collective-permute-start = (f32[96,2048]{1,0:T(8,128)S(1)}, f32[96,2048]{1,0:T(8,128)}, u32[]{:S(2)}, u32[]{:S(2)}) collective-permute-start(f32[96,2048]{1,0:T(8,128)S(1)} %get-tuple-element.96.refs_0_), channel_id=1, source_target_pairs={{0,2},{1,5},{2,0},{3,7},{4,6},{5,1},{6,4},{7,3},{8,10},{9,13},{10,... | collective-permute-start | bytes 2359304 | tf_op jit(solution)/shard_map/ppermute | solution.py:249
  6.1 19.7 %collective-permute-start.2 = (f32[96,2048]{1,0:T(8,128)S(1)}, f32[96,2048]{1,0:T(8,128)S(1)}, u32[]{:S(2)}, u32[]{:S(2)}) collective-permute-start(f32[96,2048]{1,0:T(8,128)S(1)} %get-tuple-element.96.refs_0_), channel_id=1, source_target_pairs={{0,4},{1,3},{2,6},{3,1},{4,0},{5,7},{6,2},{7,5},{8,12},{9,11},{10,... | collective-permute-start | bytes 2359304 | tf_op jit(solution)/shard_map/ppermute | solution.py:249
  7.3 30.1 %collective-permute-start.3 = (f32[96,2048]{1,0:T(8,128)S(1)}, f32[96,2048]{1,0:T(8,128)}, u32[]{:S(2)}, u32[]{:S(2)}) collective-permute-start(f32[96,2048]{1,0:T(8,128)S(1)} %get-tuple-element.88.refs_0_), channel_id=1, source_target_pairs={{0,2},{1,5},{2,0},{3,7},{4,6},{5,1},{6,4},{7,3},{8,10},{9,13},{10,... | collective-permute-start | bytes 2359304 | tf_op jit(solution)/shard_map/ppermute | solution.py:249
  22.0 19.2 %collective-permute-start.4 = (f32[96,2048]{1,0:T(8,128)}, f32[96,2048]{1,0:T(8,128)}, u32[]{:S(2)}, u32[]{:S(2)}) collective-permute-start(f32[96,2048]{1,0:T(8,128)} %collective-permute-done.refs_1_), channel_id=1, source_target_pairs={{0,4},{1,3},{2,6},{3,1},{4,0},{5,7},{6,2},{7,5},{8,12},{9,11},{10,... | collective-permute-start | bytes 2359304 | tf_op jit(solution)/shard_map/ppermute | solution.py:249
  25.8 30.8 %collective-permute-start.5 = (f32[96,2048]{1,0:T(8,128)S(1)}, f32[96,2048]{1,0:T(8,128)}, u32[]{:S(2)}, u32[]{:S(2)}) collective-permute-start(f32[96,2048]{1,0:T(8,128)S(1)} %get-tuple-element.88.refs_0_), channel_id=1, source_target_pairs={{0,4},{1,3},{2,6},{3,1},{4,0},{5,7},{6,2},{7,5},{8,12},{9,11},{10,... | collective-permute-start | bytes 2359304 | tf_op jit(solution)/shard_map/ppermute | solution.py:249
  37.4 20.9 %collective-permute-start.6 = (f32[96,2048]{1,0:T(8,128)S(1)}, f32[96,2048]{1,0:T(8,128)}, u32[]{:S(2)}, u32[]{:S(2)}) collective-permute-start(f32[96,2048]{1,0:T(8,128)S(1)} %get-tuple-element.105.refs_0_), channel_id=1, source_target_pairs={{0,2},{1,5},{2,0},{3,7},{4,6},{5,1},{6,4},{7,3},{8,10},{9,13},{10,... | collective-permute-start | bytes 2359304 | tf_op jit(solution)/shard_map/ppermute | solution.py:249
  38.6 27.9 %collective-permute-start.7 = (f32[96,2048]{1,0:T(8,128)}, f32[96,2048]{1,0:T(8,128)}, u32[]{:S(2)}, u32[]{:S(2)}) collective-permute-start(f32[96,2048]{1,0:T(8,128)} %collective-permute-done.3.refs_1_), channel_id=1, source_target_pairs={{0,4},{1,3},{2,6},{3,1},{4,0},{5,7},{6,2},{7,5},{8,12},{9,11},{10,... | collective-permute-start | bytes 2359304 | tf_op jit(solution)/shard_map/ppermute | solution.py:249
  49.3 17.2 %collective-permute-start.8 = (f32[2,96,768]{2,1,0:T(8,128)}, f32[2,96,768]{2,1,0:T(8,128)}, u32[]{:S(2)}, u32[]{:S(2)}) collective-permute-start(f32[2,96,768]{2,1,0:T(8,128)} %get-tuple-element.100), channel_id=1, source_target_pairs={{0,8},{8,0},{16,24},{24,16},{1,9},{9,1},{17,25},{25,17},{2,10},{10... | collective-permute-start | bytes 1769480 | tf_op jit(solution)/shard_map/ppermute | solution.py:23
  56.6 21.8 %collective-permute-start.10 = (f32[96,2048]{1,0:T(8,128)S(1)}, f32[96,2048]{1,0:T(8,128)S(1)}, u32[]{:S(2)}, u32[]{:S(2)}) collective-permute-start(f32[96,2048]{1,0:T(8,128)S(1)} %get-tuple-element.105.refs_0_), channel_id=1, source_target_pairs={{0,4},{1,3},{2,6},{3,1},{4,0},{5,7},{6,2},{7,5},{8,12},{9,11},{10,... | collective-permute-start | bytes 2359304 | tf_op jit(solution)/shard_map/ppermute | solution.py:249
  58.3 34.4 %collective-permute-start.12 = (f32[96,2048]{1,0:T(8,128)}, f32[96,2048]{1,0:T(8,128)S(1)}, u32[]{:S(2)}, u32[]{:S(2)}) collective-permute-start(f32[96,2048]{1,0:T(8,128)} %collective-permute-done.6.refs_1_), channel_id=1, source_target_pairs={{0,4},{1,3},{2,6},{3,1},{4,0},{5,7},{6,2},{7,5},{8,12},{9,11},{10,... | collective-permute-start | bytes 2359304 | tf_op jit(solution)/shard_map/ppermute | solution.py:249
  75.5 17.2 %collective-permute-start.13 = (f32[2,96,768]{2,1,0:T(8,128)}, f32[2,96,768]{2,1,0:T(8,128)}, u32[]{:S(2)}, u32[]{:S(2)}) collective-permute-start(f32[2,96,768]{2,1,0:T(8,128)} %get-tuple-element.114), channel_id=1, source_target_pairs={{0,8},{8,0},{16,24},{24,16},{1,9},{9,1},{17,25},{25,17},{2,10},{10... | collective-permute-start | bytes 1769480 | tf_op jit(solution)/shard_map/ppermute | solution.py:23
  77.3 14.1 %collective-permute-start.11 = (f32[64,2048]{1,0:T(8,128)S(1)}, f32[64,2048]{1,0:T(8,128)}, u32[]{:S(2)}, u32[]{:S(2)}) collective-permute-start(f32[64,2048]{1,0:T(8,128)S(1)} %get-tuple-element.123.refs_0_), channel_id=1, source_target_pairs={{0,2},{1,5},{2,0},{3,7},{4,6},{5,1},{6,4},{7,3},{8,10},{9,13},{10,... | collective-permute-start | bytes 1572872 | tf_op jit(solution)/shard_map/ppermute | solution.py:249
  78.4 27.7 %collective-permute-start.15 = (f32[64,2048]{1,0:T(8,128)S(1)}, f32[64,2048]{1,0:T(8,128)S(1)}, u32[]{:S(2)}, u32[]{:S(2)}) collective-permute-start(f32[64,2048]{1,0:T(8,128)S(1)} %get-tuple-element.123.refs_0_), channel_id=1, source_target_pairs={{0,4},{1,3},{2,6},{3,1},{4,0},{5,7},{6,2},{7,5},{8,12},{9,11},{10,... | collective-permute-start | bytes 1572872 | tf_op jit(solution)/shard_map/ppermute | solution.py:249
  91.5 16.9 %collective-permute-start.16 = (f32[64,2048]{1,0:T(8,128)}, f32[64,2048]{1,0:T(8,128)}, u32[]{:S(2)}, u32[]{:S(2)}) collective-permute-start(f32[64,2048]{1,0:T(8,128)} %collective-permute-done.11.refs_1_), channel_id=1, source_target_pairs={{0,4},{1,3},{2,6},{3,1},{4,0},{5,7},{6,2},{7,5},{8,12},{9,11},{10,... | collective-permute-start | bytes 1572872 | tf_op jit(solution)/shard_map/ppermute | solution.py:249
  102.6 19.9 %collective-permute-start.14 = (f32[2,96,768]{2,1,0:T(8,128)}, f32[2,96,768]{2,1,0:T(8,128)S(1)}, u32[]{:S(2)}, u32[]{:S(2)}) collective-permute-start(f32[2,96,768]{2,1,0:T(8,128)} %get-tuple-element.116), channel_id=1, source_target_pairs={{0,8},{8,0},{16,24},{24,16},{1,9},{9,1},{17,25},{25,17},{2,10},{10... | collective-permute-start | bytes 1769480 | tf_op jit(solution)/shard_map/ppermute | solution.py:23
  103.8 19.2 %collective-permute-start.9 = (f32[1,96,768]{2,1,0:T(8,128)}, f32[1,96,768]{2,1,0:T(8,128)S(1)}, u32[]{:S(2)}, u32[]{:S(2)}) collective-permute-start(f32[1,96,768]{2,1,0:T(8,128)} %get-tuple-element.102), channel_id=1, source_target_pairs={{0,16},{8,24},{16,0},{24,8},{1,17},{9,25},{17,1},{25,9},{2,18},{10... | collective-permute-start | bytes 884744 | tf_op jit(solution)/shard_map/ppermute | solution.py:23
  106.1 16.9 %collective-permute-start.19 = (f32[32,2048]{1,0:T(8,128)S(1)}, f32[32,2048]{1,0:T(8,128)S(1)}, u32[]{:S(2)}, u32[]{:S(2)}) collective-permute-start(f32[32,2048]{1,0:T(8,128)S(1)} %get-tuple-element.132.refs_0_), channel_id=1, source_target_pairs={{0,4},{1,3},{2,6},{3,1},{4,0},{5,7},{6,2},{7,5},{8,12},{9,11},{10,... | collective-permute-start | bytes 786440 | tf_op jit(solution)/shard_map/ppermute | solution.py:249
  108.3 14.6 %collective-permute-start.20 = (f32[32,2048]{1,0:T(8,128)}, f32[32,2048]{1,0:T(8,128)S(1)}, u32[]{:S(2)}, u32[]{:S(2)}) collective-permute-start(f32[32,2048]{1,0:T(8,128)} %collective-permute-done.18.refs_1_), channel_id=1, source_target_pairs={{0,4},{1,3},{2,6},{3,1},{4,0},{5,7},{6,2},{7,5},{8,12},{9,11},{10,... | collective-permute-start | bytes 786440 | tf_op jit(solution)/shard_map/ppermute | solution.py:249
  115.1 32.3 %collective-permute-start.17 = (f32[2,64,768]{2,1,0:T(8,128)}, f32[2,64,768]{2,1,0:T(8,128)S(1)}, u32[]{:S(2)}, u32[]{:S(2)}) collective-permute-start(f32[2,64,768]{2,1,0:T(8,128)} %get-tuple-element.127), channel_id=1, source_target_pairs={{0,8},{8,0},{16,24},{24,16},{1,9},{9,1},{17,25},{25,17},{2,10},{10... | collective-permute-start | bytes 1179656 | tf_op jit(solution)/shard_map/ppermute | solution.py:23
  122.4 46.2 %collective-permute-start.22 = (f32[1,96,768]{2,1,0:T(8,128)}, f32[1,96,768]{2,1,0:T(8,128)S(1)}, u32[]{:S(2)}, u32[]{:S(2)}) collective-permute-start(f32[1,96,768]{2,1,0:T(8,128)} %get-tuple-element.138), channel_id=1, source_target_pairs={{0,16},{8,24},{16,0},{24,8},{1,17},{9,25},{17,1},{25,9},{2,18},{10... | collective-permute-start | bytes 884744 | tf_op jit(solution)/shard_map/ppermute | solution.py:23
  129.8 14.7 %collective-permute-start.21 = (f32[2,32,768]{2,1,0:T(8,128)}, f32[2,32,768]{2,1,0:T(8,128)S(1)}, u32[]{:S(2)}, u32[]{:S(2)}) collective-permute-start(f32[2,32,768]{2,1,0:T(8,128)} %get-tuple-element.135), channel_id=1, source_target_pairs={{0,8},{8,0},{16,24},{24,16},{1,9},{9,1},{17,25},{25,17},{2,10},{10... | collective-permute-start | bytes 589832 | tf_op jit(solution)/shard_map/ppermute | solution.py:23
  131.9 36.7 %collective-permute-start.23 = (f32[1,96,768]{2,1,0:T(8,128)S(1)}, f32[1,96,768]{2,1,0:T(8,128)S(1)}, u32[]{:S(2)}, u32[]{:S(2)}) collective-permute-start(f32[1,96,768]{2,1,0:T(8,128)S(1)} %get-tuple-element.139), channel_id=1, source_target_pairs={{0,16},{8,24},{16,0},{24,8},{1,17},{9,25},{17,1},{25,9},{2,18},{10... | collective-permute-start | bytes 884744 | tf_op jit(solution)/shard_map/ppermute | solution.py:23
  153.5 15.1 %collective-permute-start.24 = (f32[1,64,768]{2,1,0:T(8,128)S(1)}, f32[1,64,768]{2,1,0:T(8,128)S(1)}, u32[]{:S(2)}, u32[]{:S(2)}) collective-permute-start(f32[1,64,768]{2,1,0:T(8,128)S(1)} %get-tuple-element.140), channel_id=1, source_target_pairs={{0,16},{8,24},{16,0},{24,8},{1,17},{9,25},{17,1},{25,9},{2,18},{10... | collective-permute-start | bytes 589832 | tf_op jit(solution)/shard_map/ppermute | solution.py:23
  (26 other events, 524.6 us)
